TPU v7x, 32 devices: a whole 2x2x4 slice. The times are simulated.
32 devices in a mesh: pairs: 4 (over z), hours: 8 (over y, x, core).
Axes of the slice: x: 2, y: 2, z: 4, core: 2. Of those that a mesh axis runs over, the one named last changes fastest.
Arguments:
- spectra: bfloat16 [32, 16, 8, 2, 1024], P('pairs', 'hours'), may hold values from -6 to 6
- masks: int32 [32, 16, 8], P('pairs', 'hours'), may hold values 0 or 1
- pair_rows: int32 [48, 2], P('pairs'), may hold values from 0 to 31, as said below
- start_basis: float32 [4, 2048], replicated, may hold values from -6 to 6
Outputs:
- window_stacks: float32 [48, 16, 2048], P('pairs', 'hours')
- stack: float32 [48, 2048], P('pairs', 'hours')
- basis: float32 [48, 4, 2048], P('pairs', None, 'hours')
Inputs may be any that keep to these rules, and one draw needn't show every extreme that they name: pair_rows[p, 0] is a station of group p // 12, the group being stations 8 * i to 8 * i + 7 for group i; pair_rows[p, 1] is another station of that group or a station of the group just before or just after it, counted around all groups; each block of 12 rows has pairs with all three of these groups, and its pairs reach exactly 4 distinct stations of the group just before and exactly 4 of the group just after.
All inputs are finite; a program needn't handle non-finite values. No bound on the sum of `masks` on one device may be relied on, other than what follows from the above.
Results may differ from a plain program's by a relative error of at most 0.0064.
Values may be sent and summed in bfloat16 or wider, within the bound.
No kernel may reach another device: no remote copies, remote signals or barrier semaphores. Data moves between devices by JAX's collectives and lax.ppermute only.
A program may use at most 64 MiB of HBM per device.

v0:
```python
import math

import jax
import jax.numpy as jnp
from jax import lax
from jax.sharding import PartitionSpec as P

BAND = 64
TURNS = 2


HIGH = lax.Precision.HIGHEST


def padded(block, sides, width):
    for axis, dim in sides:
        count = lax.axis_size(axis)
        forward = [(i, i + 1) for i in range(count - 1)]
        forward.append((count - 1, 0))
        backward = [(target, source) for source, target in forward]
        low = lax.ppermute(
            lax.slice_in_dim(block, block.shape[dim] - width, None, axis=dim), axis, forward
        )
        high = lax.ppermute(lax.slice_in_dim(block, 0, width, axis=dim), axis, backward)
        block = jnp.concatenate([low, block, high], axis=dim)
    return block


def whiten(spectra, masks):
    values = spectra.astype(jnp.float32)
    shape = values.shape
    banded = values.reshape(shape[:-1] + (shape[-1] // BAND, BAND))
    power = jnp.mean(banded * banded, axis=(3, 5), keepdims=True)
    scaled = (
        banded * lax.rsqrt(power + 1e-06) * masks.astype(jnp.float32)[:, :, :, None, None, None]
    )
    return scaled.reshape(shape).astype(jnp.bfloat16)


def kernel_table(freq, lags):
    nfft = 2 * lags
    bins = jnp.arange(1, freq + 1, dtype=jnp.int32)[:, None]
    shifts = jnp.arange(lags, dtype=jnp.int32)[None, :] - lags // 2
    phase = jnp.mod(bins * shifts, nfft).astype(jnp.float32) * (2.0 * math.pi / nfft)
    scale = freq ** (-0.5)
    return jnp.concatenate([jnp.cos(phase) * scale, -jnp.sin(phase) * scale], 0).astype(
        jnp.bfloat16
    )


def cross_spectra(first, second):
    a_re = first[..., 0, :].astype(jnp.float32)
    a_im = first[..., 1, :].astype(jnp.float32)
    b_re = second[..., 0, :].astype(jnp.float32)
    b_im = second[..., 1, :].astype(jnp.float32)
    real_part = a_re * b_re + a_im * b_im
    imag_part = a_im * b_re - a_re * b_im
    return jnp.concatenate([real_part, imag_part], -1).astype(jnp.bfloat16)


def from_gram(vectors, gram):
    rank = vectors.shape[-2]
    lower = [[None] * rank for index in range(rank)]
    for row in range(rank):
        for col in range(row + 1):
            total = gram[..., row, col]
            for inner in range(col):
                total = total - lower[row][inner] * lower[col][inner]
            if row == col:
                lower[row][row] = jnp.sqrt(total)
            else:
                lower[row][col] = total / lower[col][col]
    result = []
    for row in range(rank):
        current = vectors[..., row, :]
        for inner in range(row):
            current = current - lower[row][inner][..., None] * result[inner]
        result.append(current / lower[row][row][..., None])
    return jnp.stack(result, -2)


def inner_gram(vectors):
    return jnp.einsum("...il,...jl->...ij", vectors, vectors, precision=HIGH)


def power_step(basis, corr, lags):
    proj = jnp.einsum("pwrl,pwgl->pwrg", basis, corr, precision=HIGH)
    back = jnp.einsum("pwrg,pwgl->pwrl", proj, corr, precision=HIGH)
    return back + float(lags) * basis


def on_device(spectra, masks, pair_rows, start_basis):
    stations = spectra.shape[0]
    windows_here = spectra.shape[1]
    segments = spectra.shape[2]
    freq = spectra.shape[4]
    lags = start_basis.shape[1]
    pairs_here = pair_rows.shape[0]
    groups = lax.axis_size("pairs")
    group_index = lax.axis_index("pairs")
    hour_count = lax.axis_size("hours")
    whitened = whiten(spectra, masks)
    first = pair_rows[:, 0]
    second = pair_rows[:, 1]
    second_local = jnp.mod(second, stations)
    relative = jnp.mod(second // stations - group_index + 1, groups)
    nearby = padded(whitened, (("pairs", 0),), stations)
    local_first = stations + jnp.mod(first, stations)
    local_second = relative * stations + second_local
    first_rows = jnp.take(nearby, local_first, axis=0)
    second_rows = jnp.take(nearby, local_second, axis=0)
    cross = cross_spectra(first_rows, second_rows)
    table = kernel_table(freq, lags)
    corr = jnp.dot(
        cross.reshape(pairs_here * windows_here * segments, 2 * freq),
        table,
        preferred_element_type=jnp.float32,
    )
    corr = corr.reshape(pairs_here, windows_here, segments, lags)
    basis_now = jnp.broadcast_to(start_basis, (pairs_here, windows_here) + start_basis.shape)
    for turn in range(TURNS):
        stepped = power_step(basis_now, corr, lags)
        basis_now = from_gram(stepped, inner_gram(stepped))
    final_terms = power_step(basis_now, corr, lags)
    summed = jnp.sum(corr, axis=2)
    coef = jnp.einsum("pwl,pwrl->pwr", summed, basis_now, precision=HIGH)
    window_stacks = jnp.einsum("pwr,pwrl->pwl", coef, basis_now, precision=HIGH) / math.sqrt(
        segments
    )
    merged_terms = jnp.sum(final_terms, axis=1)
    stack_terms = jnp.sum(window_stacks, axis=1) / math.sqrt(windows_here * hour_count)
    width = lags // hour_count
    merged, stack_whole = lax.psum((merged_terms, stack_terms), "hours")
    basis_whole = math.sqrt(lags) * from_gram(merged, inner_gram(merged))
    start = lax.axis_index("hours") * width
    basis = lax.dynamic_slice_in_dim(basis_whole, start, width, 2)
    stack = lax.dynamic_slice_in_dim(stack_whole, start, width, 1)
    return (window_stacks, stack, basis)


def solution(mesh):
    in_specs = (
        P("pairs", "hours", None, None, None),
        P("pairs", "hours", None),
        P("pairs", None),
        P(),
    )
    out_specs = (P("pairs", "hours", None), P("pairs", "hours"), P("pairs", None, "hours"))
    return jax.shard_map(
        on_device, mesh=mesh, in_specs=in_specs, out_specs=out_specs, check_vma=False
    )
```

profile of v0, /device:TPU:0, one launch (start us, length us, event | category | flops | bytes accessed | tf_op | source)
XLA Modules:
  0.0 166.6 jit_solution(10254665118073163575)
XLA Ops:
  7.2 1.3 fusion.7
  8.6 0.3 reduce_sum.44
  8.8 0.3 reduce_sum.45
  9.2 0.3 mul.644
  9.5 0.3 mul.645
  9.9 0.2 fusion.9
  10.1 3.1 %collective-permute-start = (bf16[8,2,8,2,1024]{4,2,3,1,0:T(8,128)(2,1)S(1)}, bf16[8,2,8,2,1024]{4,2,3,1,0:T(8,128)(2,1)S(1)}, u32[]{:S(2)}, u32[]{:S(2)}) collective-permute-start(bf16[8,2,8,2,1024]{4,2,3,1,0:T(8,128)(2,1)S(1)} %fusion.9), channel_id=1, source_target_pairs={{0,8},{8,16},{16,24},{24,0},{1,9},{9,17},{17,25},{25,1},{2,10},{10... | collective-permute-start | bytes 1572872 | tf_op jit(solution)/shard_map/ppermute | solution.py:21
  13.2 2.1 %collective-permute-start.1 = (bf16[8,2,8,2,1024]{4,2,3,1,0:T(8,128)(2,1)S(1)}, bf16[8,2,8,2,1024]{4,2,3,1,0:T(8,128)(2,1)S(1)}, u32[]{:S(2)}, u32[]{:S(2)}) collective-permute-start(bf16[8,2,8,2,1024]{4,2,3,1,0:T(8,128)(2,1)S(1)} %fusion.9), channel_id=1, source_target_pairs={{8,0},{16,8},{24,16},{0,24},{9,1},{17,9},{25,17},{1,25},{10,2},{18... | collective-permute-start | bytes 1572872 | tf_op jit(solution)/shard_map/ppermute | solution.py:24
  15.3 35.8 %multiply_convert_fusion.1 = (bf16[1024,2048]{1,0:T(8,128)(2,1)}, bf16[1024,2048]{1,0:T(8,128)(2,1)}) fusion(s32[2048]{0:T(1024)S(1)} %iota_add_fusion, s32[1024]{0:T(1024)S(1)} %iota_add_fusion.1), kind=kLoop, calls=%fused_computation.15 | loop fusion | flops 39845888 | bytes 8400896 | tf_op jit(solution)/shard_map/convert
  51.2 0.2 pad_maximum_fusion
  51.4 0.6 gather_fusion
  52.0 0.6 gather_fusion.1
  52.6 0.2 copy_select_fusion
  52.8 0.3 fusion.18
  53.1 1.6 copy-done
  54.8 4.0 %fusion.76 = (f32[12,2,2048]{2,1,0:T(2,128)S(1)}, f32[12,2,8,2048]{3,2,1,0:T(8,128)S(1)}) fusion(bf16[1024,2048]{1,0:T(8,128)(2,1)} %get-tuple-element.79, bf16[1024,2048]{1,0:T(8,128)(2,1)S(1)} %copy-done, bf16[12,2,8,1024]{3,2,1,0:T(8,128)(2,1)S(1)} %get-tuple-element.57, bf16[12,2,8,1024]{3,2,1,0:T(8,128)(2,1)S(1)} %get-tuple-element.56), kind=kOutput, calls=%fused_computation.192 | convolution fusion | flops 1629306880 | bytes 10944512 | tf_op jit(solution)/shard_map/dot_general | solution.py:114
  58.7 3.1 %fusion.19 = f32[12,2,8,4]{2,3,1,0:T(4,128)S(1)} fusion(f32[12,2,8,2048]{3,2,1,0:T(8,128)S(1)} %get-tuple-element.107, f32[4,2048]{1,0:T(4,128)S(1)} %copy-done.2), kind=kOutput, calls=%fused_computation.48 | convolution fusion | flops 18874368 | bytes 1608704 | tf_op jit(solution)/shard_map/pwrl,pwgl->pwrg/dot_general | solution.py:87
  61.8 1.4 convolution_add_fusion.2
  63.2 3.1 %fusion.77 = f32[12,2,4,4]{3,2,1,0:T(4,128)S(1)} fusion(f32[12,2,4,2048]{3,2,1,0:T(4,128)S(1)} %convolution_add_fusion.2), kind=kOutput, calls=%fused_computation.193 | convolution fusion | flops 9437184 | bytes 787968 | tf_op jit(solution)/shard_map/...il,...jl->...ij/dot_general | solution.py:83
  66.3 0.2 fusion.75
  66.6 0.1 copy.144
  66.7 0.1 copy.146
  67.0 0.1 copy.152
  67.1 0.1 copy.154
  67.2 0.1 copy.156
  67.3 0.1 copy.158
  67.4 0.1 copy.160
  67.4 0.1 copy.187
  68.6 1.8 %fusion.32 = (f32[12,2,1,2048]{3,2,1,0:T(1,128)S(1)}, f32[12,2,1,2048]{3,2,1,0:T(1,128)S(1)}, f32[12,2,1,2048]{3,2,1,0:T(1,128)S(1)}, f32[12,2,1,2048]{3,2,1,0:T(1,128)S(1)}) fusion(f32[12,2,4,2048]{3,2,1,0:T(4,128)S(1)} %convolution_add_fusion.2, f32[12,2]{1,0:T(8,128)S(1)} %copy.161, f32[12,2]{1,0:T(8,128)S(1)} %copy.159, f32[12,2]{1,0:T(8,128)S(1)} %copy.157, ...), kind=kLoop, calls=%fused_computation.70 | loop fusion | flops 786432 | bytes 1573824 | tf_op jit(solution)/shard_map/div | solution.py:78
  70.3 3.8 %fusion.34 = f32[12,2,4,8]{3,2,1,0:T(4,128)S(1)} fusion(f32[12,2,8,2048]{3,2,1,0:T(8,128)S(1)} %get-tuple-element.107, f32[12,2,1,2048]{3,2,1,0:T(1,128)S(1)} %get-tuple-element.42, f32[12,2,1,2048]{3,2,1,0:T(1,128)S(1)} %get-tuple-element.43, f32[12,2,1,2048]{3,2,1,0:T(1,128)S(1)} %get-tuple-element.44, f32[12,2,1,2048]{3,2,1,0:T(1,128)S(1)} %get-tuple-element.45), kind=kOutput, calls=%fused_computation.72 | convolution fusion | flops 19464192 | bytes 2362368 | tf_op jit(solution)/shard_map/pwrl,pwgl->pwrg/dot_general | solution.py:87
  74.2 2.1 %convolution_add_fusion.1 = f32[12,2,4,2048]{3,2,1,0:T(4,128)S(1)} fusion(f32[12,2,4,8]{3,2,1,0:T(4,128)S(1)} %fusion.34, f32[12,2,8,2048]{3,2,1,0:T(8,128)S(1)} %get-tuple-element.107, f32[12,2,1,2048]{3,2,1,0:T(1,128)S(1)} %get-tuple-element.42, f32[12,2,1,2048]{3,2,1,0:T(1,128)S(1)} %get-tuple-element.43, f32[12,2,1,2048]{3,2,1,0:T(1,128)S(1)} %get-tuple-element.44, ...), kind=kOutput, calls=%fused_computation.17 | convolution fusion | flops 19857408 | bytes 3148800 | tf_op jit(solution)/shard_map/pwrg,pwgl->pwrl/dot_general | solution.py:88
  76.3 3.1 %fusion.78 = f32[12,2,4,4]{3,2,1,0:T(4,128)S(1)} fusion(f32[12,2,4,2048]{3,2,1,0:T(4,128)S(1)} %convolution_add_fusion.1), kind=kOutput, calls=%fused_computation.194 | convolution fusion | flops 9437184 | bytes 787968 | tf_op jit(solution)/shard_map/...il,...jl->...ij/dot_general | solution.py:83
  79.4 0.2 fusion.74
  79.7 0.1 copy.164
  79.8 0.1 copy.166
  81.6 1.8 %fusion.33 = (f32[12,2,1,2048]{3,2,1,0:T(1,128)S(1)}, f32[12,2,1,2048]{3,2,1,0:T(1,128)S(1)}, f32[12,2,1,2048]{3,2,1,0:T(1,128)S(1)}, f32[12,2,1,2048]{3,2,1,0:T(1,128)S(1)}) fusion(f32[12,2,4,2048]{3,2,1,0:T(4,128)S(1)} %convolution_add_fusion.1, f32[12,2]{1,0:T(8,128)S(1)} %copy.181, f32[12,2]{1,0:T(8,128)S(1)} %copy.179, f32[12,2]{1,0:T(8,128)S(1)} %copy.177, ...), kind=kLoop, calls=%fused_computation.71 | loop fusion | flops 786432 | bytes 1573824 | tf_op jit(solution)/shard_map/div | solution.py:78
  83.5 3.8 %fusion.63 = f32[12,2,4,8]{3,2,1,0:T(4,128)S(1)} fusion(f32[12,2,8,2048]{3,2,1,0:T(8,128)S(1)} %get-tuple-element.107, f32[12,2,1,2048]{3,2,1,0:T(1,128)S(1)} %get-tuple-element.32, f32[12,2,1,2048]{3,2,1,0:T(1,128)S(1)} %get-tuple-element.33, f32[12,2,1,2048]{3,2,1,0:T(1,128)S(1)} %get-tuple-element.34, f32[12,2,1,2048]{3,2,1,0:T(1,128)S(1)} %get-tuple-element.35), kind=kOutput, calls=%fused_computation.187 | convolution fusion | flops 19464192 | bytes 2362368 | tf_op jit(solution)/shard_map/pwrl,pwgl->pwrg/dot_general | solution.py:87
  87.3 3.1 %fusion.6 = f32[12,4,2048]{2,1,0:T(4,128)} fusion(f32[12,2,4,8]{3,2,1,0:T(4,128)S(1)} %fusion.63, f32[12,2,8,2048]{3,2,1,0:T(8,128)S(1)} %get-tuple-element.107, f32[12,2,1,2048]{3,2,1,0:T(1,128)S(1)} %get-tuple-element.32, f32[12,2,1,2048]{3,2,1,0:T(1,128)S(1)} %get-tuple-element.33, f32[12,2,1,2048]{3,2,1,0:T(1,128)S(1)} %get-tuple-element.34, ...), kind=kOutput, calls=%fused_computation.22 | convolution fusion | flops 19955712 | bytes 2755584 | tf_op jit(solution)/shard_map/pwrg,pwgl->pwrl/dot_general | solution.py:88
  90.4 3.8 %convolution_bitcast_fusion = f32[12,2,4,1]{2,3,1,0:T(1,128)S(1)} fusion(f32[12,2,2048,1]{2,1,0,3:T(2,128)S(1)} %bitcast.314, f32[12,2,1,2048]{3,2,1,0:T(1,128)S(1)} %get-tuple-element.32, f32[12,2,1,2048]{3,2,1,0:T(1,128)S(1)} %get-tuple-element.33, f32[12,2,1,2048]{3,2,1,0:T(1,128)S(1)} %get-tuple-element.34, f32[12,2,1,2048]{3,2,1,0:T(1,128)S(1)} %get-tuple-element.35), kind=kOutput, calls=%fused_computation.23 | convolution fusion | flops 2949120 | bytes 983424 | tf_op jit(solution)/shard_map/pwl,pwrl->pwr/dot_general | solution.py:126
  94.2 2.0 %fusion.64 = f32[12,2,1,2048]{3,2,1,0:T(1,128)S(1)} fusion(f32[12,2,4,1]{2,3,1,0:T(1,128)S(1)} %convolution_bitcast_fusion, f32[12,2,1,2048]{3,2,1,0:T(1,128)S(1)} %get-tuple-element.32, f32[12,2,1,2048]{3,2,1,0:T(1,128)S(1)} %get-tuple-element.33, f32[12,2,1,2048]{3,2,1,0:T(1,128)S(1)} %get-tuple-element.34, f32[12,2,1,2048]{3,2,1,0:T(1,128)S(1)} %get-tuple-element.35), kind=kOutput, calls=%fused_computation.188 | convolution fusion | flops 2949120 | bytes 983424 | tf_op jit(solution)/shard_map/pwr,pwrl->pwl/dot_general | solution.py:127
  96.2 0.8 fusion.67
  97.1 0.7 broadcast_multiply_fusion
  97.8 54.4 %all-reduce.3.cloned.1.call-done = (f32[12,2048]{1,0:T(8,128)}, f32[12,4,2048]{2,1,0:T(4,128)}) async-done(((f32[12,2048]{1,0:T(8,128)}, f32[12,4,2048]{2,1,0:T(4,128)}), (f32[12,2048]{1,0:T(8,128)}, f32[12,4,2048]{2,1,0:T(4,128)})) %all-reduce.3.cloned.1.call-update) | async-done | bytes 491536 | tf_op jit(solution)/shard_map/psum | solution.py:133
  152.2 2.7 %fusion.79 = f32[12,4,4]{2,1,0:T(4,128)S(1)} fusion(f32[12,4,2048]{2,1,0:T(4,128)} %get-tuple-element.16), kind=kOutput, calls=%fused_computation.195 | convolution fusion | flops 4718592 | bytes 393984 | tf_op jit(solution)/shard_map/...il,...jl->...ij/dot_general | solution.py:83
  154.9 0.4 slice_reduce_fusion
  155.4 1.3 constant_dynamic-slice_fusion
  156.7 2.2 %fusion.40 = (f32[12,1,2048]{2,1,0:T(1,128)S(1)}, f32[12,1,2048]{2,1,0:T(1,128)S(1)}, f32[12,1,2048]{2,1,0:T(1,128)S(1)}, f32[12,1,2048]{2,1,0:T(1,128)S(1)}) fusion(f32[12,4,2048]{2,1,0:T(4,128)} %get-tuple-element.16, f32[12]{0:T(128)S(1)} %get-tuple-element.23, f32[12]{0:T(128)S(1)} %get-tuple-element.24, f32[12]{0:T(128)S(1)} %get-tuple-element.100, ...), kind=kLoop, calls=%fused_computation.82 | loop fusion | flops 393216 | bytes 786912 | tf_op jit(solution)/shard_map/div | solution.py:78
  159.0 0.8 fusion.44
  (58 shorter events, 3.2 us)
Async XLA Ops:
  7.2 2.7 %copy-start.1 = (bf16[8,2,8,2,1024]{4,3,2,1,0:T(2,128)(2,1)S(1)}, bf16[8,2,8,2,1024]{4,3,2,1,0:T(2,128)(2,1)}, u32[]{:S(2)}) copy-start(bf16[8,2,8,2,1024]{4,3,2,1,0:T(2,128)(2,1)} %param.6) | copy-start | bytes 1572868
  7.2 2.7 %copy-start.3 = (s32[8,2,8]{2,1,0:T(2,128)S(1)}, s32[8,2,8]{2,1,0:T(2,128)}, u32[]{:S(2)}) copy-start(s32[8,2,8]{2,1,0:T(2,128)} %param.7) | copy-start | bytes 1540
  7.2 8.1 %copy-start.4 = (s32[12,2]{0,1:T(2,128)S(1)}, s32[12,2]{0,1:T(2,128)}, u32[]{:S(2)}) copy-start(s32[12,2]{0,1:T(2,128)} %param.8) | copy-start | bytes 292
  7.2 145.0 %all-reduce.3.cloned.1.call-start = ((), (), s32[]{:S(2)}) async-start(), calls=%async_computation | async-start | bytes 1048576 | tf_op jit(solution)/shard_map/psum | solution.py:133
  10.1 41.1 %collective-permute-start = (bf16[8,2,8,2,1024]{4,2,3,1,0:T(8,128)(2,1)S(1)}, bf16[8,2,8,2,1024]{4,2,3,1,0:T(8,128)(2,1)S(1)}, u32[]{:S(2)}, u32[]{:S(2)}) collective-permute-start(bf16[8,2,8,2,1024]{4,2,3,1,0:T(8,128)(2,1)S(1)} %fusion.9), channel_id=1, source_target_pairs={{0,8},{8,16},{16,24},{24,0},{1,9},{9,17},{17,25},{25,1},{2,10},{10... | collective-permute-start | bytes 1572872 | tf_op jit(solution)/shard_map/ppermute | solution.py:21
  13.2 38.0 %collective-permute-start.1 = (bf16[8,2,8,2,1024]{4,2,3,1,0:T(8,128)(2,1)S(1)}, bf16[8,2,8,2,1024]{4,2,3,1,0:T(8,128)(2,1)S(1)}, u32[]{:S(2)}, u32[]{:S(2)}) collective-permute-start(bf16[8,2,8,2,1024]{4,2,3,1,0:T(8,128)(2,1)S(1)} %fusion.9), channel_id=1, source_target_pairs={{8,0},{16,8},{24,16},{0,24},{9,1},{17,9},{25,17},{1,25},{10,2},{18... | collective-permute-start | bytes 1572872 | tf_op jit(solution)/shard_map/ppermute | solution.py:24
  15.3 35.8 %copy-start.2 = (f32[4,2048]{1,0:T(4,128)S(1)}, f32[4,2048]{1,0:T(4,128)}, u32[]{:S(2)}) copy-start(f32[4,2048]{1,0:T(4,128)} %param.9) | copy-start | bytes 98308
  52.6 2.2 %copy-start = (bf16[1024,2048]{1,0:T(8,128)(2,1)S(1)}, bf16[1024,2048]{1,0:T(8,128)(2,1)}, u32[]{:S(2)}) copy-start(bf16[1024,2048]{1,0:T(8,128)(2,1)} %get-tuple-element.78) | copy-start | bytes 12582916
Sparse Core Ops, SparseCore 0:
  97.9 54.2 all-reduce.2
where the time goes:
time: 167 us
  waiting for transfers between devices  54.4 us (33%)
  other arithmetic  46.7 us (28%)
  matrix products  36.1 us (22%)
  between operations  14.3 us (9%)
  local copies, waits for them, and re-layouts  9.8 us (6%)
  starting transfers between devices  5.2 us (3%)
    psum x1, waiting for transfers between devices, on_device(): merged, stack_whole = lax.psum((merged_terms, stack_terms), 'hours')  54.4 us
    another operation x1, other arithmetic  35.8 us
    dot_general x3, matrix products, power_step(): proj = jnp.einsum('pwrl,pwgl->pwrg', basis, corr, precision=HIGH)  10.7 us
    dot_general x3, matrix products, inner_gram(): return jnp.einsum('...il,...jl->...ij', vectors, vectors, precision=HIGH)  9 us
    dot_general x3, matrix products, power_step(): back = jnp.einsum('pwrg,pwgl->pwrl', proj, corr, precision=HIGH)  6.67 us
    div x3, other arithmetic, from_gram(): result.append(current / lower[row][row][..., None])  5.83 us
    dot_general x1, matrix products, on_device(): jnp.dot(cross.reshape(pairs_here * windows_here * segments, 2 * freq), ta...  3.97 us
    dot_general x1, matrix products, on_device(): coef = jnp.einsum('pwl,pwrl->pwr', summed, basis_now, precision=HIGH)  3.81 us
  transfers between devices with their start and end apart: 3, of which 1 were waited for; matrix products, arithmetic and copies ran while one was open for 22% of the time, Pallas kernels for 0%

commit v1 on v0

v1 whole, which is shorter than its diff:
```python
import functools
import math

import jax
import jax.numpy as jnp
import numpy as np
from jax import lax
from jax.experimental import pallas as pl
from jax.experimental.pallas import tpu as pltpu
from jax.sharding import PartitionSpec as P

BAND = 64
TURNS = 2
NEAR = 4
F32 = jnp.float32
BF16 = jnp.bfloat16
VMEM = pl.BlockSpec(memory_space=pltpu.VMEM)
SMEM = pl.BlockSpec(memory_space=pltpu.SMEM)
HEAD = 128
LANE = 16


def kernel_table(freq, lags):
    nfft = 2 * lags
    bins = np.arange(1, freq + 1, dtype=np.int64)[:, None]
    shifts = np.arange(lags, dtype=np.int64)[None, :] - lags // 2
    phase = np.mod(bins * shifts, nfft).astype(np.float64) * (2.0 * math.pi / nfft)
    scale = freq ** (-0.5)
    table = np.concatenate([np.cos(phase) * scale, -np.sin(phase) * scale], 0)
    return table.astype(np.float32).astype(jnp.bfloat16)


def pick_matrix(pairs, seg, rank):
    pick = np.zeros((HEAD, 2 * HEAD), np.float32)
    side = (seg + rank) * LANE
    for pair in range(pairs):
        for part in range(seg):
            pick[pair * seg + part, part * LANE + pair] = 1
            pick[pair * seg + part, side + pair] = 1
    for row in range(rank):
        pick[pairs * seg + row, (seg + row) * LANE : (seg + row + 1) * LANE] = 1
    return pick.astype(jnp.bfloat16)


def spread_matrix(pairs, seg, rank):
    spread = np.zeros((HEAD, (rank + 1) * HEAD), np.float32)
    for row in range(rank + 1):
        for part in range(seg):
            for pair in range(pairs):
                spread[row * LANE + part, row * HEAD + pair * seg + part] = 1
        for other in range(rank):
            spread[row * LANE + seg + other, row * HEAD + pairs * seg + other] = 1
    return spread.astype(jnp.bfloat16)


def two_parts(values):
    high = values.astype(BF16)
    return high, (values - high.astype(F32)).astype(BF16)


def three_parts(values):
    high = values.astype(BF16)
    rest = values - high.astype(F32)
    mid = rest.astype(BF16)
    return high, mid, (rest - mid.astype(F32)).astype(BF16)


def dot(left, right):
    return jnp.dot(left, right, preferred_element_type=F32)


def dot_rows(left, right):
    return lax.dot_general(left, right, (((1,), (1,)), ((), ())), preferred_element_type=F32)


def lower_factor(gram, rank):
    lower = [[None] * rank for _ in range(rank)]
    inverse = [None] * rank
    for row in range(rank):
        for col in range(row + 1):
            total = gram[row][col]
            for inner in range(col):
                total = total - lower[row][inner] * lower[col][inner]
            if row == col:
                inverse[row] = lax.rsqrt(total)
                lower[row][row] = total * inverse[row]
            else:
                lower[row][col] = total * inverse[col]
    return lower, inverse


def solve_rows(rows, lower, inverse):
    result = []
    for row, current in enumerate(rows):
        for inner in range(row):
            current = current - lower[row][inner] * result[inner]
        result.append(current * inverse[row])
    return result


def select_kernel(stations, place, before, after, *refs):
    windows = len(refs) // 3
    whitened, to_next, to_last = refs[:windows], refs[windows : 2 * windows], refs[2 * windows :]
    low = place[0] * stations
    for rows, outs in ((after, to_next), (before, to_last)):
        needed = jnp.int32(0)
        for row in range(rows.shape[0]):
            local = rows[row, 1] - low
            here = jnp.logical_and(local >= 0, local < stations)
            bit = jnp.left_shift(jnp.int32(1), jnp.clip(local, 0, stations - 1))
            needed = jnp.where(here, jnp.bitwise_or(needed, bit), needed)
        slot = jnp.int32(0)
        for station in range(stations):
            wanted = jnp.bitwise_and(jnp.right_shift(needed, station), 1)
            spot = jnp.minimum(slot, NEAR - 1)

            @pl.when(wanted == 1)
            def _():
                for source, target in zip(whitened, outs):
                    target[spot] = source[station]

            slot = slot + wanted


def window_kernel(sizes, index, own, low, high, table, start, pick, spread, *refs):
    pairs, seg, rank, lags, freq, total_windows, slices, first_window = sizes
    rows = pairs * seg
    if first_window:
        win_out, merged_out, near, cross, vectors, high_part, low_part = refs
    else:
        (core, partial, win_out, send_out, keep_out, near, cross, vectors, high_part, low_part, pieces) = refs
    stations = own.shape[0]
    near[0:NEAR] = low[...]
    near[NEAR : NEAR + stations] = own[...]
    near[NEAR + stations :] = high[...]
    for pair in range(0, pairs, 2):
        real, imag = [], []
        for one in (pair, pair + 1):
            a = near[NEAR + index[0, one]].astype(F32)
            b = near[index[1, one]].astype(F32)
            a_re, a_im, b_re, b_im = a[:seg], a[seg:], b[:seg], b[seg:]
            real.append(a_re * b_re + a_im * b_im)
            imag.append(a_im * b_re - a_re * b_im)
        block = pl.ds(pair * seg, 2 * seg)
        cross[block, 0:freq] = jnp.concatenate(real, 0).astype(BF16)
        cross[block, freq:] = jnp.concatenate(imag, 0).astype(BF16)
    vectors[rows : rows + rank] = start[...]
    vectors[rows + rank :] = jnp.zeros((HEAD - rows - rank, lags), F32)
    step = 512
    for at in range(0, lags, step):
        vectors[0:rows, at : at + step] = dot(cross[...], table[:, at : at + step])
    every = vectors[...]
    high_part[...] = every.astype(BF16)
    low_part[...] = (every - high_part[...].astype(F32)).astype(BF16)
    gram = dot_rows(high_part[...], high_part[...])
    side = dot_rows(low_part[...], high_part[...])
    gram = gram + side + side.T
    lane = lax.broadcasted_iota(jnp.int32, (seg, HEAD), 1)
    sub = lax.broadcasted_iota(jnp.int32, (seg, HEAD), 0)
    blocks = jnp.zeros((seg, HEAD), F32)
    for pair in range(pairs):
        blocks = blocks + jnp.where(lane // seg == pair, gram[pair * seg : (pair + 1) * seg], 0.0)
    basis_rows = gram[rows : rows + 8]
    turned = [
        jnp.where(lane % seg == sub, jnp.broadcast_to(basis_rows[row : row + 1], (seg, HEAD)), 0.0)
        for row in range(rank)
    ]
    stacked = jnp.concatenate([blocks, basis_rows] + turned, 0)
    count = stacked.shape[0]
    moved = dot(jnp.concatenate(three_parts(stacked), 0), pick[...])
    moved = moved[0:count] + moved[count : 2 * count] + moved[2 * count :]
    products = [moved[0:16, k * LANE : (k + 1) * LANE] for k in range(seg)]
    side_at = (seg + rank) * LANE
    for row in range(rank):
        upper = moved[16 + row * seg : 16 + (row + 1) * seg, side_at : side_at + LANE]
        under = moved[8:16, (seg + row) * LANE : (seg + row + 1) * LANE]
        products.append(jnp.concatenate([upper, under], 0))
    level = lax.broadcasted_iota(jnp.int32, (16, LANE), 0)
    of_corr = level < seg
    known = [jnp.where(level == seg + row, 1.0, 0.0) for row in range(rank)]
    reach = [jnp.where(of_corr, products[seg + row], 0.0) for row in range(rank)]
    for turn in range(TURNS):
        known = [known[r] + reach[r] * (1.0 / lags) for r in range(rank)]
        images = []
        for r in range(rank):
            image = known[r][0:1] * products[0]
            for k in range(1, seg + rank):
                image = image + known[r][k : k + 1] * products[k]
            images.append(image)
        inner = [
            [jnp.sum(images[r] * known[s], 0, keepdims=True) for s in range(r + 1)] for r in range(rank)
        ]
        lower, inverse = lower_factor(inner, rank)
        known = solve_rows(known, lower, inverse)
        reach = [jnp.where(of_corr, v, 0.0) for v in solve_rows(images, lower, inverse)]
    outs = [reach[r] + float(lags) * known[r] for r in range(rank)]
    window = jnp.zeros_like(known[0])
    for r in range(rank):
        window = window + jnp.sum(reach[r], 0, keepdims=True) * known[r]
    outs.append(window * (1.0 / math.sqrt(seg)))
    coefs = jnp.concatenate(outs + [jnp.zeros((HEAD - (rank + 1) * 16, LANE), F32)], 0)
    coefs = jnp.concatenate([coefs, jnp.zeros((HEAD, HEAD - LANE), F32)], 1).T[0:LANE]
    wide = dot(jnp.concatenate(two_parts(coefs), 0), spread[...])
    wide = wide[0:LANE] + wide[LANE:]
    row_of = lax.broadcasted_iota(jnp.int32, (LANE, HEAD), 0)
    lane_of = lax.broadcasted_iota(jnp.int32, (LANE, HEAD), 1)
    mine = jnp.logical_or(lane_of // seg == row_of, lane_of >= rows)
    weights = [
        jnp.where(mine, wide[:, r * HEAD : (r + 1) * HEAD], 0.0)[0:pairs] for r in range(rank + 1)
    ]
    filled = (rank + 1) * pairs
    height = -(-filled // 16) * 16
    weights = jnp.concatenate(weights + [jnp.zeros((height - filled, HEAD), F32)], 0)
    w_high, w_low = two_parts(weights)
    both = jnp.concatenate([w_high, w_low], 0)
    scale = 1.0 / math.sqrt(total_windows)
    width = lags // slices
    top = rank * pairs
    for at in range(0, lags, step):
        part = dot(both, high_part[:, at : at + step])
        result = part[0:height] + part[height:] + dot(w_high, low_part[:, at : at + step])
        win_out[:, at : at + step] = result[top:filled]
        result = jnp.concatenate([result[0:top], result[top:] * scale], 0)
        if first_window:
            merged_out[:, at : at + step] = result
        else:
            result = result + partial[:, at : at + step]
            for piece in range(at // width, (at + step) // width):
                pieces[piece] = result[:, piece * width - at : (piece + 1) * width - at]
    if not first_window:
        for piece in range(slices // 2):
            send_out[piece] = pieces[2 * piece + 1 - core[0]].astype(BF16)
            keep_out[piece] = pieces[2 * piece + core[0]]


def add_kernel(chip, keep, got, mine_out, *sends):
    mine_out[...] = keep[chip[0]] + got[chip[0]].astype(F32)
    for step, out in enumerate(sends):
        other = jnp.bitwise_xor(chip[0], step + 1)
        out[...] = (keep[other] + got[other].astype(F32)).astype(BF16)


def gram_kernel(pairs, rank, mine, *refs):
    got, (total_out, gram_out) = refs[:-2], refs[-2:]
    total = mine[...]
    for one in got:
        total = total + one[...].astype(F32)
    total_out[...] = total
    rows = [total[r * pairs : (r + 1) * pairs] for r in range(rank)]
    lane = lax.broadcasted_iota(jnp.int32, (pairs, 128), 1)
    gram = jnp.zeros((pairs, 128), F32)
    for r in range(rank):
        for s in range(r + 1):
            gram = jnp.where(lane == r * rank + s, jnp.sum(rows[r] * rows[s], 1, keepdims=True), gram)
    gram_out[...] = gram


def finish_kernel(pairs, rank, lags, total, *refs):
    grams, (stack_out, basis_out) = refs[:-2], refs[-2:]
    gram = grams[0][...]
    for one in grams[1:]:
        gram = gram + one[...]
    entries = [[gram[:, r * rank + s : r * rank + s + 1] for s in range(r + 1)] for r in range(rank)]
    lower, inverse = lower_factor(entries, rank)
    rows = [total[r * pairs : (r + 1) * pairs] for r in range(rank)]
    for r, row in enumerate(solve_rows(rows, lower, inverse)):
        basis_out[:, r, :] = row * math.sqrt(lags)
    stack_out[...] = total[rank * pairs : (rank + 1) * pairs]


def call(kernel, out_shape, in_specs, out_specs, scratch=(), flops=0, moved=0):
    return pl.pallas_call(
        kernel,
        out_shape=out_shape,
        in_specs=in_specs,
        out_specs=out_specs,
        scratch_shapes=list(scratch),
        compiler_params=pltpu.CompilerParams(vmem_limit_bytes=32 * 1024 * 1024),
        cost_estimate=pl.CostEstimate(flops=flops, bytes_accessed=moved, transcendentals=0),
    )


def struct(shape, dtype=F32):
    return jax.ShapeDtypeStruct(shape, dtype)


def whiten(spectra, masks):
    values = spectra.astype(F32)
    shape = values.shape
    banded = values.reshape(shape[:-1] + (shape[-1] // BAND, BAND))
    power = jnp.mean(banded * banded, axis=(3, 5), keepdims=True)
    scaled = banded * lax.rsqrt(power + 1e-06) * masks.astype(F32)[:, :, :, None, None, None]
    whitened = scaled.reshape(shape).astype(BF16).transpose(0, 1, 3, 2, 4)
    shape = whitened.shape
    whitened = whitened.reshape(shape[0], shape[1], shape[2] * shape[3], shape[4])
    return [whitened[:, w] for w in range(shape[1])]


def pair_index(pair_rows, stations, group_index, groups):
    first, second = pair_rows[:, 0], pair_rows[:, 1]
    local = jnp.mod(second, stations)
    relative = jnp.mod(second // stations - group_index + 1, groups)
    number = jnp.arange(stations, dtype=jnp.int32)

    def slot(side):
        used = jnp.logical_and(relative[:, None] == side, local[:, None] == number[None, :])
        used = jnp.any(used, 0)
        return jnp.sum(jnp.where(jnp.logical_and(used[None, :], number[None, :] < local[:, None]), 1, 0), 1)

    spot = jnp.where(
        relative == 0, slot(0), jnp.where(relative == 1, NEAR + local, NEAR + stations + slot(2))
    )
    return jnp.stack([jnp.mod(first, stations), spot]).astype(jnp.int32)


def on_device(spectra, masks, pair_rows, start_basis):
    stations, windows, seg, parts, freq = spectra.shape
    rank, lags = start_basis.shape
    pairs = pair_rows.shape[0]
    groups = lax.axis_size("pairs")
    group_index = lax.axis_index("pairs")
    slices = lax.axis_size("hours")
    hour = lax.axis_index("hours")
    width = lags // slices
    chips = slices // 2
    forward = [(i, (i + 1) % groups) for i in range(groups)]
    backward = [(target, source) for source, target in forward]
    before = lax.ppermute(pair_rows, "pairs", forward)
    after = lax.ppermute(pair_rows, "pairs", backward)
    whitened = whiten(spectra, masks)
    index = pair_index(pair_rows, stations, group_index, groups)
    block = struct((NEAR, parts * seg, freq), BF16)
    sends = call(
        functools.partial(select_kernel, stations),
        [block] * (2 * windows),
        [SMEM] * 3 + [VMEM] * windows,
        [VMEM] * (2 * windows),
    )(group_index.reshape(1).astype(jnp.int32), before, after, *whitened)
    lows = [lax.ppermute(sends[w], "pairs", forward) for w in range(windows)]
    highs = [lax.ppermute(sends[windows + w], "pairs", backward) for w in range(windows)]
    table = jnp.asarray(kernel_table(freq, lags))
    pick = jnp.asarray(pick_matrix(pairs, seg, rank))
    spread = jnp.asarray(spread_matrix(pairs, seg, rank))
    core = jnp.mod(hour, 2).reshape(1).astype(jnp.int32)
    chip = (hour // 2).reshape(1).astype(jnp.int32)
    height = -(-(rank + 1) * pairs // 16) * 16
    total_windows = windows * slices
    partial, stacks = None, []
    for w in range(windows):
        last = w == windows - 1
        sizes = (pairs, seg, rank, lags, freq, total_windows, slices, w == 0)
        scratch = [
            pltpu.VMEM((stations + 2 * NEAR, parts * seg, freq), BF16),
            pltpu.VMEM((pairs * seg, parts * freq), BF16),
            pltpu.VMEM((HEAD, lags), F32),
            pltpu.VMEM((HEAD, lags), BF16),
            pltpu.VMEM((HEAD, lags), BF16),
        ]
        args = [index, whitened[w], lows[w], highs[w], table, start_basis, pick, spread]
        specs = [SMEM] + [VMEM] * 7
        outs = [struct((pairs, lags))]
        if w == 0:
            outs.append(struct((height, lags)))
        else:
            args += [core, partial]
            specs += [SMEM, VMEM]
            outs += [struct((chips, height, width), BF16), struct((chips, height, width))]
            scratch.append(pltpu.VMEM((slices, height, width), F32))
        result = call(
            functools.partial(window_kernel, sizes),
            outs,
            specs,
            [VMEM] * len(outs),
            scratch,
            flops=2 * pairs * seg * parts * freq * lags,
            moved=parts * freq * lags * 2,
        )(*args)
        stacks.append(result[0])
        if w == 0:
            partial = result[1]
        else:
            send, keep = result[1:]
    window_stacks = jnp.stack(stacks, 1)
    swap = lambda value, step: lax.ppermute(value, "hours", [(k, k ^ step) for k in range(slices)])
    got = swap(send, 1)
    piece = struct((height, width))
    pieces = call(
        add_kernel,
        [piece] + [struct((height, width), BF16)] * (chips - 1),
        [SMEM, VMEM, VMEM],
        [VMEM] * chips,
    )(chip, keep, got)
    arrived = [swap(one, 2 * (step + 1)) for step, one in enumerate(pieces[1:])]
    total, gram = call(
        functools.partial(gram_kernel, pairs, rank),
        [piece, struct((pairs, 128))],
        [VMEM] * chips,
        [VMEM] * 2,
    )(pieces[0], *arrived)
    gram = gram + swap(gram, 1)
    grams = [gram] + [swap(gram, 2 * (step + 1)) for step in range(chips - 1)]
    stack, basis = call(
        functools.partial(finish_kernel, pairs, rank, lags),
        [struct((pairs, width)), struct((pairs, rank, width))],
        [VMEM] * (chips + 1),
        [VMEM] * 2,
    )(total, *grams)
    return (window_stacks, stack, basis)


def solution(mesh):
    in_specs = (
        P("pairs", "hours", None, None, None),
        P("pairs", "hours", None),
        P("pairs", None),
        P(),
    )
    out_specs = (P("pairs", "hours", None), P("pairs", "hours"), P("pairs", None, "hours"))
    return jax.shard_map(
        on_device, mesh=mesh, in_specs=in_specs, out_specs=out_specs, check_vma=False
    )
```

time: 167 us -> 52.2 us (0.31)
  waiting for transfers between devices: 54.4 us -> 9.51 us
  other arithmetic: 46.7 us -> 6.14 us
  matrix products: 36.1 us -> 0 us
  starting transfers between devices: 5.2 us -> 20 us
  between operations: 14.3 us -> 0.88 us
  Pallas kernels: 0 us -> 9.19 us
  local copies, waits for them, and re-layouts: 9.8 us -> 6.15 us
    psum x1 -> x0, waiting for transfers between devices: 54.4 us -> none  [on_device(): merged, stack_whole = lax.psum((merged_terms, stack_terms), 'hours')]
    dot_general x12 -> x0, matrix products: 36.1 us -> none  [the longest x3 10.7 us: power_step(): proj = jnp.einsum('pwrl,pwgl->pwrg', basis, corr, precision=HIGH)]
    another operation x1 -> x2, other arithmetic: 35.8 us -> 0.03 us  [the longest x1 0.02 us: on_device(): window_stacks = jnp.stack(stacks, 1)]
    ppermute x2 -> x14, starting transfers between devices: 5.17 us -> 20 us  [the longest x2 7.68 us: on_device(): lax.ppermute(sends[windows + w], 'pairs', backward)]
    ppermute x2 -> x14, waiting for transfers between devices: 0.01 us -> 9.51 us  [the longest x8 8.12 us: on_device(): lax.ppermute(value, 'hours', [(k, k ^ step) for k in range(slices)])]
    pallas_call x0 -> x6, Pallas kernels: none -> 9.19 us  [the longest x2 6.93 us: on_device(): call(functools.partial(window_kernel, sizes), outs, specs, [VMEM] * len(o...]
    div x4 -> x0, other arithmetic: 6.5 us -> none  [the longest x3 5.83 us: from_gram(): result.append(current / lower[row][row][..., None])]
    unnamed x12 -> x14, local copies, waits for them, and re-layouts: 1.83 us -> 5.08 us
  transfers between devices with their start and end apart: 3 -> 14, of which waited for: 1 -> 9; matrix products, arithmetic and copies ran while one was open for 22% -> 15% of each run, Pallas kernels for 0% -> 7%
where the time goes in v1:
time: 52.2 us; the launch traced here: 51.9 us
  starting transfers between devices  20 us (38%)
  waiting for transfers between devices  9.51 us (18%)
  Pallas kernels  9.19 us (18%)
  local copies, waits for them, and re-layouts  6.15 us (12%)
  other arithmetic  6.14 us (12%)
  between operations  0.88 us (2%)
    ppermute x8, waiting for transfers between devices, on_device(): lax.ppermute(value, 'hours', [(k, k ^ step) for k in range(slices)])  8.12 us
    ppermute x2, starting transfers between devices, on_device(): lax.ppermute(sends[windows + w], 'pairs', backward)  7.68 us
    ppermute x8, starting transfers between devices, on_device(): lax.ppermute(value, 'hours', [(k, k ^ step) for k in range(slices)])  7.18 us
    pallas_call x2, Pallas kernels, on_device(): call(functools.partial(window_kernel, sizes), outs, specs, [VMEM] * len(o...  6.93 us
    unnamed x14, local copies, waits for them, and re-layouts  5.08 us
    ppermute x1, starting transfers between devices, on_device(): after = lax.ppermute(pair_rows, 'pairs', backward)  5.05 us
    reduce_sum x2, other arithmetic, whiten(): power = jnp.mean(banded * banded, axis=(3, 5), keepdims=True)  2.77 us
    transpose x1, other arithmetic, whiten(): whitened = scaled.reshape(shape).astype(BF16).transpose(0, 1, 3, 2, 4)  1.64 us
  transfers between devices with their start and end apart: 14, of which 9 were waited for; matrix products, arithmetic and copies ran while one was open for 15% of the time, Pallas kernels for 7%

profile of v1, /device:TPU:0, one launch (start us, length us, event | category | flops | bytes accessed | tf_op | source)
XLA Modules:
  0.0 51.9 jit_solution(922884216342212421)
XLA Ops:
  0.6 0.0 copy-start.2
  0.6 0.0 copy-start.3
  0.7 0.0 copy-start.5
  0.7 0.8 %copy.15 = s32[12,2]{1,0:T(8,128)S(1)} copy(s32[12,2]{0,1:T(2,128)} %param.9) | data formatting | bytes 192 | tf_op args[2]
  1.5 5.0 %collective-permute-start.1 = (s32[12,2]{1,0:T(8,128)S(1)}, s32[12,2]{1,0:T(8,128)S(1)}, u32[]{:S(2)}, u32[]{:S(2)}) collective-permute-start(s32[12,2]{1,0:T(8,128)S(1)} %copy.15), channel_id=1, source_target_pairs={{8,0},{16,8},{24,16},{0,24},{9,1},{17,9},{25,17},{1,25},{10,2},{18... | collective-permute-start | bytes 296 | tf_op jit(solution)/shard_map/ppermute | solution.py:329
  6.6 0.0 collective-permute-start
  6.6 0.7 %compare_bitcast_fusion.1 = (pred[12]{0:T(512)(128)(4,1)S(1)}, s32[12,1]{0,1:T(1,128)S(1)}, s32[12,1]{0,1:T(1,128)S(1)}) fusion(s32[]{:T(128)} %axis_index.23, s32[12,2]{0,1:T(2,128)} %param.9), kind=kLoop, calls=%fused_computation.31 | loop fusion | flops 348 | bytes 160 | tf_op jit(solution)/shard_map/and | solution.py:306
  7.3 0.7 %convert_element_type.10 = f32[8,2,8]{2,1,0:T(2,128)S(1)} convert(s32[8,2,8]{2,1,0:T(2,128)} %param.8) | non-fusion elementwise | flops 128 | bytes 1024 | tf_op jit(solution)/shard_map/convert_element_type | solution.py:292
  8.0 2.4 %fusion = f32[8,2,8,1024]{3,2,1,0:T(8,128)S(1)} fusion(bf16[8,2,8,2,1024]{4,3,2,1,0:T(2,128)(2,1)} %param.7), kind=kLoop, calls=%fused_computation.2 | loop fusion | flops 655360 | bytes 1048576 | tf_op jit(solution)/shard_map/reduce_sum | solution.py:291
  10.4 0.3 reduce_sum.40
  10.7 0.3 reduce_sum.41
  11.1 0.3 mul.27
  11.4 0.3 mul.28
  11.7 1.6 %fusion.3 = bf16[8,2,2,8,1024]{4,2,3,1,0:T(2,128)(2,1)S(1)} fusion(bf16[8,2,8,2,1024]{4,3,2,1,0:T(2,128)(2,1)} %param.7, f32[8,2,8]{2,1,0:T(2,128)S(1)} %convert_element_type.10, f32[8,2,8,1024]{3,2,1,0:T(8,128)S(1)} %mul.28), kind=kLoop, calls=%fused_computation.5 | loop fusion | flops 1048576 | bytes 1573376 | tf_op jit(solution)/shard_map/transpose | solution.py:293
  13.4 0.1 copy.19
  13.6 0.1 fusion.9
  13.7 0.1 select_reduce_fusion
  13.8 0.0 collective-permute-done.1.after
  13.8 0.0 collective-permute-done.before
  13.8 1.0 %shard_map.94 = (bf16[4,16,1024]{2,1,0:T(8,128)(2,1)S(1)}, bf16[4,16,1024]{2,1,0:T(8,128)(2,1)S(1)}, bf16[4,16,1024]{2,1,0:T(8,128)(2,1)S(1)}, bf16[4,16,1024]{2,1,0:T(8,128)(2,1)S(1)}) custom-call(s32[1]{0:T(128)} %bitcast.10.place, s32[12,2]{1,0:T(8,128)S(1)} %collective-permute-done.before, s32[12,2]{1,0:T(8,128)S(1)} %collective-permute-done.1.after, ...), custom_call_target="tpu_custom_call" | custom-call | tf_op jit(solution)/shard_map/pallas_call | solution.py:333
  14.8 0.1 collective-permute-start.2
  14.9 3.9 %collective-permute-start.3 = (bf16[4,16,1024]{2,1,0:T(8,128)(2,1)S(1)}, bf16[4,16,1024]{2,1,0:T(8,128)(2,1)S(1)}, u32[]{:S(2)}, u32[]{:S(2)}) collective-permute-start(bf16[4,16,1024]{2,1,0:T(8,128)(2,1)S(1)} %get-tuple-element.21), channel_id=1, source_target_pairs={{8,0},{16,8},{24,16},{0,24},{9,1},{17,9},{25,17},{1,25},{10,2},{18... | collective-permute-start | bytes 393224 | tf_op jit(solution)/shard_map/ppermute | solution.py:340
  18.8 0.1 collective-permute-start.4
  18.9 3.8 %collective-permute-start.5 = (bf16[4,16,1024]{2,1,0:T(8,128)(2,1)S(1)}, bf16[4,16,1024]{2,1,0:T(8,128)(2,1)S(1)}, u32[]{:S(2)}, u32[]{:S(2)}) collective-permute-start(bf16[4,16,1024]{2,1,0:T(8,128)(2,1)S(1)} %get-tuple-element.24), channel_id=1, source_target_pairs={{8,0},{16,8},{24,16},{0,24},{9,1},{17,9},{25,17},{1,25},{10,2},{18... | collective-permute-start | bytes 393224 | tf_op jit(solution)/shard_map/ppermute | solution.py:340
  22.7 0.3 collective-permute-done.2.low
  23.0 1.1 %collective-permute-done.3.high = bf16[4,16,1024]{2,1,0:T(8,128)(2,1)S(1)} collective-permute-done((bf16[4,16,1024]{2,1,0:T(8,128)(2,1)S(1)}, bf16[4,16,1024]{2,1,0:T(8,128)(2,1)S(1)}, u32[]{:S(2)}, u32[]{:S(2)}) %collective-permute-start.3) | collective-permute-done | bytes 131104 | tf_op jit(solution)/shard_map/ppermute | solution.py:340
  24.1 0.0 copy-start
  24.1 3.4 %copy-done = bf16[2048,2048]{1,0:T(8,128)(2,1)S(1)} copy-done((bf16[2048,2048]{1,0:T(8,128)(2,1)S(1)}, bf16[2048,2048]{1,0:T(8,128)(2,1)}, u32[]{:S(2)}) %copy-start) | copy-done | bytes 8388632
  27.5 3.4 %shard_map.95 = (f32[12,2048]{1,0:T(8,128)S(1)}, f32[64,2048]{1,0:T(8,128)S(1)}) custom-call(s32[2,12]{1,0:T(2,128)S(1)} %pad_add_fusion.index, bf16[8,16,1024]{2,1,0:T(8,128)(2,1)S(1)} %get-tuple-element.50.refs_0_.own, bf16[4,16,1024]{2,1,0:T(8,128)(2,1)S(1)} %collective-permute-done.2.low, bf16[4,16,1024]{2,1,0:T(8,128)(2,1)S(1)} %collective-permute-done.3.high, ...), custom_call_target="tpu_custom_call" | custom-call | flops 805306368 | bytes 8388608 | tf_op jit(solution)/shard_map/pallas_call | solution.py:369
  30.9 3.5 %shard_map.96 = (f32[12,2048]{1,0:T(8,128)S(1)}, bf16[4,64,256]{2,1,0:T(8,128)(2,1)S(1)}, f32[4,64,256]{2,1,0:T(8,128)S(1)}) custom-call(s32[2,12]{1,0:T(2,128)S(1)} %pad_add_fusion.index, bf16[8,16,1024]{2,1,0:T(8,128)(2,1)S(1)} %get-tuple-element.51.refs_1_.own, bf16[4,16,1024]{2,1,0:T(8,128)(2,1)S(1)} %collective-permute-done.4.low, ...), custom_call_target="tpu_custom_call" | custom-call | flops 805306368 | bytes 8388608 | tf_op jit(solution)/shard_map/pallas_call | solution.py:369
  34.4 0.1 collective-permute-start.6
  34.5 1.3 %collective-permute-done.6.got = bf16[4,64,256]{2,1,0:T(8,128)(2,1)S(1)} collective-permute-done((bf16[4,64,256]{2,1,0:T(8,128)(2,1)S(1)}, bf16[4,64,256]{2,1,0:T(8,128)(2,1)S(1)}, u32[]{:S(2)}, u32[]{:S(2)}) %collective-permute-start.6) | collective-permute-done | bytes 131104 | tf_op jit(solution)/shard_map/ppermute | solution.py:384
  35.9 1.6 %collective-permute-start.7 = (bf16[64,256]{1,0:T(8,128)(2,1)S(1)}, bf16[64,256]{1,0:T(8,128)(2,1)S(1)}, u32[]{:S(2)}, u32[]{:S(2)}) collective-permute-start(bf16[64,256]{1,0:T(8,128)(2,1)S(1)} %get-tuple-element.30), channel_id=1, source_target_pairs={{0,2},{1,3},{2,0},{3,1},{4,6},{5,7},{6,4},{7,5},{8,10},{9,11},{10,... | collective-permute-start | bytes 98312 | tf_op jit(solution)/shard_map/ppermute | solution.py:384
  37.4 1.5 %collective-permute-start.8 = (bf16[64,256]{1,0:T(8,128)(2,1)S(1)}, bf16[64,256]{1,0:T(8,128)(2,1)S(1)}, u32[]{:S(2)}, u32[]{:S(2)}) collective-permute-start(bf16[64,256]{1,0:T(8,128)(2,1)S(1)} %get-tuple-element.31), channel_id=1, source_target_pairs={{0,4},{1,5},{2,6},{3,7},{4,0},{5,1},{6,2},{7,3},{8,12},{9,13},{10,... | collective-permute-start | bytes 98312 | tf_op jit(solution)/shard_map/ppermute | solution.py:384
  39.0 0.5 collective-permute-start.9
  39.4 0.4 collective-permute-done.7.refs_0_
  39.9 1.5 %collective-permute-done.8.refs_1_ = bf16[64,256]{1,0:T(8,128)(2,1)S(1)} collective-permute-done((bf16[64,256]{1,0:T(8,128)(2,1)S(1)}, bf16[64,256]{1,0:T(8,128)(2,1)S(1)}, u32[]{:S(2)}, u32[]{:S(2)}) %collective-permute-start.8) | collective-permute-done | bytes 32800 | tf_op jit(solution)/shard_map/ppermute | solution.py:384
  41.4 2.4 %collective-permute-done.9.refs_2_ = bf16[64,256]{1,0:T(8,128)(2,1)S(1)} collective-permute-done((bf16[64,256]{1,0:T(8,128)(2,1)S(1)}, bf16[64,256]{1,0:T(8,128)(2,1)S(1)}, u32[]{:S(2)}, u32[]{:S(2)}) %collective-permute-start.9) | collective-permute-done | bytes 32800 | tf_op jit(solution)/shard_map/ppermute | solution.py:384
  43.8 0.1 shard_map.98
  43.9 0.1 collective-permute-start.10
  44.0 1.2 %collective-permute-done.10 = f32[12,128]{1,0:T(8,128)S(1)} collective-permute-done((f32[12,128]{1,0:T(8,128)S(1)}, f32[12,128]{1,0:T(8,128)S(1)}, u32[]{:S(2)}, u32[]{:S(2)}) %collective-permute-start.10) | collective-permute-done | bytes 6176 | tf_op jit(solution)/shard_map/ppermute | solution.py:384
  45.1 0.5 collective-permute-start.13
  45.6 1.5 %collective-permute-start.12 = (f32[12,128]{1,0:T(8,128)S(1)}, f32[12,128]{1,0:T(8,128)S(1)}, u32[]{:S(2)}, u32[]{:S(2)}) collective-permute-start(f32[12,128]{1,0:T(8,128)S(1)} %add.121.refs_0_), channel_id=1, source_target_pairs={{0,4},{1,5},{2,6},{3,7},{4,0},{5,1},{6,2},{7,3},{8,12},{9,13},{10,... | collective-permute-start | bytes 18440 | tf_op jit(solution)/shard_map/ppermute | solution.py:384
  47.1 1.5 %collective-permute-start.11 = (f32[12,128]{1,0:T(8,128)S(1)}, f32[12,128]{1,0:T(8,128)S(1)}, u32[]{:S(2)}, u32[]{:S(2)}) collective-permute-start(f32[12,128]{1,0:T(8,128)S(1)} %add.121.refs_0_), channel_id=1, source_target_pairs={{0,2},{1,3},{2,0},{3,1},{4,6},{5,7},{6,4},{7,5},{8,10},{9,11},{10,... | collective-permute-start | bytes 18440 | tf_op jit(solution)/shard_map/ppermute | solution.py:384
  48.6 0.8 %copy.17 = f32[12,2,2048]{2,1,0:T(2,128)} copy(f32[12,2,2048]{2,0,1:T(8,128)S(1)} %pad_maximum_fusion) | data formatting | bytes 393216
  49.5 0.2 collective-permute-done.13.refs_3_
  49.7 1.1 %collective-permute-done.11.refs_1_ = f32[12,128]{1,0:T(8,128)S(1)} collective-permute-done((f32[12,128]{1,0:T(8,128)S(1)}, f32[12,128]{1,0:T(8,128)S(1)}, u32[]{:S(2)}, u32[]{:S(2)}) %collective-permute-start.11) | collective-permute-done | bytes 6176 | tf_op jit(solution)/shard_map/ppermute | solution.py:384
  50.8 1.1 %shard_map.99 = (f32[12,256]{1,0:T(8,128)}, f32[12,4,256]{2,1,0:T(4,128)}) custom-call(f32[64,256]{1,0:T(8,128)S(1)} %get-tuple-element.33.total, f32[12,128]{1,0:T(8,128)S(1)} %add.121.refs_0_, f32[12,128]{1,0:T(8,128)S(1)} %collective-permute-done.11.refs_1_, f32[12,128]{1,0:T(8,128)S(1)} %collective-permute-done.12.refs_2_, ...), custom_call_target="tpu_custom_call" | custom-call | tf_op jit(solution)/shard_map/pallas_call | solution.py:402
  (19 shorter events, 0.2 us)
Async XLA Ops:
  0.6 23.4 %copy-start.2 = (bf16[128,640]{1,0:T(8,128)(2,1)S(1)}, bf16[128,640]{1,0:T(8,128)(2,1)}, u32[]{:S(2)}) copy-start(bf16[128,640]{1,0:T(8,128)(2,1)} %constant.102.clone.spread) | copy-start | bytes 491524
  0.6 23.4 %copy-start.3 = (bf16[128,256]{1,0:T(8,128)(2,1)S(1)}, bf16[128,256]{1,0:T(8,128)(2,1)}, u32[]{:S(2)}) copy-start(bf16[128,256]{1,0:T(8,128)(2,1)} %constant.101.clone.pick) | copy-start | bytes 196612
  0.7 18.1 %copy-start.5 = (s32[12,2]{0,1:T(2,128)S(1)}, s32[12,2]{0,1:T(2,128)}, u32[]{:S(2)}) copy-start(s32[12,2]{0,1:T(2,128)} %param.9) | copy-start | bytes 292
  0.7 23.4 %copy-start.4 = (f32[4,2048]{1,0:T(4,128)S(1)}, f32[4,2048]{1,0:T(4,128)}, u32[]{:S(2)}) copy-start(f32[4,2048]{1,0:T(4,128)} %start.3) | copy-start | bytes 98308
  1.5 12.3 %collective-permute-start.1 = (s32[12,2]{1,0:T(8,128)S(1)}, s32[12,2]{1,0:T(8,128)S(1)}, u32[]{:S(2)}, u32[]{:S(2)}) collective-permute-start(s32[12,2]{1,0:T(8,128)S(1)} %copy.15), channel_id=1, source_target_pairs={{8,0},{16,8},{24,16},{0,24},{9,1},{17,9},{25,17},{1,25},{10,2},{18... | collective-permute-start | bytes 296 | tf_op jit(solution)/shard_map/ppermute | solution.py:329
  6.6 7.2 %collective-permute-start = (s32[12,2]{1,0:T(8,128)S(1)}, s32[12,2]{1,0:T(8,128)S(1)}, u32[]{:S(2)}, u32[]{:S(2)}) collective-permute-start(s32[12,2]{1,0:T(8,128)S(1)} %copy.15), channel_id=1, source_target_pairs={{0,8},{8,16},{16,24},{24,0},{1,9},{9,17},{17,25},{25,1},{2,10},{10... | collective-permute-start | bytes 296 | tf_op jit(solution)/shard_map/ppermute | solution.py:328
  14.8 8.2 %collective-permute-start.2 = (bf16[4,16,1024]{2,1,0:T(8,128)(2,1)S(1)}, bf16[4,16,1024]{2,1,0:T(8,128)(2,1)S(1)}, u32[]{:S(2)}, u32[]{:S(2)}) collective-permute-start(bf16[4,16,1024]{2,1,0:T(8,128)(2,1)S(1)} %get-tuple-element.20), channel_id=1, source_target_pairs={{0,8},{8,16},{16,24},{24,0},{1,9},{9,17},{17,25},{25,1},{2,10},{10... | collective-permute-start | bytes 393224 | tf_op jit(solution)/shard_map/ppermute | solution.py:339
  14.9 9.2 %collective-permute-start.3 = (bf16[4,16,1024]{2,1,0:T(8,128)(2,1)S(1)}, bf16[4,16,1024]{2,1,0:T(8,128)(2,1)S(1)}, u32[]{:S(2)}, u32[]{:S(2)}) collective-permute-start(bf16[4,16,1024]{2,1,0:T(8,128)(2,1)S(1)} %get-tuple-element.21), channel_id=1, source_target_pairs={{8,0},{16,8},{24,16},{0,24},{9,1},{17,9},{25,17},{1,25},{10,2},{18... | collective-permute-start | bytes 393224 | tf_op jit(solution)/shard_map/ppermute | solution.py:340
  18.8 12.1 %collective-permute-start.4 = (bf16[4,16,1024]{2,1,0:T(8,128)(2,1)S(1)}, bf16[4,16,1024]{2,1,0:T(8,128)(2,1)S(1)}, u32[]{:S(2)}, u32[]{:S(2)}) collective-permute-start(bf16[4,16,1024]{2,1,0:T(8,128)(2,1)S(1)} %get-tuple-element.23), channel_id=1, source_target_pairs={{0,8},{8,16},{16,24},{24,0},{1,9},{9,17},{17,25},{25,1},{2,10},{10... | collective-permute-start | bytes 393224 | tf_op jit(solution)/shard_map/ppermute | solution.py:339
  18.9 12.1 %collective-permute-start.5 = (bf16[4,16,1024]{2,1,0:T(8,128)(2,1)S(1)}, bf16[4,16,1024]{2,1,0:T(8,128)(2,1)S(1)}, u32[]{:S(2)}, u32[]{:S(2)}) collective-permute-start(bf16[4,16,1024]{2,1,0:T(8,128)(2,1)S(1)} %get-tuple-element.24), channel_id=1, source_target_pairs={{8,0},{16,8},{24,16},{0,24},{9,1},{17,9},{25,17},{1,25},{10,2},{18... | collective-permute-start | bytes 393224 | tf_op jit(solution)/shard_map/ppermute | solution.py:340
  24.1 3.4 %copy-start = (bf16[2048,2048]{1,0:T(8,128)(2,1)S(1)}, bf16[2048,2048]{1,0:T(8,128)(2,1)}, u32[]{:S(2)}) copy-start(bf16[2048,2048]{1,0:T(8,128)(2,1)} %constant.100.clone.table) | copy-start | bytes 25165828
  27.5 3.5 %copy-start.1 = (bf16[2048,2048]{1,0:T(8,128)(2,1)S(1)}, bf16[2048,2048]{1,0:T(8,128)(2,1)}, u32[]{:S(2)}) copy-start(bf16[2048,2048]{1,0:T(8,128)(2,1)} %constant.100.clone.table) | copy-start | bytes 25165828
  34.4 1.4 %collective-permute-start.6 = (bf16[4,64,256]{2,1,0:T(8,128)(2,1)S(1)}, bf16[4,64,256]{2,1,0:T(8,128)(2,1)S(1)}, u32[]{:S(2)}, u32[]{:S(2)}) collective-permute-start(bf16[4,64,256]{2,1,0:T(8,128)(2,1)S(1)} %get-tuple-element.28), channel_id=1, source_target_pairs={{0,1},{1,0},{2,3},{3,2},{4,5},{5,4},{6,7},{7,6},{8,9},{9,8},{10,11... | collective-permute-start | bytes 393224 | tf_op jit(solution)/shard_map/ppermute | solution.py:384
  35.9 4.0 %collective-permute-start.7 = (bf16[64,256]{1,0:T(8,128)(2,1)S(1)}, bf16[64,256]{1,0:T(8,128)(2,1)S(1)}, u32[]{:S(2)}, u32[]{:S(2)}) collective-permute-start(bf16[64,256]{1,0:T(8,128)(2,1)S(1)} %get-tuple-element.30), channel_id=1, source_target_pairs={{0,2},{1,3},{2,0},{3,1},{4,6},{5,7},{6,4},{7,5},{8,10},{9,11},{10,... | collective-permute-start | bytes 98312 | tf_op jit(solution)/shard_map/ppermute | solution.py:384
  37.4 3.9 %collective-permute-start.8 = (bf16[64,256]{1,0:T(8,128)(2,1)S(1)}, bf16[64,256]{1,0:T(8,128)(2,1)S(1)}, u32[]{:S(2)}, u32[]{:S(2)}) collective-permute-start(bf16[64,256]{1,0:T(8,128)(2,1)S(1)} %get-tuple-element.31), channel_id=1, source_target_pairs={{0,4},{1,5},{2,6},{3,7},{4,0},{5,1},{6,2},{7,3},{8,12},{9,13},{10,... | collective-permute-start | bytes 98312 | tf_op jit(solution)/shard_map/ppermute | solution.py:384
  39.0 4.8 %collective-permute-start.9 = (bf16[64,256]{1,0:T(8,128)(2,1)S(1)}, bf16[64,256]{1,0:T(8,128)(2,1)S(1)}, u32[]{:S(2)}, u32[]{:S(2)}) collective-permute-start(bf16[64,256]{1,0:T(8,128)(2,1)S(1)} %get-tuple-element.32), channel_id=1, source_target_pairs={{0,6},{1,7},{2,4},{3,5},{4,2},{5,3},{6,0},{7,1},{8,14},{9,15},{10,... | collective-permute-start | bytes 98312 | tf_op jit(solution)/shard_map/ppermute | solution.py:384
  43.9 1.2 %collective-permute-start.10 = (f32[12,128]{1,0:T(8,128)S(1)}, f32[12,128]{1,0:T(8,128)S(1)}, u32[]{:S(2)}, u32[]{:S(2)}) collective-permute-start(f32[12,128]{1,0:T(8,128)S(1)} %get-tuple-element.34), channel_id=1, source_target_pairs={{0,1},{1,0},{2,3},{3,2},{4,5},{5,4},{6,7},{7,6},{8,9},{9,8},{10,11... | collective-permute-start | bytes 18440 | tf_op jit(solution)/shard_map/ppermute | solution.py:384
  45.1 4.5 %collective-permute-start.13 = (f32[12,128]{1,0:T(8,128)S(1)}, f32[12,128]{1,0:T(8,128)S(1)}, u32[]{:S(2)}, u32[]{:S(2)}) collective-permute-start(f32[12,128]{1,0:T(8,128)S(1)} %add.121.refs_0_), channel_id=1, source_target_pairs={{0,6},{1,7},{2,4},{3,5},{4,2},{5,3},{6,0},{7,1},{8,14},{9,15},{10,... | collective-permute-start | bytes 18440 | tf_op jit(solution)/shard_map/ppermute | solution.py:384
  45.6 4.1 %collective-permute-start.12 = (f32[12,128]{1,0:T(8,128)S(1)}, f32[12,128]{1,0:T(8,128)S(1)}, u32[]{:S(2)}, u32[]{:S(2)}) collective-permute-start(f32[12,128]{1,0:T(8,128)S(1)} %add.121.refs_0_), channel_id=1, source_target_pairs={{0,4},{1,5},{2,6},{3,7},{4,0},{5,1},{6,2},{7,3},{8,12},{9,13},{10,... | collective-permute-start | bytes 18440 | tf_op jit(solution)/shard_map/ppermute | solution.py:384
  47.1 3.7 %collective-permute-start.11 = (f32[12,128]{1,0:T(8,128)S(1)}, f32[12,128]{1,0:T(8,128)S(1)}, u32[]{:S(2)}, u32[]{:S(2)}) collective-permute-start(f32[12,128]{1,0:T(8,128)S(1)} %add.121.refs_0_), channel_id=1, source_target_pairs={{0,2},{1,3},{2,0},{3,1},{4,6},{5,7},{6,4},{7,5},{8,10},{9,11},{10,... | collective-permute-start | bytes 18440 | tf_op jit(solution)/shard_map/ppermute | solution.py:384

commit v2 on v1

--- a/solution.py
+++ b/solution.py
@@ -16,6 +16,7 @@
 BF16 = jnp.bfloat16
 VMEM = pl.BlockSpec(memory_space=pltpu.VMEM)
 SMEM = pl.BlockSpec(memory_space=pltpu.SMEM)
+HBM = pl.BlockSpec(memory_space=pltpu.HBM)
 HEAD = 128
 LANE = 16
 
@@ -98,28 +99,108 @@
     return result
 
 
-def select_kernel(stations, place, before, after, *refs):
-    windows = len(refs) // 3
-    whitened, to_next, to_last = refs[:windows], refs[windows : 2 * windows], refs[2 * windows :]
-    low = place[0] * stations
-    for rows, outs in ((after, to_next), (before, to_last)):
-        needed = jnp.int32(0)
-        for row in range(rows.shape[0]):
-            local = rows[row, 1] - low
-            here = jnp.logical_and(local >= 0, local < stations)
-            bit = jnp.left_shift(jnp.int32(1), jnp.clip(local, 0, stations - 1))
-            needed = jnp.where(here, jnp.bitwise_or(needed, bit), needed)
-        slot = jnp.int32(0)
-        for station in range(stations):
-            wanted = jnp.bitwise_and(jnp.right_shift(needed, station), 1)
-            spot = jnp.minimum(slot, NEAR - 1)
-
-            @pl.when(wanted == 1)
-            def _():
-                for source, target in zip(whitened, outs):
-                    target[spot] = source[station]
-
-            slot = slot + wanted
+def popcount(bits):
+    bits = bits - jnp.bitwise_and(jnp.right_shift(bits, 1), 0x55555555)
+    bits = jnp.bitwise_and(bits, 0x33333333) + jnp.bitwise_and(jnp.right_shift(bits, 2), 0x33333333)
+    bits = jnp.bitwise_and(bits + jnp.right_shift(bits, 4), 0x0F0F0F0F)
+    bits = bits + jnp.right_shift(bits, 8)
+    return jnp.bitwise_and(bits + jnp.right_shift(bits, 16), 63)
+
+
+def used_stations(rows, low, stations):
+    used = jnp.int32(0)
+    for pair in range(rows.shape[1]):
+        local = rows[1, pair] - low
+        here = jnp.logical_and(local >= 0, local < stations)
+        bit = jnp.left_shift(jnp.int32(1), jnp.clip(local, 0, stations - 1))
+        used = jnp.bitwise_or(used, jnp.where(here, bit, 0))
+    return used
+
+
+def stage_kernel(*refs):
+    count = (len(refs) - 2) // 2
+    sources, targets, sems = refs[1 : 1 + count], refs[1 + count : -1], refs[-1]
+    copies = [
+        pltpu.make_async_copy(source, target, sems.at[number])
+        for number, (source, target) in enumerate(zip(sources, targets))
+    ]
+    for copy in copies:
+        copy.start()
+    for copy in copies:
+        copy.wait()
+
+
+def whiten_kernel(groups, place, far_rows, far_spectra, far_masks, index, *refs):
+    whitened, (spectra, masks, rows, sems) = refs[:-4], refs[-4:]
+    copies = [
+        pltpu.make_async_copy(far_spectra, spectra, sems.at[0]),
+        pltpu.make_async_copy(far_masks, masks, sems.at[1]),
+        pltpu.make_async_copy(far_rows, rows, sems.at[2]),
+    ]
+    for copy in copies:
+        copy.start()
+    stations, windows, seg, _, freq = spectra.shape
+    count = freq // BAND
+    band = lax.broadcasted_iota(jnp.int32, (count, freq), 0)
+    of_bin = lax.broadcasted_iota(jnp.int32, (count, freq), 1) // BAND
+    bands = jnp.where(band == of_bin, 1.0, 0.0).astype(BF16)
+    for copy in copies:
+        copy.wait()
+    before = lax.rem(place[0] + groups - 1, groups) * stations
+    after = lax.rem(place[0] + 1, groups) * stations
+    own = place[0] * stations
+    used_before = used_stations(rows, before, stations)
+    used_after = used_stations(rows, after, stations)
+    for pair in range(rows.shape[1]):
+        index[0, pair] = rows[0, pair] - own
+        second = rows[1, pair]
+        in_before = jnp.logical_and(second >= before, second < before + stations)
+        in_own = jnp.logical_and(second >= own, second < own + stations)
+        local = second - jnp.where(in_before, before, jnp.where(in_own, own, after))
+        below = jnp.left_shift(jnp.int32(1), local) - 1
+        slot = popcount(jnp.bitwise_and(jnp.where(in_before, used_before, used_after), below))
+        index[1, pair] = jnp.where(
+            in_before, slot, jnp.where(in_own, NEAR + local, NEAR + stations + slot)
+        )
+    values, squares, open_rows = [], [], []
+    eye = lax.broadcasted_iota(jnp.int32, (seg, seg), 0) == lax.broadcasted_iota(jnp.int32, (seg, seg), 1)
+    for station in range(stations):
+        for window in range(windows):
+            block = spectra[station, window].astype(F32)
+            real, imag = block[:, 0], block[:, 1]
+            values.append((real, imag))
+            squares.append(real * real + imag * imag)
+            mask = masks[station, window : window + 1].astype(F32)
+            mask = jnp.where(eye, jnp.broadcast_to(mask, (seg, seg)), 0.0)
+            open_rows.append(jnp.sum(mask, 1, keepdims=True))
+    high, low = two_parts(jnp.concatenate(squares, 0))
+    power = dot_rows(high, bands) + dot_rows(low, bands)
+    scale = lax.rsqrt(power * (1.0 / (2 * BAND)) + 1e-06) * jnp.concatenate(open_rows, 0)
+    high, low = two_parts(scale)
+    scale = dot(high, bands) + dot(low, bands)
+    at = 0
+    for station in range(stations):
+        for window in range(windows):
+            real, imag = values[at]
+            here = scale[at * seg : (at + 1) * seg]
+            whitened[window][station] = jnp.concatenate([real * here, imag * here], 0).astype(BF16)
+            at += 1
+
+
+def select_kernel(stations, place, rows, *refs):
+    windows = len(refs) // 2
+    needed = used_stations(rows, place[0] * stations, stations)
+    slot = jnp.int32(0)
+    for station in range(stations):
+        wanted = jnp.bitwise_and(jnp.right_shift(needed, station), 1)
+        spot = jnp.minimum(slot, NEAR - 1)
+
+        @pl.when(wanted == 1)
+        def _():
+            for source, target in zip(refs[:windows], refs[windows:]):
+                target[spot] = source[station]
+
+        slot = slot + wanted
 
 
 def window_kernel(sizes, index, own, low, high, table, start, pick, spread, *refs):
@@ -233,34 +314,52 @@
             keep_out[piece] = pieces[2 * piece + core[0]]
 
 
-def add_kernel(chip, keep, got, mine_out, *sends):
-    mine_out[...] = keep[chip[0]] + got[chip[0]].astype(F32)
+def add_kernel(top, chip, keep, got, mine_out, *sends):
+    chips, height, _ = keep.shape
+    for part in range(chips):
+        both = keep[part] + got[part].astype(F32)
+        mine_out[part] = both
+        short = both[0:top].astype(BF16)
+        for out in sends:
+            out[part * top : (part + 1) * top] = short
     for step, out in enumerate(sends):
         other = jnp.bitwise_xor(chip[0], step + 1)
-        out[...] = (keep[other] + got[other].astype(F32)).astype(BF16)
-
-
-def gram_kernel(pairs, rank, mine, *refs):
-    got, (total_out, gram_out) = refs[:-2], refs[-2:]
-    total = mine[...]
+        out[chips * top :] = mine_out[other, top:height].astype(BF16)
+
+
+def gram_kernel(pairs, rank, chip, mine, *refs):
+    got, (total_out, gram_out, parts) = refs[:-3], refs[-3:]
+    chips, height, width = mine.shape
+    top = rank * pairs
+    sums = [[jnp.zeros((pairs, width), F32) for _ in range(r + 1)] for r in range(rank)]
+    for part in range(chips):
+        block = mine[part, 0:top].astype(BF16).astype(F32)
+        for one in got:
+            block = block + one[part * top : (part + 1) * top].astype(F32)
+        parts[part] = block
+        rows = [block[r * pairs : (r + 1) * pairs] for r in range(rank)]
+        sums = [[sums[r][s] + rows[r] * rows[s] for s in range(r + 1)] for r in range(rank)]
+    stack = mine[chip[0], top:height]
     for one in got:
-        total = total + one[...].astype(F32)
-    total_out[...] = total
-    rows = [total[r * pairs : (r + 1) * pairs] for r in range(rank)]
+        stack = stack + one[chips * top :].astype(F32)
+    total_out[0:top] = parts[chip[0]]
+    total_out[top:] = stack
     lane = lax.broadcasted_iota(jnp.int32, (pairs, 128), 1)
     gram = jnp.zeros((pairs, 128), F32)
     for r in range(rank):
         for s in range(r + 1):
-            gram = jnp.where(lane == r * rank + s, jnp.sum(rows[r] * rows[s], 1, keepdims=True), gram)
+            value = jnp.sum(sums[r][s], 1, keepdims=True)
+            gram = jnp.where(lane == r * rank + s, value, gram)
     gram_out[...] = gram
 
 
-def finish_kernel(pairs, rank, lags, total, *refs):
-    grams, (stack_out, basis_out) = refs[:-2], refs[-2:]
-    gram = grams[0][...]
-    for one in grams[1:]:
-        gram = gram + one[...]
-    entries = [[gram[:, r * rank + s : r * rank + s + 1] for s in range(r + 1)] for r in range(rank)]
+def finish_kernel(pairs, rank, lags, total, mine, got, stack_out, basis_out):
+    gram = mine[...] + got[...]
+    shape = (pairs, total.shape[1])
+    entries = [
+        [jnp.broadcast_to(gram[:, r * rank + s : r * rank + s + 1], shape) for s in range(r + 1)]
+        for r in range(rank)
+    ]
     lower, inverse = lower_factor(entries, rank)
     rows = [total[r * pairs : (r + 1) * pairs] for r in range(rank)]
     for r, row in enumerate(solve_rows(rows, lower, inverse)):
@@ -275,42 +374,17 @@
         in_specs=in_specs,
         out_specs=out_specs,
         scratch_shapes=list(scratch),
-        compiler_params=pltpu.CompilerParams(vmem_limit_bytes=32 * 1024 * 1024),
+        compiler_params=pltpu.CompilerParams(vmem_limit_bytes=12 * 1024 * 1024),
         cost_estimate=pl.CostEstimate(flops=flops, bytes_accessed=moved, transcendentals=0),
     )
 
 
+def far(value):
+    return pltpu.with_memory_space_constraint(value, pltpu.HBM)
+
+
 def struct(shape, dtype=F32):
     return jax.ShapeDtypeStruct(shape, dtype)
-
-
-def whiten(spectra, masks):
-    values = spectra.astype(F32)
-    shape = values.shape
-    banded = values.reshape(shape[:-1] + (shape[-1] // BAND, BAND))
-    power = jnp.mean(banded * banded, axis=(3, 5), keepdims=True)
-    scaled = banded * lax.rsqrt(power + 1e-06) * masks.astype(F32)[:, :, :, None, None, None]
-    whitened = scaled.reshape(shape).astype(BF16).transpose(0, 1, 3, 2, 4)
-    shape = whitened.shape
-    whitened = whitened.reshape(shape[0], shape[1], shape[2] * shape[3], shape[4])
-    return [whitened[:, w] for w in range(shape[1])]
-
-
-def pair_index(pair_rows, stations, group_index, groups):
-    first, second = pair_rows[:, 0], pair_rows[:, 1]
-    local = jnp.mod(second, stations)
-    relative = jnp.mod(second // stations - group_index + 1, groups)
-    number = jnp.arange(stations, dtype=jnp.int32)
-
-    def slot(side):
-        used = jnp.logical_and(relative[:, None] == side, local[:, None] == number[None, :])
-        used = jnp.any(used, 0)
-        return jnp.sum(jnp.where(jnp.logical_and(used[None, :], number[None, :] < local[:, None]), 1, 0), 1)
-
-    spot = jnp.where(
-        relative == 0, slot(0), jnp.where(relative == 1, NEAR + local, NEAR + stations + slot(2))
-    )
-    return jnp.stack([jnp.mod(first, stations), spot]).astype(jnp.int32)
 
 
 def on_device(spectra, masks, pair_rows, start_basis):
@@ -325,22 +399,48 @@
     chips = slices // 2
     forward = [(i, (i + 1) % groups) for i in range(groups)]
     backward = [(target, source) for source, target in forward]
-    before = lax.ppermute(pair_rows, "pairs", forward)
-    after = lax.ppermute(pair_rows, "pairs", backward)
-    whitened = whiten(spectra, masks)
-    index = pair_index(pair_rows, stations, group_index, groups)
+    rows = pair_rows.T
+    before = lax.ppermute(rows, "pairs", forward)
+    after = lax.ppermute(rows, "pairs", backward)
+    place = group_index.reshape(1).astype(jnp.int32)
+    index, *whitened = call(
+        functools.partial(whiten_kernel, groups),
+        [struct(rows.shape, jnp.int32)] + [struct((stations, parts * seg, freq), BF16)] * windows,
+        [SMEM, HBM, HBM, HBM],
+        [SMEM] + [VMEM] * windows,
+        [
+            pltpu.VMEM(spectra.shape, BF16),
+            pltpu.VMEM(masks.shape, jnp.int32),
+            pltpu.SMEM(rows.shape, jnp.int32),
+            pltpu.SemaphoreType.DMA((3,)),
+        ],
+    )(place, far(rows), far(spectra), far(masks))
     block = struct((NEAR, parts * seg, freq), BF16)
-    sends = call(
-        functools.partial(select_kernel, stations),
-        [block] * (2 * windows),
-        [SMEM] * 3 + [VMEM] * windows,
-        [VMEM] * (2 * windows),
-    )(group_index.reshape(1).astype(jnp.int32), before, after, *whitened)
-    lows = [lax.ppermute(sends[w], "pairs", forward) for w in range(windows)]
-    highs = [lax.ppermute(sends[windows + w], "pairs", backward) for w in range(windows)]
-    table = jnp.asarray(kernel_table(freq, lags))
-    pick = jnp.asarray(pick_matrix(pairs, seg, rank))
-    spread = jnp.asarray(spread_matrix(pairs, seg, rank))
+    def select(wanted):
+        return call(
+            functools.partial(select_kernel, stations),
+            [block] * windows,
+            [SMEM] * 2 + [VMEM] * windows,
+            [VMEM] * windows,
+        )(place, wanted, *whitened)
+
+    to_next, to_last = select(after), select(before)
+    lows = [lax.ppermute(one, "pairs", forward) for one in to_next]
+    highs = [lax.ppermute(one, "pairs", backward) for one in to_last]
+    fixed = [
+        jnp.asarray(kernel_table(freq, lags)),
+        start_basis,
+        jnp.asarray(pick_matrix(pairs, seg, rank)),
+        jnp.asarray(spread_matrix(pairs, seg, rank)),
+    ]
+    table, start, pick, spread = call(
+        stage_kernel,
+        [struct(one.shape, one.dtype) for one in fixed],
+        [VMEM] + [HBM] * len(fixed),
+        [VMEM] * len(fixed),
+        [pltpu.SemaphoreType.DMA((len(fixed),))],
+        moved=parts * freq * lags * 2,
+    )(to_last[0], *[far(one) for one in fixed])
     core = jnp.mod(hour, 2).reshape(1).astype(jnp.int32)
     chip = (hour // 2).reshape(1).astype(jnp.int32)
     height = -(-(rank + 1) * pairs // 16) * 16
@@ -356,7 +456,7 @@
             pltpu.VMEM((HEAD, lags), BF16),
             pltpu.VMEM((HEAD, lags), BF16),
         ]
-        args = [index, whitened[w], lows[w], highs[w], table, start_basis, pick, spread]
+        args = [index, whitened[w], lows[w], highs[w], table, start, pick, spread]
         specs = [SMEM] + [VMEM] * 7
         outs = [struct((pairs, lags))]
         if w == 0:
@@ -383,28 +483,28 @@
     window_stacks = jnp.stack(stacks, 1)
     swap = lambda value, step: lax.ppermute(value, "hours", [(k, k ^ step) for k in range(slices)])
     got = swap(send, 1)
-    piece = struct((height, width))
-    pieces = call(
-        add_kernel,
-        [piece] + [struct((height, width), BF16)] * (chips - 1),
+    top = rank * pairs
+    message = struct((chips * top + height - top, width), BF16)
+    mine, *sends = call(
+        functools.partial(add_kernel, top),
+        [struct(keep.shape)] + [message] * (chips - 1),
         [SMEM, VMEM, VMEM],
         [VMEM] * chips,
     )(chip, keep, got)
-    arrived = [swap(one, 2 * (step + 1)) for step, one in enumerate(pieces[1:])]
+    arrived = [swap(one, 2 * (step + 1)) for step, one in enumerate(sends)]
     total, gram = call(
         functools.partial(gram_kernel, pairs, rank),
-        [piece, struct((pairs, 128))],
-        [VMEM] * chips,
+        [struct((height, width)), struct((pairs, 128))],
+        [SMEM] + [VMEM] * chips,
         [VMEM] * 2,
-    )(pieces[0], *arrived)
-    gram = gram + swap(gram, 1)
-    grams = [gram] + [swap(gram, 2 * (step + 1)) for step in range(chips - 1)]
+        [pltpu.VMEM((chips, top, width), F32)],
+    )(chip, mine, *arrived)
     stack, basis = call(
         functools.partial(finish_kernel, pairs, rank, lags),
         [struct((pairs, width)), struct((pairs, rank, width))],
-        [VMEM] * (chips + 1),
+        [VMEM] * 3,
         [VMEM] * 2,
-    )(total, *grams)
+    )(total, gram, swap(gram, 1))
     return (window_stacks, stack, basis)
 
 

time: 52.2 us -> 39.9 us (0.76)
  Pallas kernels: 9.19 us -> 15.5 us
  other arithmetic: 6.14 us -> 0.02 us
  local copies, waits for them, and re-layouts: 6.15 us -> 0.83 us
  starting transfers between devices: 20 us -> 14.7 us
  waiting for transfers between devices: 9.51 us -> 7.87 us
    pallas_call x3 -> x6, Pallas kernels: 1.12 us -> 7.84 us  [the longest x1 3.42 us: on_device(): call(stage_kernel, [struct(one.shape, one.dtype) for one in fixed], [VMEM...]
    unnamed x14 -> x1, local copies, waits for them, and re-layouts: 5.08 us -> 0.83 us
    ppermute x8 -> x5, starting transfers between devices: 7.18 us -> 3.69 us  [on_device(): lax.ppermute(value, 'hours', [(k, k ^ step) for k in range(slices)])]
    reduce_sum x3 -> x0, other arithmetic: 2.86 us -> none  [the longest x2 2.77 us: whiten(): power = jnp.mean(banded * banded, axis=(3, 5), keepdims=True)]
    ppermute x6, starting transfers between devices: 12.9 us -> 11.1 us  [the longest x2 5.77 us: on_device(): highs = [lax.ppermute(one, 'pairs', backward) for one in to_last]]
    transpose x1 -> x0, other arithmetic: 1.64 us -> none  [whiten(): whitened = scaled.reshape(shape).astype(BF16).transpose(0, 1, 3, 2, 4)]
    ppermute x8 -> x5, waiting for transfers between devices: 8.12 us -> 6.74 us  [on_device(): lax.ppermute(value, 'hours', [(k, k ^ step) for k in range(slices)])]
    and x2 -> x0, other arithmetic: 0.71 us -> none  [slot(): jnp.logical_and(relative[:, None] == side, local[:, None] == number[None,...]
  transfers between devices with their start and end apart: 14 -> 11, of which waited for: 9 -> 7; matrix products, arithmetic and copies ran while one was open for 15% -> 2% of each run, Pallas kernels for 7% -> 28%
where the time goes in v2:
time: 39.9 us; the launch traced here: 39.7 us
  Pallas kernels  15.5 us (39%)
  starting transfers between devices  14.7 us (37%)
  waiting for transfers between devices  7.87 us (20%)
  local copies, waits for them, and re-layouts  0.83 us (2%)
  between operations  0.75 us (2%)
    pallas_call x2, Pallas kernels, on_device(): call(functools.partial(window_kernel, sizes), outs, specs, [VMEM] * len(o...  6.94 us
    ppermute x5, waiting for transfers between devices, on_device(): lax.ppermute(value, 'hours', [(k, k ^ step) for k in range(slices)])  6.74 us
    ppermute x2, starting transfers between devices, on_device(): highs = [lax.ppermute(one, 'pairs', backward) for one in to_last]  5.77 us
    ppermute x5, starting transfers between devices, on_device(): lax.ppermute(value, 'hours', [(k, k ^ step) for k in range(slices)])  3.69 us
    pallas_call x1, Pallas kernels, on_device(): call(stage_kernel, [struct(one.shape, one.dtype) for one in fixed], [VMEM...  3.42 us
    ppermute x1, starting transfers between devices, on_device(): before = lax.ppermute(rows, 'pairs', forward)  3.08 us
    pallas_call x1, Pallas kernels, on_device(): call(functools.partial(whiten_kernel, groups), [struct(rows.shape, jnp.in...  2.91 us
    ppermute x1, starting transfers between devices, on_device(): after = lax.ppermute(rows, 'pairs', backward)  2.09 us
  transfers between devices with their start and end apart: 11, of which 7 were waited for; matrix products, arithmetic and copies ran while one was open for 2% of the time, Pallas kernels for 28%

profile of v2, /device:TPU:0, one launch (start us, length us, event | category | flops | bytes accessed | tf_op | source)
XLA Modules:
  0.0 39.7 jit_solution(7905386174481023779)
XLA Ops:
  0.6 3.1 %collective-permute-start.2 = (s32[2,12]{1,0:T(2,128)}, s32[2,12]{1,0:T(2,128)S(1)}, u32[]{:S(2)}, u32[]{:S(2)}) collective-permute-start(s32[2,12]{1,0:T(2,128)} %bitcast.8), channel_id=1, source_target_pairs={{0,8},{8,16},{16,24},{24,0},{1,9},{9,17},{17,25},{25,1},{2,10},{10... | collective-permute-start | bytes 296 | tf_op jit(solution)/shard_map/ppermute | solution.py:403
  3.7 2.1 %collective-permute-start = (s32[2,12]{1,0:T(2,128)}, s32[2,12]{1,0:T(2,128)S(1)}, u32[]{:S(2)}, u32[]{:S(2)}) collective-permute-start(s32[2,12]{1,0:T(2,128)} %bitcast.9), channel_id=1, source_target_pairs={{8,0},{16,8},{24,16},{0,24},{9,1},{17,9},{25,17},{1,25},{10,2},{18... | collective-permute-start | bytes 296 | tf_op jit(solution)/shard_map/ppermute | solution.py:404
  5.8 2.9 %shard_map.94 = (s32[2,12]{1,0:T(2,128)S(1)}, bf16[8,16,1024]{2,1,0:T(8,128)(2,1)S(1)}, bf16[8,16,1024]{2,1,0:T(8,128)(2,1)S(1)}) custom-call(s32[1]{0:T(128)} %bitcast.place, s32[2,12]{1,0:T(2,128)} %bitcast.10, bf16[8,2,8,2,1024]{4,3,2,1,0:T(2,128)(2,1)} %far_spectra.1, s32[8,2,8]{2,1,0:T(2,128)} %far_masks.1), custom_call_target="tpu_custom_call" | custom-call | tf_op jit(solution)/shard_map/pallas_call | solution.py:406
  8.7 0.0 collective-permute-done.2.rows
  8.7 0.6 %shard_map.96 = (bf16[4,16,1024]{2,1,0:T(8,128)(2,1)S(1)}, bf16[4,16,1024]{2,1,0:T(8,128)(2,1)S(1)}) custom-call(s32[1]{0:T(128)} %bitcast.place, s32[2,12]{1,0:T(2,128)S(1)} %collective-permute-done.2.rows, bf16[8,16,1024]{2,1,0:T(8,128)(2,1)S(1)} %get-tuple-element.28.refs_0_.own, bf16[8,16,1024]{2,1,0:T(8,128)(2,1)S(1)} %get-tuple-element.29.refs_1_.own), custom_call_target="tpu_custom_call" | custom-call | tf_op jit(solution)/shard_map/pallas_call | solution.py:420
  9.4 2.0 %collective-permute-start.3 = (bf16[4,16,1024]{2,1,0:T(8,128)(2,1)S(1)}, bf16[4,16,1024]{2,1,0:T(8,128)(2,1)S(1)}, u32[]{:S(2)}, u32[]{:S(2)}) collective-permute-start(bf16[4,16,1024]{2,1,0:T(8,128)(2,1)S(1)} %get-tuple-element.31.refs_0_), channel_id=1, source_target_pairs={{8,0},{16,8},{24,16},{0,24},{9,1},{17,9},{25,17},{1,25},{10,2},{18... | collective-permute-start | bytes 393224 | tf_op jit(solution)/shard_map/ppermute | solution.py:429
  11.4 0.0 collective-permute-done.rows
  11.4 0.6 %shard_map.95 = (bf16[4,16,1024]{2,1,0:T(8,128)(2,1)S(1)}, bf16[4,16,1024]{2,1,0:T(8,128)(2,1)S(1)}) custom-call(s32[1]{0:T(128)} %bitcast.place, s32[2,12]{1,0:T(2,128)S(1)} %collective-permute-done.rows, bf16[8,16,1024]{2,1,0:T(8,128)(2,1)S(1)} %get-tuple-element.28.refs_0_.own, bf16[8,16,1024]{2,1,0:T(8,128)(2,1)S(1)} %get-tuple-element.29.refs_1_.own), custom_call_target="tpu_custom_call" | custom-call | tf_op jit(solution)/shard_map/pallas_call | solution.py:420
  12.0 0.1 collective-permute-start.1
  12.2 3.8 %collective-permute-start.5 = (bf16[4,16,1024]{2,1,0:T(8,128)(2,1)S(1)}, bf16[4,16,1024]{2,1,0:T(8,128)(2,1)S(1)}, u32[]{:S(2)}, u32[]{:S(2)}) collective-permute-start(bf16[4,16,1024]{2,1,0:T(8,128)(2,1)S(1)} %get-tuple-element.38), channel_id=1, source_target_pairs={{8,0},{16,8},{24,16},{0,24},{9,1},{17,9},{25,17},{1,25},{10,2},{18... | collective-permute-start | bytes 393224 | tf_op jit(solution)/shard_map/ppermute | solution.py:429
  15.9 0.0 collective-permute-start.4
  15.9 3.4 %shard_map.97 = (bf16[2048,2048]{1,0:T(8,128)(2,1)S(1)}, f32[4,2048]{1,0:T(4,128)S(1)}, bf16[128,256]{1,0:T(8,128)(2,1)S(1)}, bf16[128,640]{1,0:T(8,128)(2,1)S(1)}) custom-call(bf16[4,16,1024]{2,1,0:T(8,128)(2,1)S(1)} %get-tuple-element.31.refs_0_, bf16[2048,2048]{1,0:T(8,128)(2,1)} %constant.38.clone.refs_1_, f32[4,2048]{1,0:T(4,128)} %refs_2_.1, ...), custom_call_target="tpu_custom_call" | custom-call | bytes 8388608 | tf_op jit(solution)/shard_map/pallas_call | solution.py:436
  19.4 0.0 collective-permute-done.3.high
  19.4 1.1 %collective-permute-done.1.low = bf16[4,16,1024]{2,1,0:T(8,128)(2,1)S(1)} collective-permute-done((bf16[4,16,1024]{2,1,0:T(8,128)(2,1)S(1)}, bf16[4,16,1024]{2,1,0:T(8,128)(2,1)S(1)}, u32[]{:S(2)}, u32[]{:S(2)}) %collective-permute-start.1) | collective-permute-done | bytes 131104 | tf_op jit(solution)/shard_map/ppermute | solution.py:428
  20.4 3.5 %shard_map.98 = (f32[12,2048]{1,0:T(8,128)S(1)}, f32[64,2048]{1,0:T(8,128)S(1)}) custom-call(s32[2,12]{1,0:T(2,128)S(1)} %get-tuple-element.27.index, bf16[8,16,1024]{2,1,0:T(8,128)(2,1)S(1)} %get-tuple-element.28.refs_0_.own, bf16[4,16,1024]{2,1,0:T(8,128)(2,1)S(1)} %collective-permute-done.1.low, bf16[4,16,1024]{2,1,0:T(8,128)(2,1)S(1)} %collective-permute-done.3.high, ...), custom_call_target="tpu_custom_call" | custom-call | flops 805306368 | bytes 8388608 | tf_op jit(solution)/shard_map/pallas_call | solution.py:469
  23.9 0.0 collective-permute-done.5.high
  23.9 0.1 collective-permute-done.4.low
  24.0 3.5 %shard_map.99 = (f32[12,2048]{1,0:T(8,128)S(1)}, bf16[4,64,256]{2,1,0:T(8,128)(2,1)S(1)}, f32[4,64,256]{2,1,0:T(8,128)S(1)}) custom-call(s32[2,12]{1,0:T(2,128)S(1)} %get-tuple-element.27.index, bf16[8,16,1024]{2,1,0:T(8,128)(2,1)S(1)} %get-tuple-element.29.refs_1_.own, bf16[4,16,1024]{2,1,0:T(8,128)(2,1)S(1)} %collective-permute-done.4.low, ...), custom_call_target="tpu_custom_call" | custom-call | flops 805306368 | bytes 8388608 | tf_op jit(solution)/shard_map/pallas_call | solution.py:469
  27.4 0.1 collective-permute-start.6
  27.5 1.3 %collective-permute-done.6.got = bf16[4,64,256]{2,1,0:T(8,128)(2,1)S(1)} collective-permute-done((bf16[4,64,256]{2,1,0:T(8,128)(2,1)S(1)}, bf16[4,64,256]{2,1,0:T(8,128)(2,1)S(1)}, u32[]{:S(2)}, u32[]{:S(2)}) %collective-permute-start.6) | collective-permute-done | bytes 131104 | tf_op jit(solution)/shard_map/ppermute | solution.py:484
  28.9 1.6 %collective-permute-start.7 = (bf16[208,256]{1,0:T(8,128)(2,1)S(1)}, bf16[208,256]{1,0:T(8,128)(2,1)S(1)}, u32[]{:S(2)}, u32[]{:S(2)}) collective-permute-start(bf16[208,256]{1,0:T(8,128)(2,1)S(1)} %get-tuple-element.44), channel_id=1, source_target_pairs={{0,2},{1,3},{2,0},{3,1},{4,6},{5,7},{6,4},{7,5},{8,10},{9,11},{10,... | collective-permute-start | bytes 319496 | tf_op jit(solution)/shard_map/ppermute | solution.py:484
  30.5 1.5 %collective-permute-start.8 = (bf16[208,256]{1,0:T(8,128)(2,1)S(1)}, bf16[208,256]{1,0:T(8,128)(2,1)S(1)}, u32[]{:S(2)}, u32[]{:S(2)}) collective-permute-start(bf16[208,256]{1,0:T(8,128)(2,1)S(1)} %get-tuple-element.45), channel_id=1, source_target_pairs={{0,4},{1,5},{2,6},{3,7},{4,0},{5,1},{6,2},{7,3},{8,12},{9,13},{10,... | collective-permute-start | bytes 319496 | tf_op jit(solution)/shard_map/ppermute | solution.py:484
  32.0 0.5 %collective-permute-start.9 = (bf16[208,256]{1,0:T(8,128)(2,1)S(1)}, bf16[208,256]{1,0:T(8,128)(2,1)S(1)}, u32[]{:S(2)}, u32[]{:S(2)}) collective-permute-start(bf16[208,256]{1,0:T(8,128)(2,1)S(1)} %get-tuple-element.46), channel_id=1, source_target_pairs={{0,6},{1,7},{2,4},{3,5},{4,2},{5,3},{6,0},{7,1},{8,14},{9,15},{10,... | collective-permute-start | bytes 319496 | tf_op jit(solution)/shard_map/ppermute | solution.py:484
  32.5 1.5 %collective-permute-done.7.refs_0_ = bf16[208,256]{1,0:T(8,128)(2,1)S(1)} collective-permute-done((bf16[208,256]{1,0:T(8,128)(2,1)S(1)}, bf16[208,256]{1,0:T(8,128)(2,1)S(1)}, u32[]{:S(2)}, u32[]{:S(2)}) %collective-permute-start.7) | collective-permute-done | bytes 106528 | tf_op jit(solution)/shard_map/ppermute | solution.py:484
  34.0 2.5 %collective-permute-done.8.refs_1_ = bf16[208,256]{1,0:T(8,128)(2,1)S(1)} collective-permute-done((bf16[208,256]{1,0:T(8,128)(2,1)S(1)}, bf16[208,256]{1,0:T(8,128)(2,1)S(1)}, u32[]{:S(2)}, u32[]{:S(2)}) %collective-permute-start.8) | collective-permute-done | bytes 106528 | tf_op jit(solution)/shard_map/ppermute | solution.py:484
  36.5 1.1 %collective-permute-done.9.refs_2_ = bf16[208,256]{1,0:T(8,128)(2,1)S(1)} collective-permute-done((bf16[208,256]{1,0:T(8,128)(2,1)S(1)}, bf16[208,256]{1,0:T(8,128)(2,1)S(1)}, u32[]{:S(2)}, u32[]{:S(2)}) %collective-permute-start.9) | collective-permute-done | bytes 106528 | tf_op jit(solution)/shard_map/ppermute | solution.py:484
  37.6 0.2 shard_map.101
  37.8 0.1 collective-permute-start.10
  37.9 0.8 %copy.10 = f32[12,2,2048]{2,1,0:T(2,128)} copy(f32[12,2,2048]{2,0,1:T(8,128)S(1)} %pad_maximum_fusion) | data formatting | bytes 393216
  38.7 0.3 collective-permute-done.10.got
  39.0 0.7 %shard_map.102 = (f32[12,256]{1,0:T(8,128)}, f32[12,4,256]{2,1,0:T(4,128)}) custom-call(f32[64,256]{1,0:T(8,128)S(1)} %get-tuple-element.47.total, f32[12,128]{1,0:T(8,128)S(1)} %get-tuple-element.48.mine, f32[12,128]{1,0:T(8,128)S(1)} %collective-permute-done.10.got), custom_call_target="tpu_custom_call" | custom-call | tf_op jit(solution)/shard_map/pallas_call | solution.py:502
  (2 shorter events, 0.1 us)
Async XLA Ops:
  0.6 8.1 %collective-permute-start.2 = (s32[2,12]{1,0:T(2,128)}, s32[2,12]{1,0:T(2,128)S(1)}, u32[]{:S(2)}, u32[]{:S(2)}) collective-permute-start(s32[2,12]{1,0:T(2,128)} %bitcast.8), channel_id=1, source_target_pairs={{0,8},{8,16},{16,24},{24,0},{1,9},{9,17},{17,25},{25,1},{2,10},{10... | collective-permute-start | bytes 296 | tf_op jit(solution)/shard_map/ppermute | solution.py:403
  3.7 7.7 %collective-permute-start = (s32[2,12]{1,0:T(2,128)}, s32[2,12]{1,0:T(2,128)S(1)}, u32[]{:S(2)}, u32[]{:S(2)}) collective-permute-start(s32[2,12]{1,0:T(2,128)} %bitcast.9), channel_id=1, source_target_pairs={{8,0},{16,8},{24,16},{0,24},{9,1},{17,9},{25,17},{1,25},{10,2},{18... | collective-permute-start | bytes 296 | tf_op jit(solution)/shard_map/ppermute | solution.py:404
  9.4 10.0 %collective-permute-start.3 = (bf16[4,16,1024]{2,1,0:T(8,128)(2,1)S(1)}, bf16[4,16,1024]{2,1,0:T(8,128)(2,1)S(1)}, u32[]{:S(2)}, u32[]{:S(2)}) collective-permute-start(bf16[4,16,1024]{2,1,0:T(8,128)(2,1)S(1)} %get-tuple-element.31.refs_0_), channel_id=1, source_target_pairs={{8,0},{16,8},{24,16},{0,24},{9,1},{17,9},{25,17},{1,25},{10,2},{18... | collective-permute-start | bytes 393224 | tf_op jit(solution)/shard_map/ppermute | solution.py:429
  12.0 8.4 %collective-permute-start.1 = (bf16[4,16,1024]{2,1,0:T(8,128)(2,1)S(1)}, bf16[4,16,1024]{2,1,0:T(8,128)(2,1)S(1)}, u32[]{:S(2)}, u32[]{:S(2)}) collective-permute-start(bf16[4,16,1024]{2,1,0:T(8,128)(2,1)S(1)} %get-tuple-element.30), channel_id=1, source_target_pairs={{0,8},{8,16},{16,24},{24,0},{1,9},{9,17},{17,25},{25,1},{2,10},{10... | collective-permute-start | bytes 393224 | tf_op jit(solution)/shard_map/ppermute | solution.py:428
  12.2 11.7 %collective-permute-start.5 = (bf16[4,16,1024]{2,1,0:T(8,128)(2,1)S(1)}, bf16[4,16,1024]{2,1,0:T(8,128)(2,1)S(1)}, u32[]{:S(2)}, u32[]{:S(2)}) collective-permute-start(bf16[4,16,1024]{2,1,0:T(8,128)(2,1)S(1)} %get-tuple-element.38), channel_id=1, source_target_pairs={{8,0},{16,8},{24,16},{0,24},{9,1},{17,9},{25,17},{1,25},{10,2},{18... | collective-permute-start | bytes 393224 | tf_op jit(solution)/shard_map/ppermute | solution.py:429
  15.9 8.0 %collective-permute-start.4 = (bf16[4,16,1024]{2,1,0:T(8,128)(2,1)S(1)}, bf16[4,16,1024]{2,1,0:T(8,128)(2,1)S(1)}, u32[]{:S(2)}, u32[]{:S(2)}) collective-permute-start(bf16[4,16,1024]{2,1,0:T(8,128)(2,1)S(1)} %get-tuple-element.37), channel_id=1, source_target_pairs={{0,8},{8,16},{16,24},{24,0},{1,9},{9,17},{17,25},{25,1},{2,10},{10... | collective-permute-start | bytes 393224 | tf_op jit(solution)/shard_map/ppermute | solution.py:428
  27.4 1.4 %collective-permute-start.6 = (bf16[4,64,256]{2,1,0:T(8,128)(2,1)S(1)}, bf16[4,64,256]{2,1,0:T(8,128)(2,1)S(1)}, u32[]{:S(2)}, u32[]{:S(2)}) collective-permute-start(bf16[4,64,256]{2,1,0:T(8,128)(2,1)S(1)} %get-tuple-element.42), channel_id=1, source_target_pairs={{0,1},{1,0},{2,3},{3,2},{4,5},{5,4},{6,7},{7,6},{8,9},{9,8},{10,11... | collective-permute-start | bytes 393224 | tf_op jit(solution)/shard_map/ppermute | solution.py:484
  28.9 5.1 %collective-permute-start.7 = (bf16[208,256]{1,0:T(8,128)(2,1)S(1)}, bf16[208,256]{1,0:T(8,128)(2,1)S(1)}, u32[]{:S(2)}, u32[]{:S(2)}) collective-permute-start(bf16[208,256]{1,0:T(8,128)(2,1)S(1)} %get-tuple-element.44), channel_id=1, source_target_pairs={{0,2},{1,3},{2,0},{3,1},{4,6},{5,7},{6,4},{7,5},{8,10},{9,11},{10,... | collective-permute-start | bytes 319496 | tf_op jit(solution)/shard_map/ppermute | solution.py:484
  30.5 6.1 %collective-permute-start.8 = (bf16[208,256]{1,0:T(8,128)(2,1)S(1)}, bf16[208,256]{1,0:T(8,128)(2,1)S(1)}, u32[]{:S(2)}, u32[]{:S(2)}) collective-permute-start(bf16[208,256]{1,0:T(8,128)(2,1)S(1)} %get-tuple-element.45), channel_id=1, source_target_pairs={{0,4},{1,5},{2,6},{3,7},{4,0},{5,1},{6,2},{7,3},{8,12},{9,13},{10,... | collective-permute-start | bytes 319496 | tf_op jit(solution)/shard_map/ppermute | solution.py:484
  32.0 5.6 %collective-permute-start.9 = (bf16[208,256]{1,0:T(8,128)(2,1)S(1)}, bf16[208,256]{1,0:T(8,128)(2,1)S(1)}, u32[]{:S(2)}, u32[]{:S(2)}) collective-permute-start(bf16[208,256]{1,0:T(8,128)(2,1)S(1)} %get-tuple-element.46), channel_id=1, source_target_pairs={{0,6},{1,7},{2,4},{3,5},{4,2},{5,3},{6,0},{7,1},{8,14},{9,15},{10,... | collective-permute-start | bytes 319496 | tf_op jit(solution)/shard_map/ppermute | solution.py:484
  37.8 1.2 %collective-permute-start.10 = (f32[12,128]{1,0:T(8,128)S(1)}, f32[12,128]{1,0:T(8,128)S(1)}, u32[]{:S(2)}, u32[]{:S(2)}) collective-permute-start(f32[12,128]{1,0:T(8,128)S(1)} %get-tuple-element.48.mine), channel_id=1, source_target_pairs={{0,1},{1,0},{2,3},{3,2},{4,5},{5,4},{6,7},{7,6},{8,9},{9,8},{10,11... | collective-permute-start | bytes 18440 | tf_op jit(solution)/shard_map/ppermute | solution.py:484

commit v3 on v2

--- a/solution.py
+++ b/solution.py
@@ -24,11 +24,13 @@
 def kernel_table(freq, lags):
     nfft = 2 * lags
     bins = np.arange(1, freq + 1, dtype=np.int64)[:, None]
-    shifts = np.arange(lags, dtype=np.int64)[None, :] - lags // 2
+    shifts = np.append(np.arange(lags // 2, dtype=np.int64), -(lags // 2))[None, :]
     phase = np.mod(bins * shifts, nfft).astype(np.float64) * (2.0 * math.pi / nfft)
     scale = freq ** (-0.5)
-    table = np.concatenate([np.cos(phase) * scale, -np.sin(phase) * scale], 0)
-    return table.astype(np.float32).astype(jnp.bfloat16)
+    both = np.concatenate([np.cos(phase) * scale, -np.sin(phase) * scale], 0)
+    both = both.astype(np.float32).astype(jnp.bfloat16)
+    ends = both[:, -1].astype(np.float32).reshape(2, freq)
+    return both[:, :-1], ends
 
 
 def pick_matrix(pairs, seg, rank):
@@ -99,34 +101,52 @@
     return result
 
 
-def popcount(bits):
-    bits = bits - jnp.bitwise_and(jnp.right_shift(bits, 1), 0x55555555)
-    bits = jnp.bitwise_and(bits, 0x33333333) + jnp.bitwise_and(jnp.right_shift(bits, 2), 0x33333333)
-    bits = jnp.bitwise_and(bits + jnp.right_shift(bits, 4), 0x0F0F0F0F)
-    bits = bits + jnp.right_shift(bits, 8)
-    return jnp.bitwise_and(bits + jnp.right_shift(bits, 16), 63)
-
-
-def used_stations(rows, low, stations):
-    used = jnp.int32(0)
-    for pair in range(rows.shape[1]):
-        local = rows[1, pair] - low
-        here = jnp.logical_and(local >= 0, local < stations)
-        bit = jnp.left_shift(jnp.int32(1), jnp.clip(local, 0, stations - 1))
-        used = jnp.bitwise_or(used, jnp.where(here, bit, 0))
-    return used
+def used_stations(second, low, stations):
+    number = lax.broadcasted_iota(jnp.int32, (stations, second.shape[1]), 0)
+    return jnp.max(jnp.where(second == low + number, 1.0, 0.0), 1, keepdims=True)
+
+
+def flip(values):
+    rows, width = values.shape
+    back = 127 - lax.broadcasted_iota(jnp.int32, (rows, 128), 1)
+    turned = []
+    for at in range(width - 128, -1, -128):
+        turned.append(jnp.take_along_axis(values[:, at : at + 128], back, axis=1))
+    return jnp.concatenate(turned, 1)
+
+
+def first_lane(values, first, other):
+    lane = lax.broadcasted_iota(jnp.int32, values, 1)
+    return jnp.where(lane == 0, first, other)
+
+
+def unfold(even, odd):
+    shape = even.shape
+    root = math.sqrt(2.0)
+    right = first_lane(shape, even * root, even + odd)
+    left = first_lane(shape, odd * root, even - odd)
+    return flip(pltpu.roll(left, shape[1] - 1, 1)), right
 
 
 def stage_kernel(*refs):
-    count = (len(refs) - 2) // 2
-    sources, targets, sems = refs[1 : 1 + count], refs[1 + count : -1], refs[-1]
+    count = (len(refs) - 3) // 2
+    sources, targets, natural, sems = refs[1 : 1 + count], refs[1 + count : -2], refs[-2], refs[-1]
     copies = [
         pltpu.make_async_copy(source, target, sems.at[number])
-        for number, (source, target) in enumerate(zip(sources, targets))
+        for number, (source, target) in enumerate(zip(sources, (natural, *targets[1:])))
     ]
     for copy in copies:
         copy.start()
-    for copy in copies:
+    copies[0].wait()
+    values = natural[...]
+    half = values.shape[1] // 2
+    right = values[:, half:]
+    left = pltpu.roll(flip(values[:, :half]), 1, 1)
+    shape = right.shape
+    root = math.sqrt(0.5)
+    targets[0][:, :half] = first_lane(shape, right * root, (right + left) * 0.5)
+    targets[0][:, half:] = first_lane(shape, left * root, (right - left) * 0.5)
+    for copy in copies[1:]:
         copy.wait()
 
 
@@ -144,24 +164,23 @@
     band = lax.broadcasted_iota(jnp.int32, (count, freq), 0)
     of_bin = lax.broadcasted_iota(jnp.int32, (count, freq), 1) // BAND
     bands = jnp.where(band == of_bin, 1.0, 0.0).astype(BF16)
-    for copy in copies:
-        copy.wait()
     before = lax.rem(place[0] + groups - 1, groups) * stations
     after = lax.rem(place[0] + 1, groups) * stations
     own = place[0] * stations
-    used_before = used_stations(rows, before, stations)
-    used_after = used_stations(rows, after, stations)
-    for pair in range(rows.shape[1]):
-        index[0, pair] = rows[0, pair] - own
-        second = rows[1, pair]
-        in_before = jnp.logical_and(second >= before, second < before + stations)
-        in_own = jnp.logical_and(second >= own, second < own + stations)
-        local = second - jnp.where(in_before, before, jnp.where(in_own, own, after))
-        below = jnp.left_shift(jnp.int32(1), local) - 1
-        slot = popcount(jnp.bitwise_and(jnp.where(in_before, used_before, used_after), below))
-        index[1, pair] = jnp.where(
-            in_before, slot, jnp.where(in_own, NEAR + local, NEAR + stations + slot)
-        )
+    for copy in copies:
+        copy.wait()
+    second = rows[1:2]
+    in_before = jnp.logical_and(second >= before, second < before + stations)
+    in_own = jnp.logical_and(second >= own, second < own + stations)
+    local = second - jnp.where(in_before, before, jnp.where(in_own, own, after))
+    below = lax.broadcasted_iota(jnp.int32, (stations, second.shape[1]), 0) < local
+    slots = [
+        jnp.sum(jnp.where(below, used_stations(second, low, stations), 0.0), 0, keepdims=True)
+        for low in (before, after)
+    ]
+    spot = jnp.where(in_own, NEAR + local, NEAR + stations + slots[1].astype(jnp.int32))
+    index[0:1] = rows[0:1] - own
+    index[1:2] = jnp.where(in_before, slots[0].astype(jnp.int32), spot)
     values, squares, open_rows = [], [], []
     eye = lax.broadcasted_iota(jnp.int32, (seg, seg), 0) == lax.broadcasted_iota(jnp.int32, (seg, seg), 1)
     for station in range(stations):
@@ -189,7 +208,9 @@
 
 def select_kernel(stations, place, rows, *refs):
     windows = len(refs) // 2
-    needed = used_stations(rows, place[0] * stations, stations)
+    used = used_stations(rows[1:2], place[0] * stations, stations)
+    weight = jnp.left_shift(1, lax.broadcasted_iota(jnp.int32, (stations, 1), 0)).astype(F32)
+    needed = jnp.sum(used * weight).astype(jnp.int32)
     slot = jnp.int32(0)
     for station in range(stations):
         wanted = jnp.bitwise_and(jnp.right_shift(needed, station), 1)
@@ -203,7 +224,7 @@
         slot = slot + wanted
 
 
-def window_kernel(sizes, index, own, low, high, table, start, pick, spread, *refs):
+def window_kernel(sizes, index, own, low, high, start, table, ends, pick, spread, *refs):
     pairs, seg, rank, lags, freq, total_windows, slices, first_window = sizes
     rows = pairs * seg
     if first_window:
@@ -211,31 +232,45 @@
     else:
         (core, partial, win_out, send_out, keep_out, near, cross, vectors, high_part, low_part, pieces) = refs
     stations = own.shape[0]
+    half = lags // 2
+    picked = index[...]
     near[0:NEAR] = low[...]
     near[NEAR : NEAR + stations] = own[...]
     near[NEAR + stations :] = high[...]
+    edges = []
     for pair in range(0, pairs, 2):
         real, imag = [], []
         for one in (pair, pair + 1):
-            a = near[NEAR + index[0, one]].astype(F32)
-            b = near[index[1, one]].astype(F32)
+            a = own[picked[0, one]].astype(F32)
+            b = near[picked[1, one]].astype(F32)
             a_re, a_im, b_re, b_im = a[:seg], a[seg:], b[:seg], b[seg:]
             real.append(a_re * b_re + a_im * b_im)
             imag.append(a_im * b_re - a_re * b_im)
         block = pl.ds(pair * seg, 2 * seg)
-        cross[block, 0:freq] = jnp.concatenate(real, 0).astype(BF16)
-        cross[block, freq:] = jnp.concatenate(imag, 0).astype(BF16)
+        real = jnp.concatenate(real, 0).astype(BF16)
+        imag = jnp.concatenate(imag, 0).astype(BF16)
+        cross[block, 0:freq] = real
+        cross[block, freq:] = imag
+        last = real.astype(F32) * ends[0:1] + imag.astype(F32) * ends[1:2]
+        edges.append(jnp.sum(last, 1, keepdims=True))
     vectors[rows : rows + rank] = start[...]
     vectors[rows + rank :] = jnp.zeros((HEAD - rows - rank, lags), F32)
     step = 512
-    for at in range(0, lags, step):
-        vectors[0:rows, at : at + step] = dot(cross[...], table[:, at : at + step])
+    for at in range(0, half, step):
+        vectors[0:rows, at : at + step] = dot(cross[:, 0:freq], table[0:freq, at : at + step])
+        vectors[0:rows, half + at : half + at + step] = dot(cross[:, freq:], table[freq:, at : at + step])
+    shape = (rows, 128)
+    root = math.sqrt(0.5)
+    column = vectors[0:rows, 0:128]
+    vectors[0:rows, 0:128] = first_lane(shape, column * root, column)
+    edge = jnp.broadcast_to(jnp.concatenate(edges, 0) * root, shape)
+    vectors[0:rows, half : half + 128] = first_lane(shape, edge, vectors[0:rows, half : half + 128])
     every = vectors[...]
     high_part[...] = every.astype(BF16)
     low_part[...] = (every - high_part[...].astype(F32)).astype(BF16)
     gram = dot_rows(high_part[...], high_part[...])
     side = dot_rows(low_part[...], high_part[...])
-    gram = gram + side + side.T
+    gram = 2.0 * (gram + side + side.T)
     lane = lax.broadcasted_iota(jnp.int32, (seg, HEAD), 1)
     sub = lax.broadcasted_iota(jnp.int32, (seg, HEAD), 0)
     blocks = jnp.zeros((seg, HEAD), F32)
@@ -297,17 +332,24 @@
     scale = 1.0 / math.sqrt(total_windows)
     width = lags // slices
     top = rank * pairs
-    for at in range(0, lags, step):
+
+    def combined(at):
         part = dot(both, high_part[:, at : at + step])
-        result = part[0:height] + part[height:] + dot(w_high, low_part[:, at : at + step])
-        win_out[:, at : at + step] = result[top:filled]
-        result = jnp.concatenate([result[0:top], result[top:] * scale], 0)
-        if first_window:
-            merged_out[:, at : at + step] = result
-        else:
-            result = result + partial[:, at : at + step]
-            for piece in range(at // width, (at + step) // width):
-                pieces[piece] = result[:, piece * width - at : (piece + 1) * width - at]
+        return part[0:height] + part[height:] + dot(w_high, low_part[:, at : at + step])
+
+    result = [jnp.concatenate([combined(side + at) for at in range(0, half, step)], 1) for side in (0, half)]
+    left, right = unfold(*[one[top:] for one in result])
+    win_out[:, 0:half] = left[0:pairs]
+    win_out[:, half:] = right[0:pairs]
+    result = [jnp.concatenate([one[0:top], one[top:] * scale], 0) for one in result]
+    if first_window:
+        merged_out[:, 0:half] = result[0]
+        merged_out[:, half:] = result[1]
+    else:
+        left, right = unfold(result[0] + partial[:, 0:half], result[1] + partial[:, half:])
+        for piece in range(slices // 2):
+            pieces[piece] = left[:, piece * width : (piece + 1) * width]
+            pieces[slices // 2 + piece] = right[:, piece * width : (piece + 1) * width]
     if not first_window:
         for piece in range(slices // 2):
             send_out[piece] = pieces[2 * piece + 1 - core[0]].astype(BF16)
@@ -407,11 +449,11 @@
         functools.partial(whiten_kernel, groups),
         [struct(rows.shape, jnp.int32)] + [struct((stations, parts * seg, freq), BF16)] * windows,
         [SMEM, HBM, HBM, HBM],
-        [SMEM] + [VMEM] * windows,
+        [VMEM] * (1 + windows),
         [
             pltpu.VMEM(spectra.shape, BF16),
             pltpu.VMEM(masks.shape, jnp.int32),
-            pltpu.SMEM(rows.shape, jnp.int32),
+            pltpu.VMEM(rows.shape, jnp.int32),
             pltpu.SemaphoreType.DMA((3,)),
         ],
     )(place, far(rows), far(spectra), far(masks))
@@ -420,26 +462,28 @@
         return call(
             functools.partial(select_kernel, stations),
             [block] * windows,
-            [SMEM] * 2 + [VMEM] * windows,
+            [SMEM] + [VMEM] * (1 + windows),
             [VMEM] * windows,
         )(place, wanted, *whitened)
 
     to_next, to_last = select(after), select(before)
     lows = [lax.ppermute(one, "pairs", forward) for one in to_next]
     highs = [lax.ppermute(one, "pairs", backward) for one in to_last]
+    table, ends = kernel_table(freq, lags)
     fixed = [
-        jnp.asarray(kernel_table(freq, lags)),
         start_basis,
+        jnp.asarray(table),
+        jnp.asarray(ends),
         jnp.asarray(pick_matrix(pairs, seg, rank)),
         jnp.asarray(spread_matrix(pairs, seg, rank)),
     ]
-    table, start, pick, spread = call(
+    staged = call(
         stage_kernel,
         [struct(one.shape, one.dtype) for one in fixed],
         [VMEM] + [HBM] * len(fixed),
         [VMEM] * len(fixed),
-        [pltpu.SemaphoreType.DMA((len(fixed),))],
-        moved=parts * freq * lags * 2,
+        [pltpu.VMEM(start_basis.shape, F32), pltpu.SemaphoreType.DMA((len(fixed),))],
+        moved=parts * freq * lags,
     )(to_last[0], *[far(one) for one in fixed])
     core = jnp.mod(hour, 2).reshape(1).astype(jnp.int32)
     chip = (hour // 2).reshape(1).astype(jnp.int32)
@@ -456,8 +500,8 @@
             pltpu.VMEM((HEAD, lags), BF16),
             pltpu.VMEM((HEAD, lags), BF16),
         ]
-        args = [index, whitened[w], lows[w], highs[w], table, start, pick, spread]
-        specs = [SMEM] + [VMEM] * 7
+        args = [index, whitened[w], lows[w], highs[w], *staged]
+        specs = [VMEM] * len(args)
         outs = [struct((pairs, lags))]
         if w == 0:
             outs.append(struct((height, lags)))
@@ -472,8 +516,8 @@
             specs,
             [VMEM] * len(outs),
             scratch,
-            flops=2 * pairs * seg * parts * freq * lags,
-            moved=parts * freq * lags * 2,
+            flops=pairs * seg * parts * freq * lags,
+            moved=parts * freq * lags,
         )(*args)
         stacks.append(result[0])
         if w == 0:

time: 39.9 us -> 37.6 us (0.942)
  Pallas kernels: 15.5 us -> 11.2 us
  waiting for transfers between devices: 7.87 us -> 9.9 us
    ppermute x2, waiting for transfers between devices: 1.12 us -> 3.15 us  [on_device(): lows = [lax.ppermute(one, 'pairs', forward) for one in to_next]]
    pallas_call x2, Pallas kernels: 6.94 us -> 5.23 us  [on_device(): call(functools.partial(window_kernel, sizes), outs, specs, [VMEM] * len(o...]
    pallas_call x1, Pallas kernels: 3.42 us -> 2.28 us  [on_device(): call(stage_kernel, [struct(one.shape, one.dtype) for one in fixed], [VMEM...]
    pallas_call x2, Pallas kernels: 1.29 us -> 0.51 us  [select(): call(functools.partial(select_kernel, stations), [block] * windows, [SMEM...]
    pallas_call x1, Pallas kernels: 2.91 us -> 2.19 us  [on_device(): call(functools.partial(whiten_kernel, groups), [struct(rows.shape, jnp.in...]
  transfers between devices with their start and end apart: 11 -> 11, of which waited for: 7 -> 7; matrix products, arithmetic and copies ran while one was open for 2% -> 2% of each run, Pallas kernels for 28% -> 20%
where the time goes in v3:
time: 37.6 us; the launch traced here: 37.4 us
  starting transfers between devices  14.7 us (39%)
  Pallas kernels  11.2 us (30%)
  waiting for transfers between devices  9.9 us (26%)
  local copies, waits for them, and re-layouts  0.83 us (2%)
  between operations  0.75 us (2%)
    ppermute x5, waiting for transfers between devices, on_device(): lax.ppermute(value, 'hours', [(k, k ^ step) for k in range(slices)])  6.74 us
    ppermute x2, starting transfers between devices, on_device(): highs = [lax.ppermute(one, 'pairs', backward) for one in to_last]  5.77 us
    pallas_call x2, Pallas kernels, on_device(): call(functools.partial(window_kernel, sizes), outs, specs, [VMEM] * len(o...  5.23 us
    ppermute x5, starting transfers between devices, on_device(): lax.ppermute(value, 'hours', [(k, k ^ step) for k in range(slices)])  3.69 us
    ppermute x2, waiting for transfers between devices, on_device(): lows = [lax.ppermute(one, 'pairs', forward) for one in to_next]  3.15 us
    ppermute x1, starting transfers between devices, on_device(): before = lax.ppermute(rows, 'pairs', forward)  3.08 us
    pallas_call x1, Pallas kernels, on_device(): call(stage_kernel, [struct(one.shape, one.dtype) for one in fixed], [VMEM...  2.28 us
    pallas_call x1, Pallas kernels, on_device(): call(functools.partial(whiten_kernel, groups), [struct(rows.shape, jnp.in...  2.19 us
  transfers between devices with their start and end apart: 11, of which 7 were waited for; matrix products, arithmetic and copies ran while one was open for 2% of the time, Pallas kernels for 20%

profile of v3, /device:TPU:0, one launch (start us, length us, event | category | flops | bytes accessed | tf_op | source)
XLA Modules:
  0.0 37.4 jit_solution(16079996554312923485)
XLA Ops:
  0.6 3.1 %collective-permute-start.2 = (s32[2,12]{1,0:T(2,128)}, s32[2,12]{1,0:T(2,128)S(1)}, u32[]{:S(2)}, u32[]{:S(2)}) collective-permute-start(s32[2,12]{1,0:T(2,128)} %bitcast.8), channel_id=1, source_target_pairs={{0,8},{8,16},{16,24},{24,0},{1,9},{9,17},{17,25},{25,1},{2,10},{10... | collective-permute-start | bytes 296 | tf_op jit(solution)/shard_map/ppermute | solution.py:445
  3.7 2.1 %collective-permute-start = (s32[2,12]{1,0:T(2,128)}, s32[2,12]{1,0:T(2,128)S(1)}, u32[]{:S(2)}, u32[]{:S(2)}) collective-permute-start(s32[2,12]{1,0:T(2,128)} %bitcast.9), channel_id=1, source_target_pairs={{8,0},{16,8},{24,16},{0,24},{9,1},{17,9},{25,17},{1,25},{10,2},{18... | collective-permute-start | bytes 296 | tf_op jit(solution)/shard_map/ppermute | solution.py:446
  5.8 2.2 %shard_map.103 = (s32[2,12]{1,0:T(2,128)S(1)}, bf16[8,16,1024]{2,1,0:T(8,128)(2,1)S(1)}, bf16[8,16,1024]{2,1,0:T(8,128)(2,1)S(1)}) custom-call(s32[1]{0:T(128)} %bitcast.place, s32[2,12]{1,0:T(2,128)} %bitcast.10, bf16[8,2,8,2,1024]{4,3,2,1,0:T(2,128)(2,1)} %far_spectra.1, s32[8,2,8]{2,1,0:T(2,128)} %far_masks.1), custom_call_target="tpu_custom_call" | custom-call | tf_op jit(solution)/shard_map/pallas_call | solution.py:448
  8.0 0.0 collective-permute-done.2.rows
  8.0 0.3 shard_map.105
  8.3 2.0 %collective-permute-start.3 = (bf16[4,16,1024]{2,1,0:T(8,128)(2,1)S(1)}, bf16[4,16,1024]{2,1,0:T(8,128)(2,1)S(1)}, u32[]{:S(2)}, u32[]{:S(2)}) collective-permute-start(bf16[4,16,1024]{2,1,0:T(8,128)(2,1)S(1)} %get-tuple-element.32.refs_0_), channel_id=1, source_target_pairs={{8,0},{16,8},{24,16},{0,24},{9,1},{17,9},{25,17},{1,25},{10,2},{18... | collective-permute-start | bytes 393224 | tf_op jit(solution)/shard_map/ppermute | solution.py:471
  10.3 0.0 collective-permute-done.rows
  10.3 0.3 shard_map.104
  10.5 0.1 collective-permute-start.1
  10.7 3.8 %collective-permute-start.5 = (bf16[4,16,1024]{2,1,0:T(8,128)(2,1)S(1)}, bf16[4,16,1024]{2,1,0:T(8,128)(2,1)S(1)}, u32[]{:S(2)}, u32[]{:S(2)}) collective-permute-start(bf16[4,16,1024]{2,1,0:T(8,128)(2,1)S(1)} %get-tuple-element.40), channel_id=1, source_target_pairs={{8,0},{16,8},{24,16},{0,24},{9,1},{17,9},{25,17},{1,25},{10,2},{18... | collective-permute-start | bytes 393224 | tf_op jit(solution)/shard_map/ppermute | solution.py:471
  14.4 0.0 collective-permute-start.4
  14.4 2.3 %shard_map.106 = (f32[4,2048]{1,0:T(4,128)S(1)}, bf16[2048,1024]{1,0:T(8,128)(2,1)S(1)}, f32[2,1024]{1,0:T(2,128)S(1)}, bf16[128,256]{1,0:T(8,128)(2,1)S(1)}, bf16[128,640]{1,0:T(8,128)(2,1)S(1)}) custom-call(bf16[4,16,1024]{2,1,0:T(8,128)(2,1)S(1)} %get-tuple-element.32.refs_0_, f32[4,2048]{1,0:T(4,128)} %refs_1_.1, ...), custom_call_target="tpu_custom_call" | custom-call | bytes 4194304 | tf_op jit(solution)/shard_map/pallas_call | solution.py:480
  16.7 0.0 collective-permute-done.3.high
  16.7 2.2 %collective-permute-done.1.low = bf16[4,16,1024]{2,1,0:T(8,128)(2,1)S(1)} collective-permute-done((bf16[4,16,1024]{2,1,0:T(8,128)(2,1)S(1)}, bf16[4,16,1024]{2,1,0:T(8,128)(2,1)S(1)}, u32[]{:S(2)}, u32[]{:S(2)}) %collective-permute-start.1) | collective-permute-done | bytes 131104 | tf_op jit(solution)/shard_map/ppermute | solution.py:470
  18.9 2.6 %shard_map.107 = (f32[12,2048]{1,0:T(8,128)S(1)}, f32[64,2048]{1,0:T(8,128)S(1)}) custom-call(s32[2,12]{1,0:T(2,128)S(1)} %get-tuple-element.28.index, bf16[8,16,1024]{2,1,0:T(8,128)(2,1)S(1)} %get-tuple-element.29.refs_0_.own, bf16[4,16,1024]{2,1,0:T(8,128)(2,1)S(1)} %collective-permute-done.1.low, bf16[4,16,1024]{2,1,0:T(8,128)(2,1)S(1)} %collective-permute-done.3.high, ...), custom_call_target="tpu_custom_call" | custom-call | flops 402653184 | bytes 4194304 | tf_op jit(solution)/shard_map/pallas_call | solution.py:513
  21.5 0.0 collective-permute-done.5.high
  21.5 0.9 %collective-permute-done.4.low = bf16[4,16,1024]{2,1,0:T(8,128)(2,1)S(1)} collective-permute-done((bf16[4,16,1024]{2,1,0:T(8,128)(2,1)S(1)}, bf16[4,16,1024]{2,1,0:T(8,128)(2,1)S(1)}, u32[]{:S(2)}, u32[]{:S(2)}) %collective-permute-start.4) | collective-permute-done | bytes 131104 | tf_op jit(solution)/shard_map/ppermute | solution.py:470
  22.5 2.7 %shard_map.108 = (f32[12,2048]{1,0:T(8,128)S(1)}, bf16[4,64,256]{2,1,0:T(8,128)(2,1)S(1)}, f32[4,64,256]{2,1,0:T(8,128)S(1)}) custom-call(s32[2,12]{1,0:T(2,128)S(1)} %get-tuple-element.28.index, bf16[8,16,1024]{2,1,0:T(8,128)(2,1)S(1)} %get-tuple-element.30.refs_1_.own, bf16[4,16,1024]{2,1,0:T(8,128)(2,1)S(1)} %collective-permute-done.4.low, ...), custom_call_target="tpu_custom_call" | custom-call | flops 402653184 | bytes 4194304 | tf_op jit(solution)/shard_map/pallas_call | solution.py:513
  25.1 0.1 collective-permute-start.6
  25.2 1.3 %collective-permute-done.6.got = bf16[4,64,256]{2,1,0:T(8,128)(2,1)S(1)} collective-permute-done((bf16[4,64,256]{2,1,0:T(8,128)(2,1)S(1)}, bf16[4,64,256]{2,1,0:T(8,128)(2,1)S(1)}, u32[]{:S(2)}, u32[]{:S(2)}) %collective-permute-start.6) | collective-permute-done | bytes 131104 | tf_op jit(solution)/shard_map/ppermute | solution.py:528
  26.6 1.6 %collective-permute-start.7 = (bf16[208,256]{1,0:T(8,128)(2,1)S(1)}, bf16[208,256]{1,0:T(8,128)(2,1)S(1)}, u32[]{:S(2)}, u32[]{:S(2)}) collective-permute-start(bf16[208,256]{1,0:T(8,128)(2,1)S(1)} %get-tuple-element.46), channel_id=1, source_target_pairs={{0,2},{1,3},{2,0},{3,1},{4,6},{5,7},{6,4},{7,5},{8,10},{9,11},{10,... | collective-permute-start | bytes 319496 | tf_op jit(solution)/shard_map/ppermute | solution.py:528
  28.1 1.5 %collective-permute-start.8 = (bf16[208,256]{1,0:T(8,128)(2,1)S(1)}, bf16[208,256]{1,0:T(8,128)(2,1)S(1)}, u32[]{:S(2)}, u32[]{:S(2)}) collective-permute-start(bf16[208,256]{1,0:T(8,128)(2,1)S(1)} %get-tuple-element.47), channel_id=1, source_target_pairs={{0,4},{1,5},{2,6},{3,7},{4,0},{5,1},{6,2},{7,3},{8,12},{9,13},{10,... | collective-permute-start | bytes 319496 | tf_op jit(solution)/shard_map/ppermute | solution.py:528
  29.7 0.5 %collective-permute-start.9 = (bf16[208,256]{1,0:T(8,128)(2,1)S(1)}, bf16[208,256]{1,0:T(8,128)(2,1)S(1)}, u32[]{:S(2)}, u32[]{:S(2)}) collective-permute-start(bf16[208,256]{1,0:T(8,128)(2,1)S(1)} %get-tuple-element.48), channel_id=1, source_target_pairs={{0,6},{1,7},{2,4},{3,5},{4,2},{5,3},{6,0},{7,1},{8,14},{9,15},{10,... | collective-permute-start | bytes 319496 | tf_op jit(solution)/shard_map/ppermute | solution.py:528
  30.1 1.5 %collective-permute-done.7.refs_0_ = bf16[208,256]{1,0:T(8,128)(2,1)S(1)} collective-permute-done((bf16[208,256]{1,0:T(8,128)(2,1)S(1)}, bf16[208,256]{1,0:T(8,128)(2,1)S(1)}, u32[]{:S(2)}, u32[]{:S(2)}) %collective-permute-start.7) | collective-permute-done | bytes 106528 | tf_op jit(solution)/shard_map/ppermute | solution.py:528
  31.7 2.5 %collective-permute-done.8.refs_1_ = bf16[208,256]{1,0:T(8,128)(2,1)S(1)} collective-permute-done((bf16[208,256]{1,0:T(8,128)(2,1)S(1)}, bf16[208,256]{1,0:T(8,128)(2,1)S(1)}, u32[]{:S(2)}, u32[]{:S(2)}) %collective-permute-start.8) | collective-permute-done | bytes 106528 | tf_op jit(solution)/shard_map/ppermute | solution.py:528
  34.2 1.1 %collective-permute-done.9.refs_2_ = bf16[208,256]{1,0:T(8,128)(2,1)S(1)} collective-permute-done((bf16[208,256]{1,0:T(8,128)(2,1)S(1)}, bf16[208,256]{1,0:T(8,128)(2,1)S(1)}, u32[]{:S(2)}, u32[]{:S(2)}) %collective-permute-start.9) | collective-permute-done | bytes 106528 | tf_op jit(solution)/shard_map/ppermute | solution.py:528
  35.3 0.2 shard_map.110
  35.4 0.1 collective-permute-start.10
  35.5 0.8 %copy.11 = f32[12,2,2048]{2,1,0:T(2,128)} copy(f32[12,2,2048]{2,0,1:T(8,128)S(1)} %pad_maximum_fusion) | data formatting | bytes 393216
  36.4 0.3 collective-permute-done.10.got
  36.7 0.7 %shard_map.111 = (f32[12,256]{1,0:T(8,128)}, f32[12,4,256]{2,1,0:T(4,128)}) custom-call(f32[64,256]{1,0:T(8,128)S(1)} %get-tuple-element.49.total, f32[12,128]{1,0:T(8,128)S(1)} %get-tuple-element.50.mine, f32[12,128]{1,0:T(8,128)S(1)} %collective-permute-done.10.got), custom_call_target="tpu_custom_call" | custom-call | tf_op jit(solution)/shard_map/pallas_call | solution.py:546
  (2 shorter events, 0.1 us)
Async XLA Ops:
  0.6 7.4 %collective-permute-start.2 = (s32[2,12]{1,0:T(2,128)}, s32[2,12]{1,0:T(2,128)S(1)}, u32[]{:S(2)}, u32[]{:S(2)}) collective-permute-start(s32[2,12]{1,0:T(2,128)} %bitcast.8), channel_id=1, source_target_pairs={{0,8},{8,16},{16,24},{24,0},{1,9},{9,17},{17,25},{25,1},{2,10},{10... | collective-permute-start | bytes 296 | tf_op jit(solution)/shard_map/ppermute | solution.py:445
  3.7 6.6 %collective-permute-start = (s32[2,12]{1,0:T(2,128)}, s32[2,12]{1,0:T(2,128)S(1)}, u32[]{:S(2)}, u32[]{:S(2)}) collective-permute-start(s32[2,12]{1,0:T(2,128)} %bitcast.9), channel_id=1, source_target_pairs={{8,0},{16,8},{24,16},{0,24},{9,1},{17,9},{25,17},{1,25},{10,2},{18... | collective-permute-start | bytes 296 | tf_op jit(solution)/shard_map/ppermute | solution.py:446
  8.3 8.4 %collective-permute-start.3 = (bf16[4,16,1024]{2,1,0:T(8,128)(2,1)S(1)}, bf16[4,16,1024]{2,1,0:T(8,128)(2,1)S(1)}, u32[]{:S(2)}, u32[]{:S(2)}) collective-permute-start(bf16[4,16,1024]{2,1,0:T(8,128)(2,1)S(1)} %get-tuple-element.32.refs_0_), channel_id=1, source_target_pairs={{8,0},{16,8},{24,16},{0,24},{9,1},{17,9},{25,17},{1,25},{10,2},{18... | collective-permute-start | bytes 393224 | tf_op jit(solution)/shard_map/ppermute | solution.py:471
  10.5 8.4 %collective-permute-start.1 = (bf16[4,16,1024]{2,1,0:T(8,128)(2,1)S(1)}, bf16[4,16,1024]{2,1,0:T(8,128)(2,1)S(1)}, u32[]{:S(2)}, u32[]{:S(2)}) collective-permute-start(bf16[4,16,1024]{2,1,0:T(8,128)(2,1)S(1)} %get-tuple-element.31), channel_id=1, source_target_pairs={{0,8},{8,16},{16,24},{24,0},{1,9},{9,17},{17,25},{25,1},{2,10},{10... | collective-permute-start | bytes 393224 | tf_op jit(solution)/shard_map/ppermute | solution.py:470
  10.7 10.9 %collective-permute-start.5 = (bf16[4,16,1024]{2,1,0:T(8,128)(2,1)S(1)}, bf16[4,16,1024]{2,1,0:T(8,128)(2,1)S(1)}, u32[]{:S(2)}, u32[]{:S(2)}) collective-permute-start(bf16[4,16,1024]{2,1,0:T(8,128)(2,1)S(1)} %get-tuple-element.40), channel_id=1, source_target_pairs={{8,0},{16,8},{24,16},{0,24},{9,1},{17,9},{25,17},{1,25},{10,2},{18... | collective-permute-start | bytes 393224 | tf_op jit(solution)/shard_map/ppermute | solution.py:471
  14.4 8.0 %collective-permute-start.4 = (bf16[4,16,1024]{2,1,0:T(8,128)(2,1)S(1)}, bf16[4,16,1024]{2,1,0:T(8,128)(2,1)S(1)}, u32[]{:S(2)}, u32[]{:S(2)}) collective-permute-start(bf16[4,16,1024]{2,1,0:T(8,128)(2,1)S(1)} %get-tuple-element.39), channel_id=1, source_target_pairs={{0,8},{8,16},{16,24},{24,0},{1,9},{9,17},{17,25},{25,1},{2,10},{10... | collective-permute-start | bytes 393224 | tf_op jit(solution)/shard_map/ppermute | solution.py:470
  25.1 1.4 %collective-permute-start.6 = (bf16[4,64,256]{2,1,0:T(8,128)(2,1)S(1)}, bf16[4,64,256]{2,1,0:T(8,128)(2,1)S(1)}, u32[]{:S(2)}, u32[]{:S(2)}) collective-permute-start(bf16[4,64,256]{2,1,0:T(8,128)(2,1)S(1)} %get-tuple-element.44), channel_id=1, source_target_pairs={{0,1},{1,0},{2,3},{3,2},{4,5},{5,4},{6,7},{7,6},{8,9},{9,8},{10,11... | collective-permute-start | bytes 393224 | tf_op jit(solution)/shard_map/ppermute | solution.py:528
  26.6 5.1 %collective-permute-start.7 = (bf16[208,256]{1,0:T(8,128)(2,1)S(1)}, bf16[208,256]{1,0:T(8,128)(2,1)S(1)}, u32[]{:S(2)}, u32[]{:S(2)}) collective-permute-start(bf16[208,256]{1,0:T(8,128)(2,1)S(1)} %get-tuple-element.46), channel_id=1, source_target_pairs={{0,2},{1,3},{2,0},{3,1},{4,6},{5,7},{6,4},{7,5},{8,10},{9,11},{10,... | collective-permute-start | bytes 319496 | tf_op jit(solution)/shard_map/ppermute | solution.py:528
  28.1 6.1 %collective-permute-start.8 = (bf16[208,256]{1,0:T(8,128)(2,1)S(1)}, bf16[208,256]{1,0:T(8,128)(2,1)S(1)}, u32[]{:S(2)}, u32[]{:S(2)}) collective-permute-start(bf16[208,256]{1,0:T(8,128)(2,1)S(1)} %get-tuple-element.47), channel_id=1, source_target_pairs={{0,4},{1,5},{2,6},{3,7},{4,0},{5,1},{6,2},{7,3},{8,12},{9,13},{10,... | collective-permute-start | bytes 319496 | tf_op jit(solution)/shard_map/ppermute | solution.py:528
  29.7 5.6 %collective-permute-start.9 = (bf16[208,256]{1,0:T(8,128)(2,1)S(1)}, bf16[208,256]{1,0:T(8,128)(2,1)S(1)}, u32[]{:S(2)}, u32[]{:S(2)}) collective-permute-start(bf16[208,256]{1,0:T(8,128)(2,1)S(1)} %get-tuple-element.48), channel_id=1, source_target_pairs={{0,6},{1,7},{2,4},{3,5},{4,2},{5,3},{6,0},{7,1},{8,14},{9,15},{10,... | collective-permute-start | bytes 319496 | tf_op jit(solution)/shard_map/ppermute | solution.py:528
  35.4 1.2 %collective-permute-start.10 = (f32[12,128]{1,0:T(8,128)S(1)}, f32[12,128]{1,0:T(8,128)S(1)}, u32[]{:S(2)}, u32[]{:S(2)}) collective-permute-start(f32[12,128]{1,0:T(8,128)S(1)} %get-tuple-element.50.mine), channel_id=1, source_target_pairs={{0,1},{1,0},{2,3},{3,2},{4,5},{5,4},{6,7},{7,6},{8,9},{9,8},{10,11... | collective-permute-start | bytes 18440 | tf_op jit(solution)/shard_map/ppermute | solution.py:528

commit v4 on v3

--- a/solution.py
+++ b/solution.py
@@ -128,47 +128,22 @@
     return flip(pltpu.roll(left, shape[1] - 1, 1)), right
 
 
-def stage_kernel(*refs):
-    count = (len(refs) - 3) // 2
-    sources, targets, natural, sems = refs[1 : 1 + count], refs[1 + count : -2], refs[-2], refs[-1]
+def stage_kernel(groups, stations, place, early, far_rows, *refs):
+    *refs, index, natural, rows, sems = refs
+    count = len(refs) // 2
+    sources, targets = refs[:count], refs[count:]
     copies = [
         pltpu.make_async_copy(source, target, sems.at[number])
         for number, (source, target) in enumerate(zip(sources, (natural, *targets[1:])))
     ]
     for copy in copies:
         copy.start()
-    copies[0].wait()
-    values = natural[...]
-    half = values.shape[1] // 2
-    right = values[:, half:]
-    left = pltpu.roll(flip(values[:, :half]), 1, 1)
-    shape = right.shape
-    root = math.sqrt(0.5)
-    targets[0][:, :half] = first_lane(shape, right * root, (right + left) * 0.5)
-    targets[0][:, half:] = first_lane(shape, left * root, (right - left) * 0.5)
-    for copy in copies[1:]:
-        copy.wait()
-
-
-def whiten_kernel(groups, place, far_rows, far_spectra, far_masks, index, *refs):
-    whitened, (spectra, masks, rows, sems) = refs[:-4], refs[-4:]
-    copies = [
-        pltpu.make_async_copy(far_spectra, spectra, sems.at[0]),
-        pltpu.make_async_copy(far_masks, masks, sems.at[1]),
-        pltpu.make_async_copy(far_rows, rows, sems.at[2]),
-    ]
-    for copy in copies:
-        copy.start()
-    stations, windows, seg, _, freq = spectra.shape
-    count = freq // BAND
-    band = lax.broadcasted_iota(jnp.int32, (count, freq), 0)
-    of_bin = lax.broadcasted_iota(jnp.int32, (count, freq), 1) // BAND
-    bands = jnp.where(band == of_bin, 1.0, 0.0).astype(BF16)
+    known = pltpu.make_async_copy(far_rows, rows, sems.at[count])
+    known.start()
+    known.wait()
     before = lax.rem(place[0] + groups - 1, groups) * stations
     after = lax.rem(place[0] + 1, groups) * stations
     own = place[0] * stations
-    for copy in copies:
-        copy.wait()
     second = rows[1:2]
     in_before = jnp.logical_and(second >= before, second < before + stations)
     in_own = jnp.logical_and(second >= own, second < own + stations)
@@ -181,29 +156,58 @@
     spot = jnp.where(in_own, NEAR + local, NEAR + stations + slots[1].astype(jnp.int32))
     index[0:1] = rows[0:1] - own
     index[1:2] = jnp.where(in_before, slots[0].astype(jnp.int32), spot)
-    values, squares, open_rows = [], [], []
+    copies[0].wait()
+    values = natural[...]
+    half = values.shape[1] // 2
+    right = values[:, half:]
+    left = pltpu.roll(flip(values[:, :half]), 1, 1)
+    shape = right.shape
+    root = math.sqrt(0.5)
+    targets[0][:, :half] = first_lane(shape, right * root, (right + left) * 0.5)
+    targets[0][:, half:] = first_lane(shape, left * root, (right - left) * 0.5)
+    for copy in copies[1:]:
+        copy.wait()
+
+
+def whiten_kernel(far_spectra, far_masks, *refs):
+    whitened, (spectra, masks, sems) = refs[:-3], refs[-3:]
+    stations, windows, seg, _, freq = spectra.shape
+    small = [pltpu.make_async_copy(far_masks, masks, sems.at[0])]
+    large = [pltpu.make_async_copy(far_spectra, spectra, sems.at[1])]
+    for copy in small + large:
+        copy.start()
+    count = freq // BAND
+    of_bin = lax.broadcasted_iota(jnp.int32, (count, freq), 1) // BAND
+    bands = jnp.where(lax.broadcasted_iota(jnp.int32, (count, freq), 0) == of_bin, 1.0, 0.0).astype(BF16)
+    of_bin = lax.broadcasted_iota(jnp.int32, (freq, count), 0) // BAND
+    sums = jnp.where(lax.broadcasted_iota(jnp.int32, (freq, count), 1) == of_bin, 1.0, 0.0).astype(BF16)
+    for copy in small:
+        copy.wait()
     eye = lax.broadcasted_iota(jnp.int32, (seg, seg), 0) == lax.broadcasted_iota(jnp.int32, (seg, seg), 1)
+    open_rows = []
+    for station in range(stations):
+        for window in range(windows):
+            mask = masks[station, window : window + 1].astype(F32)
+            mask = jnp.where(eye, jnp.broadcast_to(mask, (seg, seg)), 0.0)
+            open_rows.append(jnp.sum(mask, 1, keepdims=True))
+    large[0].wait()
+    values, squares = [], []
     for station in range(stations):
         for window in range(windows):
             block = spectra[station, window].astype(F32)
             real, imag = block[:, 0], block[:, 1]
             values.append((real, imag))
             squares.append(real * real + imag * imag)
-            mask = masks[station, window : window + 1].astype(F32)
-            mask = jnp.where(eye, jnp.broadcast_to(mask, (seg, seg)), 0.0)
-            open_rows.append(jnp.sum(mask, 1, keepdims=True))
-    high, low = two_parts(jnp.concatenate(squares, 0))
-    power = dot_rows(high, bands) + dot_rows(low, bands)
+    height = len(values) * seg
+    power = dot(jnp.concatenate(two_parts(jnp.concatenate(squares, 0)), 0), sums)
+    power = power[0:height] + power[height:]
     scale = lax.rsqrt(power * (1.0 / (2 * BAND)) + 1e-06) * jnp.concatenate(open_rows, 0)
-    high, low = two_parts(scale)
-    scale = dot(high, bands) + dot(low, bands)
-    at = 0
-    for station in range(stations):
-        for window in range(windows):
-            real, imag = values[at]
-            here = scale[at * seg : (at + 1) * seg]
-            whitened[window][station] = jnp.concatenate([real * here, imag * here], 0).astype(BF16)
-            at += 1
+    scale = dot(jnp.concatenate(two_parts(scale), 0), bands)
+    scale = scale[0:height] + scale[height:]
+    for number, (real, imag) in enumerate(values):
+        here = scale[number * seg : (number + 1) * seg]
+        block = jnp.concatenate([real * here, imag * here], 0).astype(BF16)
+        whitened[number % windows][number // windows] = block
 
 
 def select_kernel(stations, place, rows, *refs):
@@ -445,18 +449,17 @@
     before = lax.ppermute(rows, "pairs", forward)
     after = lax.ppermute(rows, "pairs", backward)
     place = group_index.reshape(1).astype(jnp.int32)
-    index, *whitened = call(
-        functools.partial(whiten_kernel, groups),
-        [struct(rows.shape, jnp.int32)] + [struct((stations, parts * seg, freq), BF16)] * windows,
-        [SMEM, HBM, HBM, HBM],
-        [VMEM] * (1 + windows),
+    whitened = call(
+        whiten_kernel,
+        [struct((stations, parts * seg, freq), BF16)] * windows,
+        [HBM] * 2,
+        [VMEM] * windows,
         [
             pltpu.VMEM(spectra.shape, BF16),
             pltpu.VMEM(masks.shape, jnp.int32),
-            pltpu.VMEM(rows.shape, jnp.int32),
-            pltpu.SemaphoreType.DMA((3,)),
+            pltpu.SemaphoreType.DMA((2,)),
         ],
-    )(place, far(rows), far(spectra), far(masks))
+    )(far(spectra), far(masks))
     block = struct((NEAR, parts * seg, freq), BF16)
     def select(wanted):
         return call(
@@ -477,14 +480,18 @@
         jnp.asarray(pick_matrix(pairs, seg, rank)),
         jnp.asarray(spread_matrix(pairs, seg, rank)),
     ]
-    staged = call(
-        stage_kernel,
-        [struct(one.shape, one.dtype) for one in fixed],
-        [VMEM] + [HBM] * len(fixed),
-        [VMEM] * len(fixed),
-        [pltpu.VMEM(start_basis.shape, F32), pltpu.SemaphoreType.DMA((len(fixed),))],
+    *staged, index = call(
+        functools.partial(stage_kernel, groups, stations),
+        [struct(one.shape, one.dtype) for one in fixed] + [struct(rows.shape, jnp.int32)],
+        [SMEM, VMEM] + [HBM] * (len(fixed) + 1),
+        [VMEM] * (len(fixed) + 1),
+        [
+            pltpu.VMEM(start_basis.shape, F32),
+            pltpu.VMEM(rows.shape, jnp.int32),
+            pltpu.SemaphoreType.DMA((len(fixed) + 1,)),
+        ],
         moved=parts * freq * lags,
-    )(to_last[0], *[far(one) for one in fixed])
+    )(place, to_next[0], far(rows), *[far(one) for one in fixed])
     core = jnp.mod(hour, 2).reshape(1).astype(jnp.int32)
     chip = (hour // 2).reshape(1).astype(jnp.int32)
     height = -(-(rank + 1) * pairs // 16) * 16
@@ -535,7 +542,7 @@
         [SMEM, VMEM, VMEM],
         [VMEM] * chips,
     )(chip, keep, got)
-    arrived = [swap(one, 2 * (step + 1)) for step, one in enumerate(sends)]
+    arrived = [swap(one, 2 * (step + 1)) for step, one in reversed(list(enumerate(sends)))]
     total, gram = call(
         functools.partial(gram_kernel, pairs, rank),
         [struct((height, width)), struct((pairs, 128))],

time: 37.6 us -> 37.1 us (0.987)
  waiting for transfers between devices: 9.9 us -> 9.48 us
where the time goes in v4:
time: 37.1 us; the launch traced here: 36.9 us
  starting transfers between devices  14.7 us (40%)
  Pallas kernels  11 us (30%)
  waiting for transfers between devices  9.48 us (26%)
  local copies, waits for them, and re-layouts  0.83 us (2%)
  between operations  0.75 us (2%)
    ppermute x5, waiting for transfers between devices, on_device(): lax.ppermute(value, 'hours', [(k, k ^ step) for k in range(slices)])  6.39 us
    ppermute x2, starting transfers between devices, on_device(): highs = [lax.ppermute(one, 'pairs', backward) for one in to_last]  5.77 us
    pallas_call x2, Pallas kernels, on_device(): call(functools.partial(window_kernel, sizes), outs, specs, [VMEM] * len(o...  5.23 us
    ppermute x5, starting transfers between devices, on_device(): lax.ppermute(value, 'hours', [(k, k ^ step) for k in range(slices)])  3.69 us
    ppermute x1, starting transfers between devices, on_device(): before = lax.ppermute(rows, 'pairs', forward)  3.08 us
    ppermute x2, waiting for transfers between devices, on_device(): lows = [lax.ppermute(one, 'pairs', forward) for one in to_next]  3.08 us
    pallas_call x1, Pallas kernels, on_device(): call(functools.partial(stage_kernel, groups, stations), [struct(one.shape...  2.35 us
    ppermute x1, starting transfers between devices, on_device(): after = lax.ppermute(rows, 'pairs', backward)  2.09 us
  transfers between devices with their start and end apart: 11, of which 7 were waited for; matrix products, arithmetic and copies ran while one was open for 2% of the time, Pallas kernels for 20%

profile of v4, /device:TPU:0, one launch (start us, length us, event | category | flops | bytes accessed | tf_op | source)
XLA Modules:
  0.0 36.9 jit_solution(14185850846934724181)
XLA Ops:
  0.6 3.1 %collective-permute-start.2 = (s32[2,12]{1,0:T(2,128)}, s32[2,12]{1,0:T(2,128)S(1)}, u32[]{:S(2)}, u32[]{:S(2)}) collective-permute-start(s32[2,12]{1,0:T(2,128)} %bitcast.8), channel_id=1, source_target_pairs={{0,8},{8,16},{16,24},{24,0},{1,9},{9,17},{17,25},{25,1},{2,10},{10... | collective-permute-start | bytes 296 | tf_op jit(solution)/shard_map/ppermute | solution.py:449
  3.7 2.1 %collective-permute-start = (s32[2,12]{1,0:T(2,128)}, s32[2,12]{1,0:T(2,128)S(1)}, u32[]{:S(2)}, u32[]{:S(2)}) collective-permute-start(s32[2,12]{1,0:T(2,128)} %bitcast.9), channel_id=1, source_target_pairs={{8,0},{16,8},{24,16},{0,24},{9,1},{17,9},{25,17},{1,25},{10,2},{18... | collective-permute-start | bytes 296 | tf_op jit(solution)/shard_map/ppermute | solution.py:450
  5.8 2.0 %shard_map.103 = (bf16[8,16,1024]{2,1,0:T(8,128)(2,1)S(1)}, bf16[8,16,1024]{2,1,0:T(8,128)(2,1)S(1)}) custom-call(bf16[8,2,8,2,1024]{4,3,2,1,0:T(2,128)(2,1)} %far_spectra.1, s32[8,2,8]{2,1,0:T(2,128)} %far_masks.1), custom_call_target="tpu_custom_call" | custom-call | tf_op jit(solution)/shard_map/pallas_call | solution.py:452
  7.8 0.0 collective-permute-done.2.rows
  7.8 0.3 shard_map.106
  8.1 2.0 %collective-permute-start.3 = (bf16[4,16,1024]{2,1,0:T(8,128)(2,1)S(1)}, bf16[4,16,1024]{2,1,0:T(8,128)(2,1)S(1)}, u32[]{:S(2)}, u32[]{:S(2)}) collective-permute-start(bf16[4,16,1024]{2,1,0:T(8,128)(2,1)S(1)} %get-tuple-element.32), channel_id=1, source_target_pairs={{8,0},{16,8},{24,16},{0,24},{9,1},{17,9},{25,17},{1,25},{10,2},{18... | collective-permute-start | bytes 393224 | tf_op jit(solution)/shard_map/ppermute | solution.py:474
  10.1 0.0 collective-permute-done.rows
  10.1 0.3 shard_map.104
  10.4 0.1 collective-permute-start.1
  10.5 3.8 %collective-permute-start.5 = (bf16[4,16,1024]{2,1,0:T(8,128)(2,1)S(1)}, bf16[4,16,1024]{2,1,0:T(8,128)(2,1)S(1)}, u32[]{:S(2)}, u32[]{:S(2)}) collective-permute-start(bf16[4,16,1024]{2,1,0:T(8,128)(2,1)S(1)} %get-tuple-element.40), channel_id=1, source_target_pairs={{8,0},{16,8},{24,16},{0,24},{9,1},{17,9},{25,17},{1,25},{10,2},{18... | collective-permute-start | bytes 393224 | tf_op jit(solution)/shard_map/ppermute | solution.py:474
  14.2 0.0 collective-permute-start.4
  14.2 2.3 %shard_map.105 = (f32[4,2048]{1,0:T(4,128)S(1)}, bf16[2048,1024]{1,0:T(8,128)(2,1)S(1)}, f32[2,1024]{1,0:T(2,128)S(1)}, bf16[128,256]{1,0:T(8,128)(2,1)S(1)}, bf...) custom-call(s32[1]{0:T(128)} %bitcast.place, bf16[4,16,1024]{2,1,0:T(8,128)(2,1)S(1)} %get-tuple-element.30.early, ...), custom_call_target="tpu_custom_call" | custom-call | bytes 4194304 | tf_op jit(solution)/shard_map/pallas_call | solution.py:483
  16.6 0.0 collective-permute-done.3.high
  16.6 2.1 %collective-permute-done.1.low = bf16[4,16,1024]{2,1,0:T(8,128)(2,1)S(1)} collective-permute-done((bf16[4,16,1024]{2,1,0:T(8,128)(2,1)S(1)}, bf16[4,16,1024]{2,1,0:T(8,128)(2,1)S(1)}, u32[]{:S(2)}, u32[]{:S(2)}) %collective-permute-start.1) | collective-permute-done | bytes 131104 | tf_op jit(solution)/shard_map/ppermute | solution.py:473
  18.7 2.6 %shard_map.107 = (f32[12,2048]{1,0:T(8,128)S(1)}, f32[64,2048]{1,0:T(8,128)S(1)}) custom-call(s32[2,12]{1,0:T(2,128)S(1)} %get-tuple-element.31.index, bf16[8,16,1024]{2,1,0:T(8,128)(2,1)S(1)} %get-tuple-element.28.refs_0_.own, bf16[4,16,1024]{2,1,0:T(8,128)(2,1)S(1)} %collective-permute-done.1.low, bf16[4,16,1024]{2,1,0:T(8,128)(2,1)S(1)} %collective-permute-done.3.high, ...), custom_call_target="tpu_custom_call" | custom-call | flops 402653184 | bytes 4194304 | tf_op jit(solution)/shard_map/pallas_call | solution.py:520
  21.3 0.0 collective-permute-done.5.high
  21.3 0.9 %collective-permute-done.4.low = bf16[4,16,1024]{2,1,0:T(8,128)(2,1)S(1)} collective-permute-done((bf16[4,16,1024]{2,1,0:T(8,128)(2,1)S(1)}, bf16[4,16,1024]{2,1,0:T(8,128)(2,1)S(1)}, u32[]{:S(2)}, u32[]{:S(2)}) %collective-permute-start.4) | collective-permute-done | bytes 131104 | tf_op jit(solution)/shard_map/ppermute | solution.py:473
  22.3 2.7 %shard_map.108 = (f32[12,2048]{1,0:T(8,128)S(1)}, bf16[4,64,256]{2,1,0:T(8,128)(2,1)S(1)}, f32[4,64,256]{2,1,0:T(8,128)S(1)}) custom-call(s32[2,12]{1,0:T(2,128)S(1)} %get-tuple-element.31.index, bf16[8,16,1024]{2,1,0:T(8,128)(2,1)S(1)} %get-tuple-element.29.refs_1_.own, bf16[4,16,1024]{2,1,0:T(8,128)(2,1)S(1)} %collective-permute-done.4.low, ...), custom_call_target="tpu_custom_call" | custom-call | flops 402653184 | bytes 4194304 | tf_op jit(solution)/shard_map/pallas_call | solution.py:520
  24.9 0.1 collective-permute-start.6
  25.0 1.3 %collective-permute-done.6.got = bf16[4,64,256]{2,1,0:T(8,128)(2,1)S(1)} collective-permute-done((bf16[4,64,256]{2,1,0:T(8,128)(2,1)S(1)}, bf16[4,64,256]{2,1,0:T(8,128)(2,1)S(1)}, u32[]{:S(2)}, u32[]{:S(2)}) %collective-permute-start.6) | collective-permute-done | bytes 131104 | tf_op jit(solution)/shard_map/ppermute | solution.py:535
  26.4 2.5 %collective-permute-start.7 = (bf16[208,256]{1,0:T(8,128)(2,1)S(1)}, bf16[208,256]{1,0:T(8,128)(2,1)S(1)}, u32[]{:S(2)}, u32[]{:S(2)}) collective-permute-start(bf16[208,256]{1,0:T(8,128)(2,1)S(1)} %get-tuple-element.46), channel_id=1, source_target_pairs={{0,6},{1,7},{2,4},{3,5},{4,2},{5,3},{6,0},{7,1},{8,14},{9,15},{10,... | collective-permute-start | bytes 319496 | tf_op jit(solution)/shard_map/ppermute | solution.py:535
  28.9 0.5 %collective-permute-start.8 = (bf16[208,256]{1,0:T(8,128)(2,1)S(1)}, bf16[208,256]{1,0:T(8,128)(2,1)S(1)}, u32[]{:S(2)}, u32[]{:S(2)}) collective-permute-start(bf16[208,256]{1,0:T(8,128)(2,1)S(1)} %get-tuple-element.47), channel_id=1, source_target_pairs={{0,4},{1,5},{2,6},{3,7},{4,0},{5,1},{6,2},{7,3},{8,12},{9,13},{10,... | collective-permute-start | bytes 319496 | tf_op jit(solution)/shard_map/ppermute | solution.py:535
  29.4 0.5 %collective-permute-start.9 = (bf16[208,256]{1,0:T(8,128)(2,1)S(1)}, bf16[208,256]{1,0:T(8,128)(2,1)S(1)}, u32[]{:S(2)}, u32[]{:S(2)}) collective-permute-start(bf16[208,256]{1,0:T(8,128)(2,1)S(1)} %get-tuple-element.48), channel_id=1, source_target_pairs={{0,2},{1,3},{2,0},{3,1},{4,6},{5,7},{6,4},{7,5},{8,10},{9,11},{10,... | collective-permute-start | bytes 319496 | tf_op jit(solution)/shard_map/ppermute | solution.py:535
  30.0 2.5 %collective-permute-done.7.refs_0_ = bf16[208,256]{1,0:T(8,128)(2,1)S(1)} collective-permute-done((bf16[208,256]{1,0:T(8,128)(2,1)S(1)}, bf16[208,256]{1,0:T(8,128)(2,1)S(1)}, u32[]{:S(2)}, u32[]{:S(2)}) %collective-permute-start.7) | collective-permute-done | bytes 106528 | tf_op jit(solution)/shard_map/ppermute | solution.py:535
  32.5 2.2 %collective-permute-done.8.refs_1_ = bf16[208,256]{1,0:T(8,128)(2,1)S(1)} collective-permute-done((bf16[208,256]{1,0:T(8,128)(2,1)S(1)}, bf16[208,256]{1,0:T(8,128)(2,1)S(1)}, u32[]{:S(2)}, u32[]{:S(2)}) %collective-permute-start.8) | collective-permute-done | bytes 106528 | tf_op jit(solution)/shard_map/ppermute | solution.py:535
  34.7 0.1 collective-permute-done.9.refs_2_
  34.7 0.2 shard_map.110
  34.9 0.1 collective-permute-start.10
  35.0 0.8 %copy.11 = f32[12,2,2048]{2,1,0:T(2,128)} copy(f32[12,2,2048]{2,0,1:T(8,128)S(1)} %pad_maximum_fusion) | data formatting | bytes 393216
  35.8 0.3 collective-permute-done.10.got
  36.1 0.7 %shard_map.111 = (f32[12,256]{1,0:T(8,128)}, f32[12,4,256]{2,1,0:T(4,128)}) custom-call(f32[64,256]{1,0:T(8,128)S(1)} %get-tuple-element.49.total, f32[12,128]{1,0:T(8,128)S(1)} %get-tuple-element.50.mine, f32[12,128]{1,0:T(8,128)S(1)} %collective-permute-done.10.got), custom_call_target="tpu_custom_call" | custom-call | tf_op jit(solution)/shard_map/pallas_call | solution.py:553
  (2 shorter events, 0.1 us)
Async XLA Ops:
  0.6 7.2 %collective-permute-start.2 = (s32[2,12]{1,0:T(2,128)}, s32[2,12]{1,0:T(2,128)S(1)}, u32[]{:S(2)}, u32[]{:S(2)}) collective-permute-start(s32[2,12]{1,0:T(2,128)} %bitcast.8), channel_id=1, source_target_pairs={{0,8},{8,16},{16,24},{24,0},{1,9},{9,17},{17,25},{25,1},{2,10},{10... | collective-permute-start | bytes 296 | tf_op jit(solution)/shard_map/ppermute | solution.py:449
  3.7 6.4 %collective-permute-start = (s32[2,12]{1,0:T(2,128)}, s32[2,12]{1,0:T(2,128)S(1)}, u32[]{:S(2)}, u32[]{:S(2)}) collective-permute-start(s32[2,12]{1,0:T(2,128)} %bitcast.9), channel_id=1, source_target_pairs={{8,0},{16,8},{24,16},{0,24},{9,1},{17,9},{25,17},{1,25},{10,2},{18... | collective-permute-start | bytes 296 | tf_op jit(solution)/shard_map/ppermute | solution.py:450
  8.1 8.5 %collective-permute-start.3 = (bf16[4,16,1024]{2,1,0:T(8,128)(2,1)S(1)}, bf16[4,16,1024]{2,1,0:T(8,128)(2,1)S(1)}, u32[]{:S(2)}, u32[]{:S(2)}) collective-permute-start(bf16[4,16,1024]{2,1,0:T(8,128)(2,1)S(1)} %get-tuple-element.32), channel_id=1, source_target_pairs={{8,0},{16,8},{24,16},{0,24},{9,1},{17,9},{25,17},{1,25},{10,2},{18... | collective-permute-start | bytes 393224 | tf_op jit(solution)/shard_map/ppermute | solution.py:474
  10.4 8.4 %collective-permute-start.1 = (bf16[4,16,1024]{2,1,0:T(8,128)(2,1)S(1)}, bf16[4,16,1024]{2,1,0:T(8,128)(2,1)S(1)}, u32[]{:S(2)}, u32[]{:S(2)}) collective-permute-start(bf16[4,16,1024]{2,1,0:T(8,128)(2,1)S(1)} %get-tuple-element.30.early), channel_id=1, source_target_pairs={{0,8},{8,16},{16,24},{24,0},{1,9},{9,17},{17,25},{25,1},{2,10},{10... | collective-permute-start | bytes 393224 | tf_op jit(solution)/shard_map/ppermute | solution.py:473
  10.5 10.9 %collective-permute-start.5 = (bf16[4,16,1024]{2,1,0:T(8,128)(2,1)S(1)}, bf16[4,16,1024]{2,1,0:T(8,128)(2,1)S(1)}, u32[]{:S(2)}, u32[]{:S(2)}) collective-permute-start(bf16[4,16,1024]{2,1,0:T(8,128)(2,1)S(1)} %get-tuple-element.40), channel_id=1, source_target_pairs={{8,0},{16,8},{24,16},{0,24},{9,1},{17,9},{25,17},{1,25},{10,2},{18... | collective-permute-start | bytes 393224 | tf_op jit(solution)/shard_map/ppermute | solution.py:474
  14.2 8.0 %collective-permute-start.4 = (bf16[4,16,1024]{2,1,0:T(8,128)(2,1)S(1)}, bf16[4,16,1024]{2,1,0:T(8,128)(2,1)S(1)}, u32[]{:S(2)}, u32[]{:S(2)}) collective-permute-start(bf16[4,16,1024]{2,1,0:T(8,128)(2,1)S(1)} %get-tuple-element.39), channel_id=1, source_target_pairs={{0,8},{8,16},{16,24},{24,0},{1,9},{9,17},{17,25},{25,1},{2,10},{10... | collective-permute-start | bytes 393224 | tf_op jit(solution)/shard_map/ppermute | solution.py:473
  24.9 1.4 %collective-permute-start.6 = (bf16[4,64,256]{2,1,0:T(8,128)(2,1)S(1)}, bf16[4,64,256]{2,1,0:T(8,128)(2,1)S(1)}, u32[]{:S(2)}, u32[]{:S(2)}) collective-permute-start(bf16[4,64,256]{2,1,0:T(8,128)(2,1)S(1)} %get-tuple-element.44), channel_id=1, source_target_pairs={{0,1},{1,0},{2,3},{3,2},{4,5},{5,4},{6,7},{7,6},{8,9},{9,8},{10,11... | collective-permute-start | bytes 393224 | tf_op jit(solution)/shard_map/ppermute | solution.py:535
  26.4 6.1 %collective-permute-start.7 = (bf16[208,256]{1,0:T(8,128)(2,1)S(1)}, bf16[208,256]{1,0:T(8,128)(2,1)S(1)}, u32[]{:S(2)}, u32[]{:S(2)}) collective-permute-start(bf16[208,256]{1,0:T(8,128)(2,1)S(1)} %get-tuple-element.46), channel_id=1, source_target_pairs={{0,6},{1,7},{2,4},{3,5},{4,2},{5,3},{6,0},{7,1},{8,14},{9,15},{10,... | collective-permute-start | bytes 319496 | tf_op jit(solution)/shard_map/ppermute | solution.py:535
  28.9 5.8 %collective-permute-start.8 = (bf16[208,256]{1,0:T(8,128)(2,1)S(1)}, bf16[208,256]{1,0:T(8,128)(2,1)S(1)}, u32[]{:S(2)}, u32[]{:S(2)}) collective-permute-start(bf16[208,256]{1,0:T(8,128)(2,1)S(1)} %get-tuple-element.47), channel_id=1, source_target_pairs={{0,4},{1,5},{2,6},{3,7},{4,0},{5,1},{6,2},{7,3},{8,12},{9,13},{10,... | collective-permute-start | bytes 319496 | tf_op jit(solution)/shard_map/ppermute | solution.py:535
  29.4 5.3 %collective-permute-start.9 = (bf16[208,256]{1,0:T(8,128)(2,1)S(1)}, bf16[208,256]{1,0:T(8,128)(2,1)S(1)}, u32[]{:S(2)}, u32[]{:S(2)}) collective-permute-start(bf16[208,256]{1,0:T(8,128)(2,1)S(1)} %get-tuple-element.48), channel_id=1, source_target_pairs={{0,2},{1,3},{2,0},{3,1},{4,6},{5,7},{6,4},{7,5},{8,10},{9,11},{10,... | collective-permute-start | bytes 319496 | tf_op jit(solution)/shard_map/ppermute | solution.py:535
  34.9 1.2 %collective-permute-start.10 = (f32[12,128]{1,0:T(8,128)S(1)}, f32[12,128]{1,0:T(8,128)S(1)}, u32[]{:S(2)}, u32[]{:S(2)}) collective-permute-start(f32[12,128]{1,0:T(8,128)S(1)} %get-tuple-element.50.mine), channel_id=1, source_target_pairs={{0,1},{1,0},{2,3},{3,2},{4,5},{5,4},{6,7},{7,6},{8,9},{9,8},{10,11... | collective-permute-start | bytes 18440 | tf_op jit(solution)/shard_map/ppermute | solution.py:535

commit v5 on v4

--- a/solution.py
+++ b/solution.py
@@ -176,11 +176,9 @@
     large = [pltpu.make_async_copy(far_spectra, spectra, sems.at[1])]
     for copy in small + large:
         copy.start()
-    count = freq // BAND
-    of_bin = lax.broadcasted_iota(jnp.int32, (count, freq), 1) // BAND
-    bands = jnp.where(lax.broadcasted_iota(jnp.int32, (count, freq), 0) == of_bin, 1.0, 0.0).astype(BF16)
-    of_bin = lax.broadcasted_iota(jnp.int32, (freq, count), 0) // BAND
-    sums = jnp.where(lax.broadcasted_iota(jnp.int32, (freq, count), 1) == of_bin, 1.0, 0.0).astype(BF16)
+    tile = (128, 128)
+    same = lax.broadcasted_iota(jnp.int32, tile, 0) // BAND == lax.broadcasted_iota(jnp.int32, tile, 1) // BAND
+    bands = jnp.where(same, 1.0, 0.0).astype(BF16)
     for copy in small:
         copy.wait()
     eye = lax.broadcasted_iota(jnp.int32, (seg, seg), 0) == lax.broadcasted_iota(jnp.int32, (seg, seg), 1)
@@ -199,11 +197,13 @@
             values.append((real, imag))
             squares.append(real * real + imag * imag)
     height = len(values) * seg
-    power = dot(jnp.concatenate(two_parts(jnp.concatenate(squares, 0)), 0), sums)
-    power = power[0:height] + power[height:]
-    scale = lax.rsqrt(power * (1.0 / (2 * BAND)) + 1e-06) * jnp.concatenate(open_rows, 0)
-    scale = dot(jnp.concatenate(two_parts(scale), 0), bands)
-    scale = scale[0:height] + scale[height:]
+    squares = jnp.concatenate(squares, 0)
+    here = jnp.concatenate(open_rows, 0)
+    scales = []
+    for at in range(0, freq, 128):
+        power = dot(jnp.concatenate(two_parts(squares[:, at : at + 128]), 1), jnp.concatenate([bands, bands], 0))
+        scales.append(lax.rsqrt(power * (1.0 / (2 * BAND)) + 1e-06) * here)
+    scale = jnp.concatenate(scales, 1)
     for number, (real, imag) in enumerate(values):
         here = scale[number * seg : (number + 1) * seg]
         block = jnp.concatenate([real * here, imag * here], 0).astype(BF16)

time: 37.1 us -> 36.9 us (level)
  no operation moved by 1% of the time
where the time goes in v5:
time: 36.9 us; the launch traced here: 36.7 us
  starting transfers between devices  14.8 us (40%)
  Pallas kernels  10.9 us (30%)
  waiting for transfers between devices  9.47 us (26%)
  local copies, waits for them, and re-layouts  0.83 us (2%)
  between operations  0.75 us (2%)
    ppermute x5, waiting for transfers between devices, on_device(): lax.ppermute(value, 'hours', [(k, k ^ step) for k in range(slices)])  6.39 us
    ppermute x2, starting transfers between devices, on_device(): highs = [lax.ppermute(one, 'pairs', backward) for one in to_last]  5.77 us
    pallas_call x2, Pallas kernels, on_device(): call(functools.partial(window_kernel, sizes), outs, specs, [VMEM] * len(o...  5.23 us
    ppermute x5, starting transfers between devices, on_device(): lax.ppermute(value, 'hours', [(k, k ^ step) for k in range(slices)])  3.69 us
    ppermute x1, starting transfers between devices, on_device(): before = lax.ppermute(rows, 'pairs', forward)  3.08 us
    ppermute x2, waiting for transfers between devices, on_device(): lows = [lax.ppermute(one, 'pairs', forward) for one in to_next]  3.07 us
    pallas_call x1, Pallas kernels, on_device(): call(functools.partial(stage_kernel, groups, stations), [struct(one.shape...  2.35 us
    ppermute x1, starting transfers between devices, on_device(): after = lax.ppermute(rows, 'pairs', backward)  2.09 us
  transfers between devices with their start and end apart: 11, of which 7 were waited for; matrix products, arithmetic and copies ran while one was open for 2% of the time, Pallas kernels for 20%

profile of v5, /device:TPU:0, one launch (start us, length us, event | category | flops | bytes accessed | tf_op | source)
XLA Modules:
  0.0 36.7 jit_solution(1861325260188646720)
XLA Ops:
  0.6 3.1 %collective-permute-start.2 = (s32[2,12]{1,0:T(2,128)}, s32[2,12]{1,0:T(2,128)S(1)}, u32[]{:S(2)}, u32[]{:S(2)}) collective-permute-start(s32[2,12]{1,0:T(2,128)} %bitcast.8), channel_id=1, source_target_pairs={{0,8},{8,16},{16,24},{24,0},{1,9},{9,17},{17,25},{25,1},{2,10},{10... | collective-permute-start | bytes 296 | tf_op jit(solution)/shard_map/ppermute | solution.py:449
  3.7 2.1 %collective-permute-start = (s32[2,12]{1,0:T(2,128)}, s32[2,12]{1,0:T(2,128)S(1)}, u32[]{:S(2)}, u32[]{:S(2)}) collective-permute-start(s32[2,12]{1,0:T(2,128)} %bitcast.9), channel_id=1, source_target_pairs={{8,0},{16,8},{24,16},{0,24},{9,1},{17,9},{25,17},{1,25},{10,2},{18... | collective-permute-start | bytes 296 | tf_op jit(solution)/shard_map/ppermute | solution.py:450
  5.8 1.9 %shard_map.103 = (bf16[8,16,1024]{2,1,0:T(8,128)(2,1)S(1)}, bf16[8,16,1024]{2,1,0:T(8,128)(2,1)S(1)}) custom-call(bf16[8,2,8,2,1024]{4,3,2,1,0:T(2,128)(2,1)} %far_spectra.1, s32[8,2,8]{2,1,0:T(2,128)} %far_masks.1), custom_call_target="tpu_custom_call" | custom-call | tf_op jit(solution)/shard_map/pallas_call | solution.py:452
  7.7 0.0 collective-permute-done.2.rows
  7.7 0.3 shard_map.106
  7.9 2.0 %collective-permute-start.3 = (bf16[4,16,1024]{2,1,0:T(8,128)(2,1)S(1)}, bf16[4,16,1024]{2,1,0:T(8,128)(2,1)S(1)}, u32[]{:S(2)}, u32[]{:S(2)}) collective-permute-start(bf16[4,16,1024]{2,1,0:T(8,128)(2,1)S(1)} %get-tuple-element.32), channel_id=1, source_target_pairs={{8,0},{16,8},{24,16},{0,24},{9,1},{17,9},{25,17},{1,25},{10,2},{18... | collective-permute-start | bytes 393224 | tf_op jit(solution)/shard_map/ppermute | solution.py:474
  10.0 0.0 collective-permute-done.rows
  10.0 0.3 shard_map.104
  10.2 0.1 collective-permute-start.1
  10.3 3.8 %collective-permute-start.5 = (bf16[4,16,1024]{2,1,0:T(8,128)(2,1)S(1)}, bf16[4,16,1024]{2,1,0:T(8,128)(2,1)S(1)}, u32[]{:S(2)}, u32[]{:S(2)}) collective-permute-start(bf16[4,16,1024]{2,1,0:T(8,128)(2,1)S(1)} %get-tuple-element.40), channel_id=1, source_target_pairs={{8,0},{16,8},{24,16},{0,24},{9,1},{17,9},{25,17},{1,25},{10,2},{18... | collective-permute-start | bytes 393224 | tf_op jit(solution)/shard_map/ppermute | solution.py:474
  14.1 0.0 collective-permute-start.4
  14.1 2.3 %shard_map.105 = (f32[4,2048]{1,0:T(4,128)S(1)}, bf16[2048,1024]{1,0:T(8,128)(2,1)S(1)}, f32[2,1024]{1,0:T(2,128)S(1)}, bf16[128,256]{1,0:T(8,128)(2,1)S(1)}, bf...) custom-call(s32[1]{0:T(128)} %bitcast.place, bf16[4,16,1024]{2,1,0:T(8,128)(2,1)S(1)} %get-tuple-element.30.early, ...), custom_call_target="tpu_custom_call" | custom-call | bytes 4194304 | tf_op jit(solution)/shard_map/pallas_call | solution.py:483
  16.5 0.0 collective-permute-done.3.high
  16.5 2.1 %collective-permute-done.1.low = bf16[4,16,1024]{2,1,0:T(8,128)(2,1)S(1)} collective-permute-done((bf16[4,16,1024]{2,1,0:T(8,128)(2,1)S(1)}, bf16[4,16,1024]{2,1,0:T(8,128)(2,1)S(1)}, u32[]{:S(2)}, u32[]{:S(2)}) %collective-permute-start.1) | collective-permute-done | bytes 131104 | tf_op jit(solution)/shard_map/ppermute | solution.py:473
  18.6 2.6 %shard_map.107 = (f32[12,2048]{1,0:T(8,128)S(1)}, f32[64,2048]{1,0:T(8,128)S(1)}) custom-call(s32[2,12]{1,0:T(2,128)S(1)} %get-tuple-element.31.index, bf16[8,16,1024]{2,1,0:T(8,128)(2,1)S(1)} %get-tuple-element.28.refs_0_.own, bf16[4,16,1024]{2,1,0:T(8,128)(2,1)S(1)} %collective-permute-done.1.low, bf16[4,16,1024]{2,1,0:T(8,128)(2,1)S(1)} %collective-permute-done.3.high, ...), custom_call_target="tpu_custom_call" | custom-call | flops 402653184 | bytes 4194304 | tf_op jit(solution)/shard_map/pallas_call | solution.py:520
  21.2 0.0 collective-permute-done.5.high
  21.2 0.9 %collective-permute-done.4.low = bf16[4,16,1024]{2,1,0:T(8,128)(2,1)S(1)} collective-permute-done((bf16[4,16,1024]{2,1,0:T(8,128)(2,1)S(1)}, bf16[4,16,1024]{2,1,0:T(8,128)(2,1)S(1)}, u32[]{:S(2)}, u32[]{:S(2)}) %collective-permute-start.4) | collective-permute-done | bytes 131104 | tf_op jit(solution)/shard_map/ppermute | solution.py:473
  22.1 2.7 %shard_map.108 = (f32[12,2048]{1,0:T(8,128)S(1)}, bf16[4,64,256]{2,1,0:T(8,128)(2,1)S(1)}, f32[4,64,256]{2,1,0:T(8,128)S(1)}) custom-call(s32[2,12]{1,0:T(2,128)S(1)} %get-tuple-element.31.index, bf16[8,16,1024]{2,1,0:T(8,128)(2,1)S(1)} %get-tuple-element.29.refs_1_.own, bf16[4,16,1024]{2,1,0:T(8,128)(2,1)S(1)} %collective-permute-done.4.low, ...), custom_call_target="tpu_custom_call" | custom-call | flops 402653184 | bytes 4194304 | tf_op jit(solution)/shard_map/pallas_call | solution.py:520
  24.8 0.1 collective-permute-start.6
  24.9 1.3 %collective-permute-done.6.got = bf16[4,64,256]{2,1,0:T(8,128)(2,1)S(1)} collective-permute-done((bf16[4,64,256]{2,1,0:T(8,128)(2,1)S(1)}, bf16[4,64,256]{2,1,0:T(8,128)(2,1)S(1)}, u32[]{:S(2)}, u32[]{:S(2)}) %collective-permute-start.6) | collective-permute-done | bytes 131104 | tf_op jit(solution)/shard_map/ppermute | solution.py:535
  26.3 2.5 %collective-permute-start.7 = (bf16[208,256]{1,0:T(8,128)(2,1)S(1)}, bf16[208,256]{1,0:T(8,128)(2,1)S(1)}, u32[]{:S(2)}, u32[]{:S(2)}) collective-permute-start(bf16[208,256]{1,0:T(8,128)(2,1)S(1)} %get-tuple-element.46), channel_id=1, source_target_pairs={{0,6},{1,7},{2,4},{3,5},{4,2},{5,3},{6,0},{7,1},{8,14},{9,15},{10,... | collective-permute-start | bytes 319496 | tf_op jit(solution)/shard_map/ppermute | solution.py:535
  28.8 0.5 %collective-permute-start.8 = (bf16[208,256]{1,0:T(8,128)(2,1)S(1)}, bf16[208,256]{1,0:T(8,128)(2,1)S(1)}, u32[]{:S(2)}, u32[]{:S(2)}) collective-permute-start(bf16[208,256]{1,0:T(8,128)(2,1)S(1)} %get-tuple-element.47), channel_id=1, source_target_pairs={{0,4},{1,5},{2,6},{3,7},{4,0},{5,1},{6,2},{7,3},{8,12},{9,13},{10,... | collective-permute-start | bytes 319496 | tf_op jit(solution)/shard_map/ppermute | solution.py:535
  29.3 0.5 %collective-permute-start.9 = (bf16[208,256]{1,0:T(8,128)(2,1)S(1)}, bf16[208,256]{1,0:T(8,128)(2,1)S(1)}, u32[]{:S(2)}, u32[]{:S(2)}) collective-permute-start(bf16[208,256]{1,0:T(8,128)(2,1)S(1)} %get-tuple-element.48), channel_id=1, source_target_pairs={{0,2},{1,3},{2,0},{3,1},{4,6},{5,7},{6,4},{7,5},{8,10},{9,11},{10,... | collective-permute-start | bytes 319496 | tf_op jit(solution)/shard_map/ppermute | solution.py:535
  29.8 2.5 %collective-permute-done.7.refs_0_ = bf16[208,256]{1,0:T(8,128)(2,1)S(1)} collective-permute-done((bf16[208,256]{1,0:T(8,128)(2,1)S(1)}, bf16[208,256]{1,0:T(8,128)(2,1)S(1)}, u32[]{:S(2)}, u32[]{:S(2)}) %collective-permute-start.7) | collective-permute-done | bytes 106528 | tf_op jit(solution)/shard_map/ppermute | solution.py:535
  32.4 2.2 %collective-permute-done.8.refs_1_ = bf16[208,256]{1,0:T(8,128)(2,1)S(1)} collective-permute-done((bf16[208,256]{1,0:T(8,128)(2,1)S(1)}, bf16[208,256]{1,0:T(8,128)(2,1)S(1)}, u32[]{:S(2)}, u32[]{:S(2)}) %collective-permute-start.8) | collective-permute-done | bytes 106528 | tf_op jit(solution)/shard_map/ppermute | solution.py:535
  34.5 0.1 collective-permute-done.9.refs_2_
  34.6 0.2 shard_map.110
  34.8 0.1 collective-permute-start.10
  34.9 0.8 %copy.11 = f32[12,2,2048]{2,1,0:T(2,128)} copy(f32[12,2,2048]{2,0,1:T(8,128)S(1)} %pad_maximum_fusion) | data formatting | bytes 393216
  35.7 0.3 collective-permute-done.10.got
  36.0 0.7 %shard_map.111 = (f32[12,256]{1,0:T(8,128)}, f32[12,4,256]{2,1,0:T(4,128)}) custom-call(f32[64,256]{1,0:T(8,128)S(1)} %get-tuple-element.49.total, f32[12,128]{1,0:T(8,128)S(1)} %get-tuple-element.50.mine, f32[12,128]{1,0:T(8,128)S(1)} %collective-permute-done.10.got), custom_call_target="tpu_custom_call" | custom-call | tf_op jit(solution)/shard_map/pallas_call | solution.py:553
  (2 shorter events, 0.1 us)
Async XLA Ops:
  0.6 7.0 %collective-permute-start.2 = (s32[2,12]{1,0:T(2,128)}, s32[2,12]{1,0:T(2,128)S(1)}, u32[]{:S(2)}, u32[]{:S(2)}) collective-permute-start(s32[2,12]{1,0:T(2,128)} %bitcast.8), channel_id=1, source_target_pairs={{0,8},{8,16},{16,24},{24,0},{1,9},{9,17},{17,25},{25,1},{2,10},{10... | collective-permute-start | bytes 296 | tf_op jit(solution)/shard_map/ppermute | solution.py:449
  3.7 6.2 %collective-permute-start = (s32[2,12]{1,0:T(2,128)}, s32[2,12]{1,0:T(2,128)S(1)}, u32[]{:S(2)}, u32[]{:S(2)}) collective-permute-start(s32[2,12]{1,0:T(2,128)} %bitcast.9), channel_id=1, source_target_pairs={{8,0},{16,8},{24,16},{0,24},{9,1},{17,9},{25,17},{1,25},{10,2},{18... | collective-permute-start | bytes 296 | tf_op jit(solution)/shard_map/ppermute | solution.py:450
  7.9 8.5 %collective-permute-start.3 = (bf16[4,16,1024]{2,1,0:T(8,128)(2,1)S(1)}, bf16[4,16,1024]{2,1,0:T(8,128)(2,1)S(1)}, u32[]{:S(2)}, u32[]{:S(2)}) collective-permute-start(bf16[4,16,1024]{2,1,0:T(8,128)(2,1)S(1)} %get-tuple-element.32), channel_id=1, source_target_pairs={{8,0},{16,8},{24,16},{0,24},{9,1},{17,9},{25,17},{1,25},{10,2},{18... | collective-permute-start | bytes 393224 | tf_op jit(solution)/shard_map/ppermute | solution.py:474
  10.2 8.4 %collective-permute-start.1 = (bf16[4,16,1024]{2,1,0:T(8,128)(2,1)S(1)}, bf16[4,16,1024]{2,1,0:T(8,128)(2,1)S(1)}, u32[]{:S(2)}, u32[]{:S(2)}) collective-permute-start(bf16[4,16,1024]{2,1,0:T(8,128)(2,1)S(1)} %get-tuple-element.30.early), channel_id=1, source_target_pairs={{0,8},{8,16},{16,24},{24,0},{1,9},{9,17},{17,25},{25,1},{2,10},{10... | collective-permute-start | bytes 393224 | tf_op jit(solution)/shard_map/ppermute | solution.py:473
  10.3 10.9 %collective-permute-start.5 = (bf16[4,16,1024]{2,1,0:T(8,128)(2,1)S(1)}, bf16[4,16,1024]{2,1,0:T(8,128)(2,1)S(1)}, u32[]{:S(2)}, u32[]{:S(2)}) collective-permute-start(bf16[4,16,1024]{2,1,0:T(8,128)(2,1)S(1)} %get-tuple-element.40), channel_id=1, source_target_pairs={{8,0},{16,8},{24,16},{0,24},{9,1},{17,9},{25,17},{1,25},{10,2},{18... | collective-permute-start | bytes 393224 | tf_op jit(solution)/shard_map/ppermute | solution.py:474
  14.1 8.0 %collective-permute-start.4 = (bf16[4,16,1024]{2,1,0:T(8,128)(2,1)S(1)}, bf16[4,16,1024]{2,1,0:T(8,128)(2,1)S(1)}, u32[]{:S(2)}, u32[]{:S(2)}) collective-permute-start(bf16[4,16,1024]{2,1,0:T(8,128)(2,1)S(1)} %get-tuple-element.39), channel_id=1, source_target_pairs={{0,8},{8,16},{16,24},{24,0},{1,9},{9,17},{17,25},{25,1},{2,10},{10... | collective-permute-start | bytes 393224 | tf_op jit(solution)/shard_map/ppermute | solution.py:473
  24.8 1.4 %collective-permute-start.6 = (bf16[4,64,256]{2,1,0:T(8,128)(2,1)S(1)}, bf16[4,64,256]{2,1,0:T(8,128)(2,1)S(1)}, u32[]{:S(2)}, u32[]{:S(2)}) collective-permute-start(bf16[4,64,256]{2,1,0:T(8,128)(2,1)S(1)} %get-tuple-element.44), channel_id=1, source_target_pairs={{0,1},{1,0},{2,3},{3,2},{4,5},{5,4},{6,7},{7,6},{8,9},{9,8},{10,11... | collective-permute-start | bytes 393224 | tf_op jit(solution)/shard_map/ppermute | solution.py:535
  26.3 6.1 %collective-permute-start.7 = (bf16[208,256]{1,0:T(8,128)(2,1)S(1)}, bf16[208,256]{1,0:T(8,128)(2,1)S(1)}, u32[]{:S(2)}, u32[]{:S(2)}) collective-permute-start(bf16[208,256]{1,0:T(8,128)(2,1)S(1)} %get-tuple-element.46), channel_id=1, source_target_pairs={{0,6},{1,7},{2,4},{3,5},{4,2},{5,3},{6,0},{7,1},{8,14},{9,15},{10,... | collective-permute-start | bytes 319496 | tf_op jit(solution)/shard_map/ppermute | solution.py:535
  28.8 5.8 %collective-permute-start.8 = (bf16[208,256]{1,0:T(8,128)(2,1)S(1)}, bf16[208,256]{1,0:T(8,128)(2,1)S(1)}, u32[]{:S(2)}, u32[]{:S(2)}) collective-permute-start(bf16[208,256]{1,0:T(8,128)(2,1)S(1)} %get-tuple-element.47), channel_id=1, source_target_pairs={{0,4},{1,5},{2,6},{3,7},{4,0},{5,1},{6,2},{7,3},{8,12},{9,13},{10,... | collective-permute-start | bytes 319496 | tf_op jit(solution)/shard_map/ppermute | solution.py:535
  29.3 5.3 %collective-permute-start.9 = (bf16[208,256]{1,0:T(8,128)(2,1)S(1)}, bf16[208,256]{1,0:T(8,128)(2,1)S(1)}, u32[]{:S(2)}, u32[]{:S(2)}) collective-permute-start(bf16[208,256]{1,0:T(8,128)(2,1)S(1)} %get-tuple-element.48), channel_id=1, source_target_pairs={{0,2},{1,3},{2,0},{3,1},{4,6},{5,7},{6,4},{7,5},{8,10},{9,11},{10,... | collective-permute-start | bytes 319496 | tf_op jit(solution)/shard_map/ppermute | solution.py:535
  34.8 1.2 %collective-permute-start.10 = (f32[12,128]{1,0:T(8,128)S(1)}, f32[12,128]{1,0:T(8,128)S(1)}, u32[]{:S(2)}, u32[]{:S(2)}) collective-permute-start(f32[12,128]{1,0:T(8,128)S(1)} %get-tuple-element.50.mine), channel_id=1, source_target_pairs={{0,1},{1,0},{2,3},{3,2},{4,5},{5,4},{6,7},{7,6},{8,9},{9,8},{10,11... | collective-permute-start | bytes 18440 | tf_op jit(solution)/shard_map/ppermute | solution.py:535

commit v6 on v5

--- a/solution.py
+++ b/solution.py
@@ -210,7 +210,7 @@
         whitened[number % windows][number // windows] = block
 
 
-def select_kernel(stations, place, rows, *refs):
+def select_kernel(stations, place, early, rows, *refs):
     windows = len(refs) // 2
     used = used_stations(rows[1:2], place[0] * stations, stations)
     weight = jnp.left_shift(1, lax.broadcasted_iota(jnp.int32, (stations, 1), 0)).astype(F32)
@@ -461,15 +461,16 @@
         ],
     )(far(spectra), far(masks))
     block = struct((NEAR, parts * seg, freq), BF16)
-    def select(wanted):
+    def select(wanted, early):
         return call(
             functools.partial(select_kernel, stations),
             [block] * windows,
-            [SMEM] + [VMEM] * (1 + windows),
+            [SMEM] + [VMEM] * (2 + windows),
             [VMEM] * windows,
-        )(place, wanted, *whitened)
-
-    to_next, to_last = select(after), select(before)
+        )(place, early, wanted, *whitened)
+
+    to_next = select(after, whitened[0])
+    to_last = select(before, to_next[0])
     lows = [lax.ppermute(one, "pairs", forward) for one in to_next]
     highs = [lax.ppermute(one, "pairs", backward) for one in to_last]
     table, ends = kernel_table(freq, lags)

time: 36.9 us -> 36.7 us (level)
  waiting for transfers between devices: 9.47 us -> 7.37 us
  starting transfers between devices: 14.8 us -> 16.6 us
    ppermute x2, waiting for transfers between devices: 3.07 us -> 0.36 us  [on_device(): lows = [lax.ppermute(one, 'pairs', forward) for one in to_next]]
    ppermute x2, starting transfers between devices: 0.12 us -> 1.44 us  [on_device(): lows = [lax.ppermute(one, 'pairs', forward) for one in to_next]]
    ppermute x2, waiting for transfers between devices: 0.01 us -> 0.61 us  [on_device(): highs = [lax.ppermute(one, 'pairs', backward) for one in to_last]]
    ppermute x2, starting transfers between devices: 5.77 us -> 6.31 us  [on_device(): highs = [lax.ppermute(one, 'pairs', backward) for one in to_last]]
  transfers between devices with their start and end apart: 11 -> 11, of which waited for: 7 -> 8; matrix products, arithmetic and copies ran while one was open for 2% -> 2% of each run, Pallas kernels for 20% -> 20%
where the time goes in v6:
time: 36.7 us; the launch traced here: 36.5 us
  starting transfers between devices  16.6 us (45%)
  Pallas kernels  10.9 us (30%)
  waiting for transfers between devices  7.37 us (20%)
  local copies, waits for them, and re-layouts  0.83 us (2%)
  between operations  0.74 us (2%)
    ppermute x5, waiting for transfers between devices, on_device(): lax.ppermute(value, 'hours', [(k, k ^ step) for k in range(slices)])  6.39 us
    ppermute x2, starting transfers between devices, on_device(): highs = [lax.ppermute(one, 'pairs', backward) for one in to_last]  6.31 us
    pallas_call x2, Pallas kernels, on_device(): call(functools.partial(window_kernel, sizes), outs, specs, [VMEM] * len(o...  5.23 us
    ppermute x5, starting transfers between devices, on_device(): lax.ppermute(value, 'hours', [(k, k ^ step) for k in range(slices)])  3.69 us
    ppermute x1, starting transfers between devices, on_device(): before = lax.ppermute(rows, 'pairs', forward)  3.08 us
    pallas_call x1, Pallas kernels, on_device(): call(functools.partial(stage_kernel, groups, stations), [struct(one.shape...  2.35 us
    ppermute x1, starting transfers between devices, on_device(): after = lax.ppermute(rows, 'pairs', backward)  2.09 us
    pallas_call x1, Pallas kernels, on_device(): call(whiten_kernel, [struct((stations, parts * seg, freq), BF16)] * windo...  1.86 us
  transfers between devices with their start and end apart: 11, of which 8 were waited for; matrix products, arithmetic and copies ran while one was open for 2% of the time, Pallas kernels for 20%

profile of v6, /device:TPU:0, one launch (start us, length us, event | category | flops | bytes accessed | tf_op | source)
XLA Modules:
  0.0 36.5 jit_solution(7369562838099668774)
XLA Ops:
  0.6 3.1 %collective-permute-start.2 = (s32[2,12]{1,0:T(2,128)}, s32[2,12]{1,0:T(2,128)S(1)}, u32[]{:S(2)}, u32[]{:S(2)}) collective-permute-start(s32[2,12]{1,0:T(2,128)} %bitcast.8), channel_id=1, source_target_pairs={{0,8},{8,16},{16,24},{24,0},{1,9},{9,17},{17,25},{25,1},{2,10},{10... | collective-permute-start | bytes 296 | tf_op jit(solution)/shard_map/ppermute | solution.py:449
  3.7 2.1 %collective-permute-start = (s32[2,12]{1,0:T(2,128)}, s32[2,12]{1,0:T(2,128)S(1)}, u32[]{:S(2)}, u32[]{:S(2)}) collective-permute-start(s32[2,12]{1,0:T(2,128)} %bitcast.9), channel_id=1, source_target_pairs={{8,0},{16,8},{24,16},{0,24},{9,1},{17,9},{25,17},{1,25},{10,2},{18... | collective-permute-start | bytes 296 | tf_op jit(solution)/shard_map/ppermute | solution.py:450
  5.8 1.9 %shard_map.103 = (bf16[8,16,1024]{2,1,0:T(8,128)(2,1)S(1)}, bf16[8,16,1024]{2,1,0:T(8,128)(2,1)S(1)}) custom-call(bf16[8,2,8,2,1024]{4,3,2,1,0:T(2,128)(2,1)} %far_spectra.1, s32[8,2,8]{2,1,0:T(2,128)} %far_masks.1), custom_call_target="tpu_custom_call" | custom-call | tf_op jit(solution)/shard_map/pallas_call | solution.py:452
  7.7 0.0 collective-permute-done.rows
  7.7 0.3 shard_map.104
  7.9 1.4 %collective-permute-start.1 = (bf16[4,16,1024]{2,1,0:T(8,128)(2,1)S(1)}, bf16[4,16,1024]{2,1,0:T(8,128)(2,1)S(1)}, u32[]{:S(2)}, u32[]{:S(2)}) collective-permute-start(bf16[4,16,1024]{2,1,0:T(8,128)(2,1)S(1)} %get-tuple-element.30.early), channel_id=1, source_target_pairs={{0,8},{8,16},{16,24},{24,0},{1,9},{9,17},{17,25},{25,1},{2,10},{10... | collective-permute-start | bytes 393224 | tf_op jit(solution)/shard_map/ppermute | solution.py:474
  9.4 0.0 collective-permute-done.2.rows
  9.4 0.3 shard_map.106
  9.6 2.5 %collective-permute-start.3 = (bf16[4,16,1024]{2,1,0:T(8,128)(2,1)S(1)}, bf16[4,16,1024]{2,1,0:T(8,128)(2,1)S(1)}, u32[]{:S(2)}, u32[]{:S(2)}) collective-permute-start(bf16[4,16,1024]{2,1,0:T(8,128)(2,1)S(1)} %get-tuple-element.32), channel_id=1, source_target_pairs={{8,0},{16,8},{24,16},{0,24},{9,1},{17,9},{25,17},{1,25},{10,2},{18... | collective-permute-start | bytes 393224 | tf_op jit(solution)/shard_map/ppermute | solution.py:475
  12.1 0.0 collective-permute-start.4
  12.1 3.8 %collective-permute-start.5 = (bf16[4,16,1024]{2,1,0:T(8,128)(2,1)S(1)}, bf16[4,16,1024]{2,1,0:T(8,128)(2,1)S(1)}, u32[]{:S(2)}, u32[]{:S(2)}) collective-permute-start(bf16[4,16,1024]{2,1,0:T(8,128)(2,1)S(1)} %get-tuple-element.40), channel_id=1, source_target_pairs={{8,0},{16,8},{24,16},{0,24},{9,1},{17,9},{25,17},{1,25},{10,2},{18... | collective-permute-start | bytes 393224 | tf_op jit(solution)/shard_map/ppermute | solution.py:475
  16.0 2.3 %shard_map.105 = (f32[4,2048]{1,0:T(4,128)S(1)}, bf16[2048,1024]{1,0:T(8,128)(2,1)S(1)}, f32[2,1024]{1,0:T(2,128)S(1)}, bf16[128,256]{1,0:T(8,128)(2,1)S(1)}, bf...) custom-call(s32[1]{0:T(128)} %bitcast.place, bf16[4,16,1024]{2,1,0:T(8,128)(2,1)S(1)} %get-tuple-element.30.early, ...), custom_call_target="tpu_custom_call" | custom-call | bytes 4194304 | tf_op jit(solution)/shard_map/pallas_call | solution.py:484
  18.3 0.0 collective-permute-done.1.low
  18.3 0.6 %collective-permute-done.3.high = bf16[4,16,1024]{2,1,0:T(8,128)(2,1)S(1)} collective-permute-done((bf16[4,16,1024]{2,1,0:T(8,128)(2,1)S(1)}, bf16[4,16,1024]{2,1,0:T(8,128)(2,1)S(1)}, u32[]{:S(2)}, u32[]{:S(2)}) %collective-permute-start.3) | collective-permute-done | bytes 131104 | tf_op jit(solution)/shard_map/ppermute | solution.py:475
  18.9 2.6 %shard_map.107 = (f32[12,2048]{1,0:T(8,128)S(1)}, f32[64,2048]{1,0:T(8,128)S(1)}) custom-call(s32[2,12]{1,0:T(2,128)S(1)} %get-tuple-element.31.index, bf16[8,16,1024]{2,1,0:T(8,128)(2,1)S(1)} %get-tuple-element.28.early.refs_0_.own, bf16[4,16,1024]{2,1,0:T(8,128)(2,1)S(1)} %collective-permute-done.1.low, ...), custom_call_target="tpu_custom_call" | custom-call | flops 402653184 | bytes 4194304 | tf_op jit(solution)/shard_map/pallas_call | solution.py:521
  21.5 0.4 collective-permute-done.4.low
  21.8 0.1 collective-permute-done.5.high
  21.9 2.7 %shard_map.108 = (f32[12,2048]{1,0:T(8,128)S(1)}, bf16[4,64,256]{2,1,0:T(8,128)(2,1)S(1)}, f32[4,64,256]{2,1,0:T(8,128)S(1)}) custom-call(s32[2,12]{1,0:T(2,128)S(1)} %get-tuple-element.31.index, bf16[8,16,1024]{2,1,0:T(8,128)(2,1)S(1)} %get-tuple-element.29.refs_1_.own, bf16[4,16,1024]{2,1,0:T(8,128)(2,1)S(1)} %collective-permute-done.4.low, ...), custom_call_target="tpu_custom_call" | custom-call | flops 402653184 | bytes 4194304 | tf_op jit(solution)/shard_map/pallas_call | solution.py:521
  24.5 0.1 collective-permute-start.6
  24.6 1.3 %collective-permute-done.6.got = bf16[4,64,256]{2,1,0:T(8,128)(2,1)S(1)} collective-permute-done((bf16[4,64,256]{2,1,0:T(8,128)(2,1)S(1)}, bf16[4,64,256]{2,1,0:T(8,128)(2,1)S(1)}, u32[]{:S(2)}, u32[]{:S(2)}) %collective-permute-start.6) | collective-permute-done | bytes 131104 | tf_op jit(solution)/shard_map/ppermute | solution.py:536
  26.0 2.5 %collective-permute-start.7 = (bf16[208,256]{1,0:T(8,128)(2,1)S(1)}, bf16[208,256]{1,0:T(8,128)(2,1)S(1)}, u32[]{:S(2)}, u32[]{:S(2)}) collective-permute-start(bf16[208,256]{1,0:T(8,128)(2,1)S(1)} %get-tuple-element.46), channel_id=1, source_target_pairs={{0,6},{1,7},{2,4},{3,5},{4,2},{5,3},{6,0},{7,1},{8,14},{9,15},{10,... | collective-permute-start | bytes 319496 | tf_op jit(solution)/shard_map/ppermute | solution.py:536
  28.5 0.5 %collective-permute-start.8 = (bf16[208,256]{1,0:T(8,128)(2,1)S(1)}, bf16[208,256]{1,0:T(8,128)(2,1)S(1)}, u32[]{:S(2)}, u32[]{:S(2)}) collective-permute-start(bf16[208,256]{1,0:T(8,128)(2,1)S(1)} %get-tuple-element.47), channel_id=1, source_target_pairs={{0,4},{1,5},{2,6},{3,7},{4,0},{5,1},{6,2},{7,3},{8,12},{9,13},{10,... | collective-permute-start | bytes 319496 | tf_op jit(solution)/shard_map/ppermute | solution.py:536
  29.0 0.5 %collective-permute-start.9 = (bf16[208,256]{1,0:T(8,128)(2,1)S(1)}, bf16[208,256]{1,0:T(8,128)(2,1)S(1)}, u32[]{:S(2)}, u32[]{:S(2)}) collective-permute-start(bf16[208,256]{1,0:T(8,128)(2,1)S(1)} %get-tuple-element.48), channel_id=1, source_target_pairs={{0,2},{1,3},{2,0},{3,1},{4,6},{5,7},{6,4},{7,5},{8,10},{9,11},{10,... | collective-permute-start | bytes 319496 | tf_op jit(solution)/shard_map/ppermute | solution.py:536
  29.6 2.5 %collective-permute-done.7.refs_0_ = bf16[208,256]{1,0:T(8,128)(2,1)S(1)} collective-permute-done((bf16[208,256]{1,0:T(8,128)(2,1)S(1)}, bf16[208,256]{1,0:T(8,128)(2,1)S(1)}, u32[]{:S(2)}, u32[]{:S(2)}) %collective-permute-start.7) | collective-permute-done | bytes 106528 | tf_op jit(solution)/shard_map/ppermute | solution.py:536
  32.1 2.2 %collective-permute-done.8.refs_1_ = bf16[208,256]{1,0:T(8,128)(2,1)S(1)} collective-permute-done((bf16[208,256]{1,0:T(8,128)(2,1)S(1)}, bf16[208,256]{1,0:T(8,128)(2,1)S(1)}, u32[]{:S(2)}, u32[]{:S(2)}) %collective-permute-start.8) | collective-permute-done | bytes 106528 | tf_op jit(solution)/shard_map/ppermute | solution.py:536
  34.3 0.1 collective-permute-done.9.refs_2_
  34.3 0.2 shard_map.110
  34.5 0.1 collective-permute-start.10
  34.6 0.8 %copy.11 = f32[12,2,2048]{2,1,0:T(2,128)} copy(f32[12,2,2048]{2,0,1:T(8,128)S(1)} %pad_maximum_fusion) | data formatting | bytes 393216
  35.4 0.3 collective-permute-done.10.got
  35.7 0.7 %shard_map.111 = (f32[12,256]{1,0:T(8,128)}, f32[12,4,256]{2,1,0:T(4,128)}) custom-call(f32[64,256]{1,0:T(8,128)S(1)} %get-tuple-element.49.total, f32[12,128]{1,0:T(8,128)S(1)} %get-tuple-element.50.mine, f32[12,128]{1,0:T(8,128)S(1)} %collective-permute-done.10.got), custom_call_target="tpu_custom_call" | custom-call | tf_op jit(solution)/shard_map/pallas_call | solution.py:554
  (2 shorter events, 0.1 us)
Async XLA Ops:
  0.6 8.7 %collective-permute-start.2 = (s32[2,12]{1,0:T(2,128)}, s32[2,12]{1,0:T(2,128)S(1)}, u32[]{:S(2)}, u32[]{:S(2)}) collective-permute-start(s32[2,12]{1,0:T(2,128)} %bitcast.8), channel_id=1, source_target_pairs={{0,8},{8,16},{16,24},{24,0},{1,9},{9,17},{17,25},{25,1},{2,10},{10... | collective-permute-start | bytes 296 | tf_op jit(solution)/shard_map/ppermute | solution.py:449
  3.7 4.0 %collective-permute-start = (s32[2,12]{1,0:T(2,128)}, s32[2,12]{1,0:T(2,128)S(1)}, u32[]{:S(2)}, u32[]{:S(2)}) collective-permute-start(s32[2,12]{1,0:T(2,128)} %bitcast.9), channel_id=1, source_target_pairs={{8,0},{16,8},{24,16},{0,24},{9,1},{17,9},{25,17},{1,25},{10,2},{18... | collective-permute-start | bytes 296 | tf_op jit(solution)/shard_map/ppermute | solution.py:450
  7.9 10.4 %collective-permute-start.1 = (bf16[4,16,1024]{2,1,0:T(8,128)(2,1)S(1)}, bf16[4,16,1024]{2,1,0:T(8,128)(2,1)S(1)}, u32[]{:S(2)}, u32[]{:S(2)}) collective-permute-start(bf16[4,16,1024]{2,1,0:T(8,128)(2,1)S(1)} %get-tuple-element.30.early), channel_id=1, source_target_pairs={{0,8},{8,16},{16,24},{24,0},{1,9},{9,17},{17,25},{25,1},{2,10},{10... | collective-permute-start | bytes 393224 | tf_op jit(solution)/shard_map/ppermute | solution.py:474
  9.6 9.2 %collective-permute-start.3 = (bf16[4,16,1024]{2,1,0:T(8,128)(2,1)S(1)}, bf16[4,16,1024]{2,1,0:T(8,128)(2,1)S(1)}, u32[]{:S(2)}, u32[]{:S(2)}) collective-permute-start(bf16[4,16,1024]{2,1,0:T(8,128)(2,1)S(1)} %get-tuple-element.32), channel_id=1, source_target_pairs={{8,0},{16,8},{24,16},{0,24},{9,1},{17,9},{25,17},{1,25},{10,2},{18... | collective-permute-start | bytes 393224 | tf_op jit(solution)/shard_map/ppermute | solution.py:475
  12.1 9.7 %collective-permute-start.4 = (bf16[4,16,1024]{2,1,0:T(8,128)(2,1)S(1)}, bf16[4,16,1024]{2,1,0:T(8,128)(2,1)S(1)}, u32[]{:S(2)}, u32[]{:S(2)}) collective-permute-start(bf16[4,16,1024]{2,1,0:T(8,128)(2,1)S(1)} %get-tuple-element.39), channel_id=1, source_target_pairs={{0,8},{8,16},{16,24},{24,0},{1,9},{9,17},{17,25},{25,1},{2,10},{10... | collective-permute-start | bytes 393224 | tf_op jit(solution)/shard_map/ppermute | solution.py:474
  12.1 9.7 %collective-permute-start.5 = (bf16[4,16,1024]{2,1,0:T(8,128)(2,1)S(1)}, bf16[4,16,1024]{2,1,0:T(8,128)(2,1)S(1)}, u32[]{:S(2)}, u32[]{:S(2)}) collective-permute-start(bf16[4,16,1024]{2,1,0:T(8,128)(2,1)S(1)} %get-tuple-element.40), channel_id=1, source_target_pairs={{8,0},{16,8},{24,16},{0,24},{9,1},{17,9},{25,17},{1,25},{10,2},{18... | collective-permute-start | bytes 393224 | tf_op jit(solution)/shard_map/ppermute | solution.py:475
  24.5 1.4 %collective-permute-start.6 = (bf16[4,64,256]{2,1,0:T(8,128)(2,1)S(1)}, bf16[4,64,256]{2,1,0:T(8,128)(2,1)S(1)}, u32[]{:S(2)}, u32[]{:S(2)}) collective-permute-start(bf16[4,64,256]{2,1,0:T(8,128)(2,1)S(1)} %get-tuple-element.44), channel_id=1, source_target_pairs={{0,1},{1,0},{2,3},{3,2},{4,5},{5,4},{6,7},{7,6},{8,9},{9,8},{10,11... | collective-permute-start | bytes 393224 | tf_op jit(solution)/shard_map/ppermute | solution.py:536
  26.0 6.1 %collective-permute-start.7 = (bf16[208,256]{1,0:T(8,128)(2,1)S(1)}, bf16[208,256]{1,0:T(8,128)(2,1)S(1)}, u32[]{:S(2)}, u32[]{:S(2)}) collective-permute-start(bf16[208,256]{1,0:T(8,128)(2,1)S(1)} %get-tuple-element.46), channel_id=1, source_target_pairs={{0,6},{1,7},{2,4},{3,5},{4,2},{5,3},{6,0},{7,1},{8,14},{9,15},{10,... | collective-permute-start | bytes 319496 | tf_op jit(solution)/shard_map/ppermute | solution.py:536
  28.5 5.8 %collective-permute-start.8 = (bf16[208,256]{1,0:T(8,128)(2,1)S(1)}, bf16[208,256]{1,0:T(8,128)(2,1)S(1)}, u32[]{:S(2)}, u32[]{:S(2)}) collective-permute-start(bf16[208,256]{1,0:T(8,128)(2,1)S(1)} %get-tuple-element.47), channel_id=1, source_target_pairs={{0,4},{1,5},{2,6},{3,7},{4,0},{5,1},{6,2},{7,3},{8,12},{9,13},{10,... | collective-permute-start | bytes 319496 | tf_op jit(solution)/shard_map/ppermute | solution.py:536
  29.0 5.3 %collective-permute-start.9 = (bf16[208,256]{1,0:T(8,128)(2,1)S(1)}, bf16[208,256]{1,0:T(8,128)(2,1)S(1)}, u32[]{:S(2)}, u32[]{:S(2)}) collective-permute-start(bf16[208,256]{1,0:T(8,128)(2,1)S(1)} %get-tuple-element.48), channel_id=1, source_target_pairs={{0,2},{1,3},{2,0},{3,1},{4,6},{5,7},{6,4},{7,5},{8,10},{9,11},{10,... | collective-permute-start | bytes 319496 | tf_op jit(solution)/shard_map/ppermute | solution.py:536
  34.5 1.2 %collective-permute-start.10 = (f32[12,128]{1,0:T(8,128)S(1)}, f32[12,128]{1,0:T(8,128)S(1)}, u32[]{:S(2)}, u32[]{:S(2)}) collective-permute-start(f32[12,128]{1,0:T(8,128)S(1)} %get-tuple-element.50.mine), channel_id=1, source_target_pairs={{0,1},{1,0},{2,3},{3,2},{4,5},{5,4},{6,7},{7,6},{8,9},{9,8},{10,11... | collective-permute-start | bytes 18440 | tf_op jit(solution)/shard_map/ppermute | solution.py:536

commit v7 on v6

--- a/solution.py
+++ b/solution.py
@@ -261,8 +261,11 @@
     vectors[rows + rank :] = jnp.zeros((HEAD - rows - rank, lags), F32)
     step = 512
     for at in range(0, half, step):
-        vectors[0:rows, at : at + step] = dot(cross[:, 0:freq], table[0:freq, at : at + step])
-        vectors[0:rows, half + at : half + at + step] = dot(cross[:, freq:], table[freq:, at : at + step])
+        for part in (0, 1):
+            block = cross[:, part * freq : (part + 1) * freq]
+            block = jnp.concatenate([block, block[0 : HEAD - rows]], 0)
+            block = dot(block, table[part * freq : (part + 1) * freq, at : at + step])
+            vectors[0:rows, part * half + at : part * half + at + step] = block[0:rows]
     shape = (rows, 128)
     root = math.sqrt(0.5)
     column = vectors[0:rows, 0:128]

time: 36.7 us -> 36.6 us (level)
  no operation moved by 1% of the time
where the time goes in v7:
time: 36.6 us; the launch traced here: 36.4 us
  starting transfers between devices  16.6 us (45%)
  Pallas kernels  10.7 us (29%)
  waiting for transfers between devices  7.48 us (20%)
  local copies, waits for them, and re-layouts  0.83 us (2%)
  between operations  0.74 us (2%)
    ppermute x5, waiting for transfers between devices, on_device(): lax.ppermute(value, 'hours', [(k, k ^ step) for k in range(slices)])  6.39 us
    ppermute x2, starting transfers between devices, on_device(): highs = [lax.ppermute(one, 'pairs', backward) for one in to_last]  6.31 us
    pallas_call x2, Pallas kernels, on_device(): call(functools.partial(window_kernel, sizes), outs, specs, [VMEM] * len(o...  5 us
    ppermute x5, starting transfers between devices, on_device(): lax.ppermute(value, 'hours', [(k, k ^ step) for k in range(slices)])  3.69 us
    ppermute x1, starting transfers between devices, on_device(): before = lax.ppermute(rows, 'pairs', forward)  3.08 us
    pallas_call x1, Pallas kernels, on_device(): call(functools.partial(stage_kernel, groups, stations), [struct(one.shape...  2.35 us
    ppermute x1, starting transfers between devices, on_device(): after = lax.ppermute(rows, 'pairs', backward)  2.09 us
    pallas_call x1, Pallas kernels, on_device(): call(whiten_kernel, [struct((stations, parts * seg, freq), BF16)] * windo...  1.86 us
  transfers between devices with their start and end apart: 11, of which 8 were waited for; matrix products, arithmetic and copies ran while one was open for 2% of the time, Pallas kernels for 20%

profile of v7, /device:TPU:0, one launch (start us, length us, event | category | flops | bytes accessed | tf_op | source)
XLA Modules:
  0.0 36.4 jit_solution(9560854392712852059)
XLA Ops:
  0.6 3.1 %collective-permute-start.2 = (s32[2,12]{1,0:T(2,128)}, s32[2,12]{1,0:T(2,128)S(1)}, u32[]{:S(2)}, u32[]{:S(2)}) collective-permute-start(s32[2,12]{1,0:T(2,128)} %bitcast.8), channel_id=1, source_target_pairs={{0,8},{8,16},{16,24},{24,0},{1,9},{9,17},{17,25},{25,1},{2,10},{10... | collective-permute-start | bytes 296 | tf_op jit(solution)/shard_map/ppermute | solution.py:452
  3.7 2.1 %collective-permute-start = (s32[2,12]{1,0:T(2,128)}, s32[2,12]{1,0:T(2,128)S(1)}, u32[]{:S(2)}, u32[]{:S(2)}) collective-permute-start(s32[2,12]{1,0:T(2,128)} %bitcast.9), channel_id=1, source_target_pairs={{8,0},{16,8},{24,16},{0,24},{9,1},{17,9},{25,17},{1,25},{10,2},{18... | collective-permute-start | bytes 296 | tf_op jit(solution)/shard_map/ppermute | solution.py:453
  5.8 1.9 %shard_map.103 = (bf16[8,16,1024]{2,1,0:T(8,128)(2,1)S(1)}, bf16[8,16,1024]{2,1,0:T(8,128)(2,1)S(1)}) custom-call(bf16[8,2,8,2,1024]{4,3,2,1,0:T(2,128)(2,1)} %far_spectra.1, s32[8,2,8]{2,1,0:T(2,128)} %far_masks.1), custom_call_target="tpu_custom_call" | custom-call | tf_op jit(solution)/shard_map/pallas_call | solution.py:455
  7.7 0.0 collective-permute-done.rows
  7.7 0.3 shard_map.104
  7.9 1.4 %collective-permute-start.1 = (bf16[4,16,1024]{2,1,0:T(8,128)(2,1)S(1)}, bf16[4,16,1024]{2,1,0:T(8,128)(2,1)S(1)}, u32[]{:S(2)}, u32[]{:S(2)}) collective-permute-start(bf16[4,16,1024]{2,1,0:T(8,128)(2,1)S(1)} %get-tuple-element.30.early), channel_id=1, source_target_pairs={{0,8},{8,16},{16,24},{24,0},{1,9},{9,17},{17,25},{25,1},{2,10},{10... | collective-permute-start | bytes 393224 | tf_op jit(solution)/shard_map/ppermute | solution.py:477
  9.4 0.0 collective-permute-done.2.rows
  9.4 0.3 shard_map.106
  9.6 2.5 %collective-permute-start.3 = (bf16[4,16,1024]{2,1,0:T(8,128)(2,1)S(1)}, bf16[4,16,1024]{2,1,0:T(8,128)(2,1)S(1)}, u32[]{:S(2)}, u32[]{:S(2)}) collective-permute-start(bf16[4,16,1024]{2,1,0:T(8,128)(2,1)S(1)} %get-tuple-element.32), channel_id=1, source_target_pairs={{8,0},{16,8},{24,16},{0,24},{9,1},{17,9},{25,17},{1,25},{10,2},{18... | collective-permute-start | bytes 393224 | tf_op jit(solution)/shard_map/ppermute | solution.py:478
  12.1 0.0 collective-permute-start.4
  12.1 3.8 %collective-permute-start.5 = (bf16[4,16,1024]{2,1,0:T(8,128)(2,1)S(1)}, bf16[4,16,1024]{2,1,0:T(8,128)(2,1)S(1)}, u32[]{:S(2)}, u32[]{:S(2)}) collective-permute-start(bf16[4,16,1024]{2,1,0:T(8,128)(2,1)S(1)} %get-tuple-element.40), channel_id=1, source_target_pairs={{8,0},{16,8},{24,16},{0,24},{9,1},{17,9},{25,17},{1,25},{10,2},{18... | collective-permute-start | bytes 393224 | tf_op jit(solution)/shard_map/ppermute | solution.py:478
  16.0 2.3 %shard_map.105 = (f32[4,2048]{1,0:T(4,128)S(1)}, bf16[2048,1024]{1,0:T(8,128)(2,1)S(1)}, f32[2,1024]{1,0:T(2,128)S(1)}, bf16[128,256]{1,0:T(8,128)(2,1)S(1)}, bf...) custom-call(s32[1]{0:T(128)} %bitcast.place, bf16[4,16,1024]{2,1,0:T(8,128)(2,1)S(1)} %get-tuple-element.30.early, ...), custom_call_target="tpu_custom_call" | custom-call | bytes 4194304 | tf_op jit(solution)/shard_map/pallas_call | solution.py:487
  18.3 0.0 collective-permute-done.1.low
  18.3 0.6 %collective-permute-done.3.high = bf16[4,16,1024]{2,1,0:T(8,128)(2,1)S(1)} collective-permute-done((bf16[4,16,1024]{2,1,0:T(8,128)(2,1)S(1)}, bf16[4,16,1024]{2,1,0:T(8,128)(2,1)S(1)}, u32[]{:S(2)}, u32[]{:S(2)}) %collective-permute-start.3) | collective-permute-done | bytes 131104 | tf_op jit(solution)/shard_map/ppermute | solution.py:478
  18.9 2.5 %shard_map.107 = (f32[12,2048]{1,0:T(8,128)S(1)}, f32[64,2048]{1,0:T(8,128)S(1)}) custom-call(s32[2,12]{1,0:T(2,128)S(1)} %get-tuple-element.31.index, bf16[8,16,1024]{2,1,0:T(8,128)(2,1)S(1)} %get-tuple-element.28.early.refs_0_.own, bf16[4,16,1024]{2,1,0:T(8,128)(2,1)S(1)} %collective-permute-done.1.low, ...), custom_call_target="tpu_custom_call" | custom-call | flops 402653184 | bytes 4194304 | tf_op jit(solution)/shard_map/pallas_call | solution.py:524
  21.3 0.5 %collective-permute-done.4.low = bf16[4,16,1024]{2,1,0:T(8,128)(2,1)S(1)} collective-permute-done((bf16[4,16,1024]{2,1,0:T(8,128)(2,1)S(1)}, bf16[4,16,1024]{2,1,0:T(8,128)(2,1)S(1)}, u32[]{:S(2)}, u32[]{:S(2)}) %collective-permute-start.4) | collective-permute-done | bytes 131104 | tf_op jit(solution)/shard_map/ppermute | solution.py:477
  21.8 0.1 collective-permute-done.5.high
  21.9 2.5 %shard_map.108 = (f32[12,2048]{1,0:T(8,128)S(1)}, bf16[4,64,256]{2,1,0:T(8,128)(2,1)S(1)}, f32[4,64,256]{2,1,0:T(8,128)S(1)}) custom-call(s32[2,12]{1,0:T(2,128)S(1)} %get-tuple-element.31.index, bf16[8,16,1024]{2,1,0:T(8,128)(2,1)S(1)} %get-tuple-element.29.refs_1_.own, bf16[4,16,1024]{2,1,0:T(8,128)(2,1)S(1)} %collective-permute-done.4.low, ...), custom_call_target="tpu_custom_call" | custom-call | flops 402653184 | bytes 4194304 | tf_op jit(solution)/shard_map/pallas_call | solution.py:524
  24.4 0.1 collective-permute-start.6
  24.5 1.3 %collective-permute-done.6.got = bf16[4,64,256]{2,1,0:T(8,128)(2,1)S(1)} collective-permute-done((bf16[4,64,256]{2,1,0:T(8,128)(2,1)S(1)}, bf16[4,64,256]{2,1,0:T(8,128)(2,1)S(1)}, u32[]{:S(2)}, u32[]{:S(2)}) %collective-permute-start.6) | collective-permute-done | bytes 131104 | tf_op jit(solution)/shard_map/ppermute | solution.py:539
  25.9 2.5 %collective-permute-start.7 = (bf16[208,256]{1,0:T(8,128)(2,1)S(1)}, bf16[208,256]{1,0:T(8,128)(2,1)S(1)}, u32[]{:S(2)}, u32[]{:S(2)}) collective-permute-start(bf16[208,256]{1,0:T(8,128)(2,1)S(1)} %get-tuple-element.46), channel_id=1, source_target_pairs={{0,6},{1,7},{2,4},{3,5},{4,2},{5,3},{6,0},{7,1},{8,14},{9,15},{10,... | collective-permute-start | bytes 319496 | tf_op jit(solution)/shard_map/ppermute | solution.py:539
  28.4 0.5 %collective-permute-start.8 = (bf16[208,256]{1,0:T(8,128)(2,1)S(1)}, bf16[208,256]{1,0:T(8,128)(2,1)S(1)}, u32[]{:S(2)}, u32[]{:S(2)}) collective-permute-start(bf16[208,256]{1,0:T(8,128)(2,1)S(1)} %get-tuple-element.47), channel_id=1, source_target_pairs={{0,4},{1,5},{2,6},{3,7},{4,0},{5,1},{6,2},{7,3},{8,12},{9,13},{10,... | collective-permute-start | bytes 319496 | tf_op jit(solution)/shard_map/ppermute | solution.py:539
  28.9 0.5 %collective-permute-start.9 = (bf16[208,256]{1,0:T(8,128)(2,1)S(1)}, bf16[208,256]{1,0:T(8,128)(2,1)S(1)}, u32[]{:S(2)}, u32[]{:S(2)}) collective-permute-start(bf16[208,256]{1,0:T(8,128)(2,1)S(1)} %get-tuple-element.48), channel_id=1, source_target_pairs={{0,2},{1,3},{2,0},{3,1},{4,6},{5,7},{6,4},{7,5},{8,10},{9,11},{10,... | collective-permute-start | bytes 319496 | tf_op jit(solution)/shard_map/ppermute | solution.py:539
  29.4 2.5 %collective-permute-done.7.refs_0_ = bf16[208,256]{1,0:T(8,128)(2,1)S(1)} collective-permute-done((bf16[208,256]{1,0:T(8,128)(2,1)S(1)}, bf16[208,256]{1,0:T(8,128)(2,1)S(1)}, u32[]{:S(2)}, u32[]{:S(2)}) %collective-permute-start.7) | collective-permute-done | bytes 106528 | tf_op jit(solution)/shard_map/ppermute | solution.py:539
  32.0 2.2 %collective-permute-done.8.refs_1_ = bf16[208,256]{1,0:T(8,128)(2,1)S(1)} collective-permute-done((bf16[208,256]{1,0:T(8,128)(2,1)S(1)}, bf16[208,256]{1,0:T(8,128)(2,1)S(1)}, u32[]{:S(2)}, u32[]{:S(2)}) %collective-permute-start.8) | collective-permute-done | bytes 106528 | tf_op jit(solution)/shard_map/ppermute | solution.py:539
  34.2 0.1 collective-permute-done.9.refs_2_
  34.2 0.2 shard_map.110
  34.4 0.1 collective-permute-start.10
  34.5 0.8 %copy.11 = f32[12,2,2048]{2,1,0:T(2,128)} copy(f32[12,2,2048]{2,0,1:T(8,128)S(1)} %pad_maximum_fusion) | data formatting | bytes 393216
  35.3 0.3 collective-permute-done.10.got
  35.6 0.7 %shard_map.111 = (f32[12,256]{1,0:T(8,128)}, f32[12,4,256]{2,1,0:T(4,128)}) custom-call(f32[64,256]{1,0:T(8,128)S(1)} %get-tuple-element.49.total, f32[12,128]{1,0:T(8,128)S(1)} %get-tuple-element.50.mine, f32[12,128]{1,0:T(8,128)S(1)} %collective-permute-done.10.got), custom_call_target="tpu_custom_call" | custom-call | tf_op jit(solution)/shard_map/pallas_call | solution.py:557
  (2 shorter events, 0.1 us)
Async XLA Ops:
  0.6 8.7 %collective-permute-start.2 = (s32[2,12]{1,0:T(2,128)}, s32[2,12]{1,0:T(2,128)S(1)}, u32[]{:S(2)}, u32[]{:S(2)}) collective-permute-start(s32[2,12]{1,0:T(2,128)} %bitcast.8), channel_id=1, source_target_pairs={{0,8},{8,16},{16,24},{24,0},{1,9},{9,17},{17,25},{25,1},{2,10},{10... | collective-permute-start | bytes 296 | tf_op jit(solution)/shard_map/ppermute | solution.py:452
  3.7 4.0 %collective-permute-start = (s32[2,12]{1,0:T(2,128)}, s32[2,12]{1,0:T(2,128)S(1)}, u32[]{:S(2)}, u32[]{:S(2)}) collective-permute-start(s32[2,12]{1,0:T(2,128)} %bitcast.9), channel_id=1, source_target_pairs={{8,0},{16,8},{24,16},{0,24},{9,1},{17,9},{25,17},{1,25},{10,2},{18... | collective-permute-start | bytes 296 | tf_op jit(solution)/shard_map/ppermute | solution.py:453
  7.9 10.4 %collective-permute-start.1 = (bf16[4,16,1024]{2,1,0:T(8,128)(2,1)S(1)}, bf16[4,16,1024]{2,1,0:T(8,128)(2,1)S(1)}, u32[]{:S(2)}, u32[]{:S(2)}) collective-permute-start(bf16[4,16,1024]{2,1,0:T(8,128)(2,1)S(1)} %get-tuple-element.30.early), channel_id=1, source_target_pairs={{0,8},{8,16},{16,24},{24,0},{1,9},{9,17},{17,25},{25,1},{2,10},{10... | collective-permute-start | bytes 393224 | tf_op jit(solution)/shard_map/ppermute | solution.py:477
  9.6 9.2 %collective-permute-start.3 = (bf16[4,16,1024]{2,1,0:T(8,128)(2,1)S(1)}, bf16[4,16,1024]{2,1,0:T(8,128)(2,1)S(1)}, u32[]{:S(2)}, u32[]{:S(2)}) collective-permute-start(bf16[4,16,1024]{2,1,0:T(8,128)(2,1)S(1)} %get-tuple-element.32), channel_id=1, source_target_pairs={{8,0},{16,8},{24,16},{0,24},{9,1},{17,9},{25,17},{1,25},{10,2},{18... | collective-permute-start | bytes 393224 | tf_op jit(solution)/shard_map/ppermute | solution.py:478
  12.1 9.7 %collective-permute-start.4 = (bf16[4,16,1024]{2,1,0:T(8,128)(2,1)S(1)}, bf16[4,16,1024]{2,1,0:T(8,128)(2,1)S(1)}, u32[]{:S(2)}, u32[]{:S(2)}) collective-permute-start(bf16[4,16,1024]{2,1,0:T(8,128)(2,1)S(1)} %get-tuple-element.39), channel_id=1, source_target_pairs={{0,8},{8,16},{16,24},{24,0},{1,9},{9,17},{17,25},{25,1},{2,10},{10... | collective-permute-start | bytes 393224 | tf_op jit(solution)/shard_map/ppermute | solution.py:477
  12.1 9.7 %collective-permute-start.5 = (bf16[4,16,1024]{2,1,0:T(8,128)(2,1)S(1)}, bf16[4,16,1024]{2,1,0:T(8,128)(2,1)S(1)}, u32[]{:S(2)}, u32[]{:S(2)}) collective-permute-start(bf16[4,16,1024]{2,1,0:T(8,128)(2,1)S(1)} %get-tuple-element.40), channel_id=1, source_target_pairs={{8,0},{16,8},{24,16},{0,24},{9,1},{17,9},{25,17},{1,25},{10,2},{18... | collective-permute-start | bytes 393224 | tf_op jit(solution)/shard_map/ppermute | solution.py:478
  24.4 1.4 %collective-permute-start.6 = (bf16[4,64,256]{2,1,0:T(8,128)(2,1)S(1)}, bf16[4,64,256]{2,1,0:T(8,128)(2,1)S(1)}, u32[]{:S(2)}, u32[]{:S(2)}) collective-permute-start(bf16[4,64,256]{2,1,0:T(8,128)(2,1)S(1)} %get-tuple-element.44), channel_id=1, source_target_pairs={{0,1},{1,0},{2,3},{3,2},{4,5},{5,4},{6,7},{7,6},{8,9},{9,8},{10,11... | collective-permute-start | bytes 393224 | tf_op jit(solution)/shard_map/ppermute | solution.py:539
  25.9 6.1 %collective-permute-start.7 = (bf16[208,256]{1,0:T(8,128)(2,1)S(1)}, bf16[208,256]{1,0:T(8,128)(2,1)S(1)}, u32[]{:S(2)}, u32[]{:S(2)}) collective-permute-start(bf16[208,256]{1,0:T(8,128)(2,1)S(1)} %get-tuple-element.46), channel_id=1, source_target_pairs={{0,6},{1,7},{2,4},{3,5},{4,2},{5,3},{6,0},{7,1},{8,14},{9,15},{10,... | collective-permute-start | bytes 319496 | tf_op jit(solution)/shard_map/ppermute | solution.py:539
  28.4 5.8 %collective-permute-start.8 = (bf16[208,256]{1,0:T(8,128)(2,1)S(1)}, bf16[208,256]{1,0:T(8,128)(2,1)S(1)}, u32[]{:S(2)}, u32[]{:S(2)}) collective-permute-start(bf16[208,256]{1,0:T(8,128)(2,1)S(1)} %get-tuple-element.47), channel_id=1, source_target_pairs={{0,4},{1,5},{2,6},{3,7},{4,0},{5,1},{6,2},{7,3},{8,12},{9,13},{10,... | collective-permute-start | bytes 319496 | tf_op jit(solution)/shard_map/ppermute | solution.py:539
  28.9 5.3 %collective-permute-start.9 = (bf16[208,256]{1,0:T(8,128)(2,1)S(1)}, bf16[208,256]{1,0:T(8,128)(2,1)S(1)}, u32[]{:S(2)}, u32[]{:S(2)}) collective-permute-start(bf16[208,256]{1,0:T(8,128)(2,1)S(1)} %get-tuple-element.48), channel_id=1, source_target_pairs={{0,2},{1,3},{2,0},{3,1},{4,6},{5,7},{6,4},{7,5},{8,10},{9,11},{10,... | collective-permute-start | bytes 319496 | tf_op jit(solution)/shard_map/ppermute | solution.py:539
  34.4 1.2 %collective-permute-start.10 = (f32[12,128]{1,0:T(8,128)S(1)}, f32[12,128]{1,0:T(8,128)S(1)}, u32[]{:S(2)}, u32[]{:S(2)}) collective-permute-start(f32[12,128]{1,0:T(8,128)S(1)} %get-tuple-element.50.mine), channel_id=1, source_target_pairs={{0,1},{1,0},{2,3},{3,2},{4,5},{5,4},{6,7},{7,6},{8,9},{9,8},{10,11... | collective-permute-start | bytes 18440 | tf_op jit(solution)/shard_map/ppermute | solution.py:539

commit v8 on v7

--- a/solution.py
+++ b/solution.py
@@ -234,7 +234,7 @@
     if first_window:
         win_out, merged_out, near, cross, vectors, high_part, low_part = refs
     else:
-        (core, partial, win_out, send_out, keep_out, near, cross, vectors, high_part, low_part, pieces) = refs
+        (core, partial, win_out, send_out, keep_out, near, cross, vectors, high_part, low_part) = refs
     stations = own.shape[0]
     half = lags // 2
     picked = index[...]
@@ -354,13 +354,12 @@
         merged_out[:, half:] = result[1]
     else:
         left, right = unfold(result[0] + partial[:, 0:half], result[1] + partial[:, half:])
+        swapped = core[0] == 1
         for piece in range(slices // 2):
-            pieces[piece] = left[:, piece * width : (piece + 1) * width]
-            pieces[slices // 2 + piece] = right[:, piece * width : (piece + 1) * width]
-    if not first_window:
-        for piece in range(slices // 2):
-            send_out[piece] = pieces[2 * piece + 1 - core[0]].astype(BF16)
-            keep_out[piece] = pieces[2 * piece + core[0]]
+            side, at = (left, right)[piece // (slices // 4)], 2 * piece * width % half
+            one, two = side[:, at : at + width], side[:, at + width : at + 2 * width]
+            send_out[piece] = jnp.where(swapped, one, two).astype(BF16)
+            keep_out[piece] = jnp.where(swapped, two, one)
 
 
 def add_kernel(top, chip, keep, got, mine_out, *sends):
@@ -520,7 +519,6 @@
             args += [core, partial]
             specs += [SMEM, VMEM]
             outs += [struct((chips, height, width), BF16), struct((chips, height, width))]
-            scratch.append(pltpu.VMEM((slices, height, width), F32))
         result = call(
             functools.partial(window_kernel, sizes),
             outs,

time: 36.6 us -> 36.5 us (level)
  no operation moved by 1% of the time
where the time goes in v8:
time: 36.5 us; the launch traced here: 36.3 us
  starting transfers between devices  16.6 us (45%)
  Pallas kernels  10.6 us (29%)
  waiting for transfers between devices  7.49 us (21%)
  local copies, waits for them, and re-layouts  0.83 us (2%)
  between operations  0.74 us (2%)
    ppermute x5, waiting for transfers between devices, on_device(): lax.ppermute(value, 'hours', [(k, k ^ step) for k in range(slices)])  6.39 us
    ppermute x2, starting transfers between devices, on_device(): highs = [lax.ppermute(one, 'pairs', backward) for one in to_last]  6.31 us
    pallas_call x2, Pallas kernels, on_device(): call(functools.partial(window_kernel, sizes), outs, specs, [VMEM] * len(o...  4.96 us
    ppermute x5, starting transfers between devices, on_device(): lax.ppermute(value, 'hours', [(k, k ^ step) for k in range(slices)])  3.69 us
    ppermute x1, starting transfers between devices, on_device(): before = lax.ppermute(rows, 'pairs', forward)  3.08 us
    pallas_call x1, Pallas kernels, on_device(): call(functools.partial(stage_kernel, groups, stations), [struct(one.shape...  2.35 us
    ppermute x1, starting transfers between devices, on_device(): after = lax.ppermute(rows, 'pairs', backward)  2.09 us
    pallas_call x1, Pallas kernels, on_device(): call(whiten_kernel, [struct((stations, parts * seg, freq), BF16)] * windo...  1.86 us
  transfers between devices with their start and end apart: 11, of which 8 were waited for; matrix products, arithmetic and copies ran while one was open for 2% of the time, Pallas kernels for 20%

profile of v8, /device:TPU:0, one launch (start us, length us, event | category | flops | bytes accessed | tf_op | source)
XLA Modules:
  0.0 36.3 jit_solution(4428325770889878553)
XLA Ops:
  0.6 3.1 %collective-permute-start.2 = (s32[2,12]{1,0:T(2,128)}, s32[2,12]{1,0:T(2,128)S(1)}, u32[]{:S(2)}, u32[]{:S(2)}) collective-permute-start(s32[2,12]{1,0:T(2,128)} %bitcast.8), channel_id=1, source_target_pairs={{0,8},{8,16},{16,24},{24,0},{1,9},{9,17},{17,25},{25,1},{2,10},{10... | collective-permute-start | bytes 296 | tf_op jit(solution)/shard_map/ppermute | solution.py:451
  3.7 2.1 %collective-permute-start = (s32[2,12]{1,0:T(2,128)}, s32[2,12]{1,0:T(2,128)S(1)}, u32[]{:S(2)}, u32[]{:S(2)}) collective-permute-start(s32[2,12]{1,0:T(2,128)} %bitcast.9), channel_id=1, source_target_pairs={{8,0},{16,8},{24,16},{0,24},{9,1},{17,9},{25,17},{1,25},{10,2},{18... | collective-permute-start | bytes 296 | tf_op jit(solution)/shard_map/ppermute | solution.py:452
  5.8 1.9 %shard_map.103 = (bf16[8,16,1024]{2,1,0:T(8,128)(2,1)S(1)}, bf16[8,16,1024]{2,1,0:T(8,128)(2,1)S(1)}) custom-call(bf16[8,2,8,2,1024]{4,3,2,1,0:T(2,128)(2,1)} %far_spectra.1, s32[8,2,8]{2,1,0:T(2,128)} %far_masks.1), custom_call_target="tpu_custom_call" | custom-call | tf_op jit(solution)/shard_map/pallas_call | solution.py:454
  7.7 0.0 collective-permute-done.rows
  7.7 0.3 shard_map.104
  7.9 1.4 %collective-permute-start.1 = (bf16[4,16,1024]{2,1,0:T(8,128)(2,1)S(1)}, bf16[4,16,1024]{2,1,0:T(8,128)(2,1)S(1)}, u32[]{:S(2)}, u32[]{:S(2)}) collective-permute-start(bf16[4,16,1024]{2,1,0:T(8,128)(2,1)S(1)} %get-tuple-element.30.early), channel_id=1, source_target_pairs={{0,8},{8,16},{16,24},{24,0},{1,9},{9,17},{17,25},{25,1},{2,10},{10... | collective-permute-start | bytes 393224 | tf_op jit(solution)/shard_map/ppermute | solution.py:476
  9.4 0.0 collective-permute-done.2.rows
  9.4 0.3 shard_map.106
  9.6 2.5 %collective-permute-start.3 = (bf16[4,16,1024]{2,1,0:T(8,128)(2,1)S(1)}, bf16[4,16,1024]{2,1,0:T(8,128)(2,1)S(1)}, u32[]{:S(2)}, u32[]{:S(2)}) collective-permute-start(bf16[4,16,1024]{2,1,0:T(8,128)(2,1)S(1)} %get-tuple-element.32), channel_id=1, source_target_pairs={{8,0},{16,8},{24,16},{0,24},{9,1},{17,9},{25,17},{1,25},{10,2},{18... | collective-permute-start | bytes 393224 | tf_op jit(solution)/shard_map/ppermute | solution.py:477
  12.1 0.0 collective-permute-start.4
  12.1 3.8 %collective-permute-start.5 = (bf16[4,16,1024]{2,1,0:T(8,128)(2,1)S(1)}, bf16[4,16,1024]{2,1,0:T(8,128)(2,1)S(1)}, u32[]{:S(2)}, u32[]{:S(2)}) collective-permute-start(bf16[4,16,1024]{2,1,0:T(8,128)(2,1)S(1)} %get-tuple-element.40), channel_id=1, source_target_pairs={{8,0},{16,8},{24,16},{0,24},{9,1},{17,9},{25,17},{1,25},{10,2},{18... | collective-permute-start | bytes 393224 | tf_op jit(solution)/shard_map/ppermute | solution.py:477
  16.0 2.3 %shard_map.105 = (f32[4,2048]{1,0:T(4,128)S(1)}, bf16[2048,1024]{1,0:T(8,128)(2,1)S(1)}, f32[2,1024]{1,0:T(2,128)S(1)}, bf16[128,256]{1,0:T(8,128)(2,1)S(1)}, bf...) custom-call(s32[1]{0:T(128)} %bitcast.place, bf16[4,16,1024]{2,1,0:T(8,128)(2,1)S(1)} %get-tuple-element.30.early, ...), custom_call_target="tpu_custom_call" | custom-call | bytes 4194304 | tf_op jit(solution)/shard_map/pallas_call | solution.py:486
  18.3 0.0 collective-permute-done.1.low
  18.3 0.6 %collective-permute-done.3.high = bf16[4,16,1024]{2,1,0:T(8,128)(2,1)S(1)} collective-permute-done((bf16[4,16,1024]{2,1,0:T(8,128)(2,1)S(1)}, bf16[4,16,1024]{2,1,0:T(8,128)(2,1)S(1)}, u32[]{:S(2)}, u32[]{:S(2)}) %collective-permute-start.3) | collective-permute-done | bytes 131104 | tf_op jit(solution)/shard_map/ppermute | solution.py:477
  18.9 2.5 %shard_map.107 = (f32[12,2048]{1,0:T(8,128)S(1)}, f32[64,2048]{1,0:T(8,128)S(1)}) custom-call(s32[2,12]{1,0:T(2,128)S(1)} %get-tuple-element.31.index, bf16[8,16,1024]{2,1,0:T(8,128)(2,1)S(1)} %get-tuple-element.28.early.refs_0_.own, bf16[4,16,1024]{2,1,0:T(8,128)(2,1)S(1)} %collective-permute-done.1.low, ...), custom_call_target="tpu_custom_call" | custom-call | flops 402653184 | bytes 4194304 | tf_op jit(solution)/shard_map/pallas_call | solution.py:522
  21.3 0.5 %collective-permute-done.4.low = bf16[4,16,1024]{2,1,0:T(8,128)(2,1)S(1)} collective-permute-done((bf16[4,16,1024]{2,1,0:T(8,128)(2,1)S(1)}, bf16[4,16,1024]{2,1,0:T(8,128)(2,1)S(1)}, u32[]{:S(2)}, u32[]{:S(2)}) %collective-permute-start.4) | collective-permute-done | bytes 131104 | tf_op jit(solution)/shard_map/ppermute | solution.py:476
  21.8 0.1 collective-permute-done.5.high
  21.9 2.5 %shard_map.108 = (f32[12,2048]{1,0:T(8,128)S(1)}, bf16[4,64,256]{2,1,0:T(8,128)(2,1)S(1)}, f32[4,64,256]{2,1,0:T(8,128)S(1)}) custom-call(s32[2,12]{1,0:T(2,128)S(1)} %get-tuple-element.31.index, bf16[8,16,1024]{2,1,0:T(8,128)(2,1)S(1)} %get-tuple-element.29.refs_1_.own, bf16[4,16,1024]{2,1,0:T(8,128)(2,1)S(1)} %collective-permute-done.4.low, ...), custom_call_target="tpu_custom_call" | custom-call | flops 402653184 | bytes 4194304 | tf_op jit(solution)/shard_map/pallas_call | solution.py:522
  24.4 0.1 collective-permute-start.6
  24.5 1.3 %collective-permute-done.6.got = bf16[4,64,256]{2,1,0:T(8,128)(2,1)S(1)} collective-permute-done((bf16[4,64,256]{2,1,0:T(8,128)(2,1)S(1)}, bf16[4,64,256]{2,1,0:T(8,128)(2,1)S(1)}, u32[]{:S(2)}, u32[]{:S(2)}) %collective-permute-start.6) | collective-permute-done | bytes 131104 | tf_op jit(solution)/shard_map/ppermute | solution.py:537
  25.8 2.5 %collective-permute-start.7 = (bf16[208,256]{1,0:T(8,128)(2,1)S(1)}, bf16[208,256]{1,0:T(8,128)(2,1)S(1)}, u32[]{:S(2)}, u32[]{:S(2)}) collective-permute-start(bf16[208,256]{1,0:T(8,128)(2,1)S(1)} %get-tuple-element.46), channel_id=1, source_target_pairs={{0,6},{1,7},{2,4},{3,5},{4,2},{5,3},{6,0},{7,1},{8,14},{9,15},{10,... | collective-permute-start | bytes 319496 | tf_op jit(solution)/shard_map/ppermute | solution.py:537
  28.4 0.5 %collective-permute-start.8 = (bf16[208,256]{1,0:T(8,128)(2,1)S(1)}, bf16[208,256]{1,0:T(8,128)(2,1)S(1)}, u32[]{:S(2)}, u32[]{:S(2)}) collective-permute-start(bf16[208,256]{1,0:T(8,128)(2,1)S(1)} %get-tuple-element.47), channel_id=1, source_target_pairs={{0,4},{1,5},{2,6},{3,7},{4,0},{5,1},{6,2},{7,3},{8,12},{9,13},{10,... | collective-permute-start | bytes 319496 | tf_op jit(solution)/shard_map/ppermute | solution.py:537
  28.9 0.5 %collective-permute-start.9 = (bf16[208,256]{1,0:T(8,128)(2,1)S(1)}, bf16[208,256]{1,0:T(8,128)(2,1)S(1)}, u32[]{:S(2)}, u32[]{:S(2)}) collective-permute-start(bf16[208,256]{1,0:T(8,128)(2,1)S(1)} %get-tuple-element.48), channel_id=1, source_target_pairs={{0,2},{1,3},{2,0},{3,1},{4,6},{5,7},{6,4},{7,5},{8,10},{9,11},{10,... | collective-permute-start | bytes 319496 | tf_op jit(solution)/shard_map/ppermute | solution.py:537
  29.4 2.5 %collective-permute-done.7.refs_0_ = bf16[208,256]{1,0:T(8,128)(2,1)S(1)} collective-permute-done((bf16[208,256]{1,0:T(8,128)(2,1)S(1)}, bf16[208,256]{1,0:T(8,128)(2,1)S(1)}, u32[]{:S(2)}, u32[]{:S(2)}) %collective-permute-start.7) | collective-permute-done | bytes 106528 | tf_op jit(solution)/shard_map/ppermute | solution.py:537
  31.9 2.2 %collective-permute-done.8.refs_1_ = bf16[208,256]{1,0:T(8,128)(2,1)S(1)} collective-permute-done((bf16[208,256]{1,0:T(8,128)(2,1)S(1)}, bf16[208,256]{1,0:T(8,128)(2,1)S(1)}, u32[]{:S(2)}, u32[]{:S(2)}) %collective-permute-start.8) | collective-permute-done | bytes 106528 | tf_op jit(solution)/shard_map/ppermute | solution.py:537
  34.1 0.1 collective-permute-done.9.refs_2_
  34.2 0.2 shard_map.110
  34.3 0.1 collective-permute-start.10
  34.4 0.8 %copy.11 = f32[12,2,2048]{2,1,0:T(2,128)} copy(f32[12,2,2048]{2,0,1:T(8,128)S(1)} %pad_maximum_fusion) | data formatting | bytes 393216
  35.3 0.3 collective-permute-done.10.got
  35.6 0.7 %shard_map.111 = (f32[12,256]{1,0:T(8,128)}, f32[12,4,256]{2,1,0:T(4,128)}) custom-call(f32[64,256]{1,0:T(8,128)S(1)} %get-tuple-element.49.total, f32[12,128]{1,0:T(8,128)S(1)} %get-tuple-element.50.mine, f32[12,128]{1,0:T(8,128)S(1)} %collective-permute-done.10.got), custom_call_target="tpu_custom_call" | custom-call | tf_op jit(solution)/shard_map/pallas_call | solution.py:555
  (2 shorter events, 0.1 us)
Async XLA Ops:
  0.6 8.7 %collective-permute-start.2 = (s32[2,12]{1,0:T(2,128)}, s32[2,12]{1,0:T(2,128)S(1)}, u32[]{:S(2)}, u32[]{:S(2)}) collective-permute-start(s32[2,12]{1,0:T(2,128)} %bitcast.8), channel_id=1, source_target_pairs={{0,8},{8,16},{16,24},{24,0},{1,9},{9,17},{17,25},{25,1},{2,10},{10... | collective-permute-start | bytes 296 | tf_op jit(solution)/shard_map/ppermute | solution.py:451
  3.7 4.0 %collective-permute-start = (s32[2,12]{1,0:T(2,128)}, s32[2,12]{1,0:T(2,128)S(1)}, u32[]{:S(2)}, u32[]{:S(2)}) collective-permute-start(s32[2,12]{1,0:T(2,128)} %bitcast.9), channel_id=1, source_target_pairs={{8,0},{16,8},{24,16},{0,24},{9,1},{17,9},{25,17},{1,25},{10,2},{18... | collective-permute-start | bytes 296 | tf_op jit(solution)/shard_map/ppermute | solution.py:452
  7.9 10.4 %collective-permute-start.1 = (bf16[4,16,1024]{2,1,0:T(8,128)(2,1)S(1)}, bf16[4,16,1024]{2,1,0:T(8,128)(2,1)S(1)}, u32[]{:S(2)}, u32[]{:S(2)}) collective-permute-start(bf16[4,16,1024]{2,1,0:T(8,128)(2,1)S(1)} %get-tuple-element.30.early), channel_id=1, source_target_pairs={{0,8},{8,16},{16,24},{24,0},{1,9},{9,17},{17,25},{25,1},{2,10},{10... | collective-permute-start | bytes 393224 | tf_op jit(solution)/shard_map/ppermute | solution.py:476
  9.6 9.2 %collective-permute-start.3 = (bf16[4,16,1024]{2,1,0:T(8,128)(2,1)S(1)}, bf16[4,16,1024]{2,1,0:T(8,128)(2,1)S(1)}, u32[]{:S(2)}, u32[]{:S(2)}) collective-permute-start(bf16[4,16,1024]{2,1,0:T(8,128)(2,1)S(1)} %get-tuple-element.32), channel_id=1, source_target_pairs={{8,0},{16,8},{24,16},{0,24},{9,1},{17,9},{25,17},{1,25},{10,2},{18... | collective-permute-start | bytes 393224 | tf_op jit(solution)/shard_map/ppermute | solution.py:477
  12.1 9.7 %collective-permute-start.4 = (bf16[4,16,1024]{2,1,0:T(8,128)(2,1)S(1)}, bf16[4,16,1024]{2,1,0:T(8,128)(2,1)S(1)}, u32[]{:S(2)}, u32[]{:S(2)}) collective-permute-start(bf16[4,16,1024]{2,1,0:T(8,128)(2,1)S(1)} %get-tuple-element.39), channel_id=1, source_target_pairs={{0,8},{8,16},{16,24},{24,0},{1,9},{9,17},{17,25},{25,1},{2,10},{10... | collective-permute-start | bytes 393224 | tf_op jit(solution)/shard_map/ppermute | solution.py:476
  12.1 9.7 %collective-permute-start.5 = (bf16[4,16,1024]{2,1,0:T(8,128)(2,1)S(1)}, bf16[4,16,1024]{2,1,0:T(8,128)(2,1)S(1)}, u32[]{:S(2)}, u32[]{:S(2)}) collective-permute-start(bf16[4,16,1024]{2,1,0:T(8,128)(2,1)S(1)} %get-tuple-element.40), channel_id=1, source_target_pairs={{8,0},{16,8},{24,16},{0,24},{9,1},{17,9},{25,17},{1,25},{10,2},{18... | collective-permute-start | bytes 393224 | tf_op jit(solution)/shard_map/ppermute | solution.py:477
  24.4 1.4 %collective-permute-start.6 = (bf16[4,64,256]{2,1,0:T(8,128)(2,1)S(1)}, bf16[4,64,256]{2,1,0:T(8,128)(2,1)S(1)}, u32[]{:S(2)}, u32[]{:S(2)}) collective-permute-start(bf16[4,64,256]{2,1,0:T(8,128)(2,1)S(1)} %get-tuple-element.44), channel_id=1, source_target_pairs={{0,1},{1,0},{2,3},{3,2},{4,5},{5,4},{6,7},{7,6},{8,9},{9,8},{10,11... | collective-permute-start | bytes 393224 | tf_op jit(solution)/shard_map/ppermute | solution.py:537
  25.8 6.1 %collective-permute-start.7 = (bf16[208,256]{1,0:T(8,128)(2,1)S(1)}, bf16[208,256]{1,0:T(8,128)(2,1)S(1)}, u32[]{:S(2)}, u32[]{:S(2)}) collective-permute-start(bf16[208,256]{1,0:T(8,128)(2,1)S(1)} %get-tuple-element.46), channel_id=1, source_target_pairs={{0,6},{1,7},{2,4},{3,5},{4,2},{5,3},{6,0},{7,1},{8,14},{9,15},{10,... | collective-permute-start | bytes 319496 | tf_op jit(solution)/shard_map/ppermute | solution.py:537
  28.4 5.7 %collective-permute-start.8 = (bf16[208,256]{1,0:T(8,128)(2,1)S(1)}, bf16[208,256]{1,0:T(8,128)(2,1)S(1)}, u32[]{:S(2)}, u32[]{:S(2)}) collective-permute-start(bf16[208,256]{1,0:T(8,128)(2,1)S(1)} %get-tuple-element.47), channel_id=1, source_target_pairs={{0,4},{1,5},{2,6},{3,7},{4,0},{5,1},{6,2},{7,3},{8,12},{9,13},{10,... | collective-permute-start | bytes 319496 | tf_op jit(solution)/shard_map/ppermute | solution.py:537
  28.9 5.3 %collective-permute-start.9 = (bf16[208,256]{1,0:T(8,128)(2,1)S(1)}, bf16[208,256]{1,0:T(8,128)(2,1)S(1)}, u32[]{:S(2)}, u32[]{:S(2)}) collective-permute-start(bf16[208,256]{1,0:T(8,128)(2,1)S(1)} %get-tuple-element.48), channel_id=1, source_target_pairs={{0,2},{1,3},{2,0},{3,1},{4,6},{5,7},{6,4},{7,5},{8,10},{9,11},{10,... | collective-permute-start | bytes 319496 | tf_op jit(solution)/shard_map/ppermute | solution.py:537
  34.3 1.2 %collective-permute-start.10 = (f32[12,128]{1,0:T(8,128)S(1)}, f32[12,128]{1,0:T(8,128)S(1)}, u32[]{:S(2)}, u32[]{:S(2)}) collective-permute-start(f32[12,128]{1,0:T(8,128)S(1)} %get-tuple-element.50.mine), channel_id=1, source_target_pairs={{0,1},{1,0},{2,3},{3,2},{4,5},{5,4},{6,7},{7,6},{8,9},{9,8},{10,11... | collective-permute-start | bytes 18440 | tf_op jit(solution)/shard_map/ppermute | solution.py:537

commit v9 on v8

--- a/solution.py
+++ b/solution.py
@@ -215,17 +215,14 @@
     used = used_stations(rows[1:2], place[0] * stations, stations)
     weight = jnp.left_shift(1, lax.broadcasted_iota(jnp.int32, (stations, 1), 0)).astype(F32)
     needed = jnp.sum(used * weight).astype(jnp.int32)
-    slot = jnp.int32(0)
-    for station in range(stations):
-        wanted = jnp.bitwise_and(jnp.right_shift(needed, station), 1)
-        spot = jnp.minimum(slot, NEAR - 1)
-
-        @pl.when(wanted == 1)
-        def _():
-            for source, target in zip(refs[:windows], refs[windows:]):
-                target[spot] = source[station]
-
-        slot = slot + wanted
+    for slot in range(NEAR):
+        lowest = jnp.bitwise_and(needed, -needed)
+        station = jnp.int32(0)
+        for number in range(1, stations):
+            station = station + jnp.where(lowest >= (1 << number), 1, 0)
+        for source, target in zip(refs[:windows], refs[windows:]):
+            target[slot] = source[station]
+        needed = needed - lowest
 
 
 def window_kernel(sizes, index, own, low, high, start, table, ends, pick, spread, *refs):

time: 36.5 us -> 36.5 us (level)
  no operation moved by 1% of the time
where the time goes in v9:
time: 36.5 us; the launch traced here: 36.3 us
  starting transfers between devices  16.6 us (45%)
  Pallas kernels  10.6 us (29%)
  waiting for transfers between devices  7.49 us (21%)
  local copies, waits for them, and re-layouts  0.83 us (2%)
  between operations  0.74 us (2%)
    ppermute x5, waiting for transfers between devices, on_device(): lax.ppermute(value, 'hours', [(k, k ^ step) for k in range(slices)])  6.39 us
    ppermute x2, starting transfers between devices, on_device(): highs = [lax.ppermute(one, 'pairs', backward) for one in to_last]  6.31 us
    pallas_call x2, Pallas kernels, on_device(): call(functools.partial(window_kernel, sizes), outs, specs, [VMEM] * len(o...  4.97 us
    ppermute x5, starting transfers between devices, on_device(): lax.ppermute(value, 'hours', [(k, k ^ step) for k in range(slices)])  3.69 us
    ppermute x1, starting transfers between devices, on_device(): before = lax.ppermute(rows, 'pairs', forward)  3.08 us
    pallas_call x1, Pallas kernels, on_device(): call(functools.partial(stage_kernel, groups, stations), [struct(one.shape...  2.35 us
    ppermute x1, starting transfers between devices, on_device(): after = lax.ppermute(rows, 'pairs', backward)  2.09 us
    pallas_call x1, Pallas kernels, on_device(): call(whiten_kernel, [struct((stations, parts * seg, freq), BF16)] * windo...  1.86 us
  transfers between devices with their start and end apart: 11, of which 8 were waited for; matrix products, arithmetic and copies ran while one was open for 2% of the time, Pallas kernels for 20%

profile of v9, /device:TPU:0, one launch (start us, length us, event | category | flops | bytes accessed | tf_op | source)
XLA Modules:
  0.0 36.3 jit_solution(2146354606764230626)
XLA Ops:
  0.6 3.1 %collective-permute-start.2 = (s32[2,12]{1,0:T(2,128)}, s32[2,12]{1,0:T(2,128)S(1)}, u32[]{:S(2)}, u32[]{:S(2)}) collective-permute-start(s32[2,12]{1,0:T(2,128)} %bitcast.8), channel_id=1, source_target_pairs={{0,8},{8,16},{16,24},{24,0},{1,9},{9,17},{17,25},{25,1},{2,10},{10... | collective-permute-start | bytes 296 | tf_op jit(solution)/shard_map/ppermute | solution.py:448
  3.7 2.1 %collective-permute-start = (s32[2,12]{1,0:T(2,128)}, s32[2,12]{1,0:T(2,128)S(1)}, u32[]{:S(2)}, u32[]{:S(2)}) collective-permute-start(s32[2,12]{1,0:T(2,128)} %bitcast.9), channel_id=1, source_target_pairs={{8,0},{16,8},{24,16},{0,24},{9,1},{17,9},{25,17},{1,25},{10,2},{18... | collective-permute-start | bytes 296 | tf_op jit(solution)/shard_map/ppermute | solution.py:449
  5.8 1.9 %shard_map.103 = (bf16[8,16,1024]{2,1,0:T(8,128)(2,1)S(1)}, bf16[8,16,1024]{2,1,0:T(8,128)(2,1)S(1)}) custom-call(bf16[8,2,8,2,1024]{4,3,2,1,0:T(2,128)(2,1)} %far_spectra.1, s32[8,2,8]{2,1,0:T(2,128)} %far_masks.1), custom_call_target="tpu_custom_call" | custom-call | tf_op jit(solution)/shard_map/pallas_call | solution.py:451
  7.7 0.0 collective-permute-done.rows
  7.7 0.2 shard_map.104
  7.9 1.4 %collective-permute-start.1 = (bf16[4,16,1024]{2,1,0:T(8,128)(2,1)S(1)}, bf16[4,16,1024]{2,1,0:T(8,128)(2,1)S(1)}, u32[]{:S(2)}, u32[]{:S(2)}) collective-permute-start(bf16[4,16,1024]{2,1,0:T(8,128)(2,1)S(1)} %get-tuple-element.30.early), channel_id=1, source_target_pairs={{0,8},{8,16},{16,24},{24,0},{1,9},{9,17},{17,25},{25,1},{2,10},{10... | collective-permute-start | bytes 393224 | tf_op jit(solution)/shard_map/ppermute | solution.py:473
  9.4 0.0 collective-permute-done.2.rows
  9.4 0.2 shard_map.106
  9.6 2.5 %collective-permute-start.3 = (bf16[4,16,1024]{2,1,0:T(8,128)(2,1)S(1)}, bf16[4,16,1024]{2,1,0:T(8,128)(2,1)S(1)}, u32[]{:S(2)}, u32[]{:S(2)}) collective-permute-start(bf16[4,16,1024]{2,1,0:T(8,128)(2,1)S(1)} %get-tuple-element.32), channel_id=1, source_target_pairs={{8,0},{16,8},{24,16},{0,24},{9,1},{17,9},{25,17},{1,25},{10,2},{18... | collective-permute-start | bytes 393224 | tf_op jit(solution)/shard_map/ppermute | solution.py:474
  12.1 0.0 collective-permute-start.4
  12.1 3.8 %collective-permute-start.5 = (bf16[4,16,1024]{2,1,0:T(8,128)(2,1)S(1)}, bf16[4,16,1024]{2,1,0:T(8,128)(2,1)S(1)}, u32[]{:S(2)}, u32[]{:S(2)}) collective-permute-start(bf16[4,16,1024]{2,1,0:T(8,128)(2,1)S(1)} %get-tuple-element.40), channel_id=1, source_target_pairs={{8,0},{16,8},{24,16},{0,24},{9,1},{17,9},{25,17},{1,25},{10,2},{18... | collective-permute-start | bytes 393224 | tf_op jit(solution)/shard_map/ppermute | solution.py:474
  15.9 2.3 %shard_map.105 = (f32[4,2048]{1,0:T(4,128)S(1)}, bf16[2048,1024]{1,0:T(8,128)(2,1)S(1)}, f32[2,1024]{1,0:T(2,128)S(1)}, bf16[128,256]{1,0:T(8,128)(2,1)S(1)}, bf...) custom-call(s32[1]{0:T(128)} %bitcast.place, bf16[4,16,1024]{2,1,0:T(8,128)(2,1)S(1)} %get-tuple-element.30.early, ...), custom_call_target="tpu_custom_call" | custom-call | bytes 4194304 | tf_op jit(solution)/shard_map/pallas_call | solution.py:483
  18.3 0.0 collective-permute-done.1.low
  18.3 0.6 %collective-permute-done.3.high = bf16[4,16,1024]{2,1,0:T(8,128)(2,1)S(1)} collective-permute-done((bf16[4,16,1024]{2,1,0:T(8,128)(2,1)S(1)}, bf16[4,16,1024]{2,1,0:T(8,128)(2,1)S(1)}, u32[]{:S(2)}, u32[]{:S(2)}) %collective-permute-start.3) | collective-permute-done | bytes 131104 | tf_op jit(solution)/shard_map/ppermute | solution.py:474
  18.9 2.5 %shard_map.107 = (f32[12,2048]{1,0:T(8,128)S(1)}, f32[64,2048]{1,0:T(8,128)S(1)}) custom-call(s32[2,12]{1,0:T(2,128)S(1)} %get-tuple-element.31.index, bf16[8,16,1024]{2,1,0:T(8,128)(2,1)S(1)} %get-tuple-element.28.early.refs_0_.own, bf16[4,16,1024]{2,1,0:T(8,128)(2,1)S(1)} %collective-permute-done.1.low, ...), custom_call_target="tpu_custom_call" | custom-call | flops 402653184 | bytes 4194304 | tf_op jit(solution)/shard_map/pallas_call | solution.py:519
  21.4 0.5 %collective-permute-done.4.low = bf16[4,16,1024]{2,1,0:T(8,128)(2,1)S(1)} collective-permute-done((bf16[4,16,1024]{2,1,0:T(8,128)(2,1)S(1)}, bf16[4,16,1024]{2,1,0:T(8,128)(2,1)S(1)}, u32[]{:S(2)}, u32[]{:S(2)}) %collective-permute-start.4) | collective-permute-done | bytes 131104 | tf_op jit(solution)/shard_map/ppermute | solution.py:473
  21.8 0.1 collective-permute-done.5.high
  21.9 2.5 %shard_map.108 = (f32[12,2048]{1,0:T(8,128)S(1)}, bf16[4,64,256]{2,1,0:T(8,128)(2,1)S(1)}, f32[4,64,256]{2,1,0:T(8,128)S(1)}) custom-call(s32[2,12]{1,0:T(2,128)S(1)} %get-tuple-element.31.index, bf16[8,16,1024]{2,1,0:T(8,128)(2,1)S(1)} %get-tuple-element.29.refs_1_.own, bf16[4,16,1024]{2,1,0:T(8,128)(2,1)S(1)} %collective-permute-done.4.low, ...), custom_call_target="tpu_custom_call" | custom-call | flops 402653184 | bytes 4194304 | tf_op jit(solution)/shard_map/pallas_call | solution.py:519
  24.4 0.1 collective-permute-start.6
  24.5 1.3 %collective-permute-done.6.got = bf16[4,64,256]{2,1,0:T(8,128)(2,1)S(1)} collective-permute-done((bf16[4,64,256]{2,1,0:T(8,128)(2,1)S(1)}, bf16[4,64,256]{2,1,0:T(8,128)(2,1)S(1)}, u32[]{:S(2)}, u32[]{:S(2)}) %collective-permute-start.6) | collective-permute-done | bytes 131104 | tf_op jit(solution)/shard_map/ppermute | solution.py:534
  25.8 2.5 %collective-permute-start.7 = (bf16[208,256]{1,0:T(8,128)(2,1)S(1)}, bf16[208,256]{1,0:T(8,128)(2,1)S(1)}, u32[]{:S(2)}, u32[]{:S(2)}) collective-permute-start(bf16[208,256]{1,0:T(8,128)(2,1)S(1)} %get-tuple-element.46), channel_id=1, source_target_pairs={{0,6},{1,7},{2,4},{3,5},{4,2},{5,3},{6,0},{7,1},{8,14},{9,15},{10,... | collective-permute-start | bytes 319496 | tf_op jit(solution)/shard_map/ppermute | solution.py:534
  28.4 0.5 %collective-permute-start.8 = (bf16[208,256]{1,0:T(8,128)(2,1)S(1)}, bf16[208,256]{1,0:T(8,128)(2,1)S(1)}, u32[]{:S(2)}, u32[]{:S(2)}) collective-permute-start(bf16[208,256]{1,0:T(8,128)(2,1)S(1)} %get-tuple-element.47), channel_id=1, source_target_pairs={{0,4},{1,5},{2,6},{3,7},{4,0},{5,1},{6,2},{7,3},{8,12},{9,13},{10,... | collective-permute-start | bytes 319496 | tf_op jit(solution)/shard_map/ppermute | solution.py:534
  28.9 0.5 %collective-permute-start.9 = (bf16[208,256]{1,0:T(8,128)(2,1)S(1)}, bf16[208,256]{1,0:T(8,128)(2,1)S(1)}, u32[]{:S(2)}, u32[]{:S(2)}) collective-permute-start(bf16[208,256]{1,0:T(8,128)(2,1)S(1)} %get-tuple-element.48), channel_id=1, source_target_pairs={{0,2},{1,3},{2,0},{3,1},{4,6},{5,7},{6,4},{7,5},{8,10},{9,11},{10,... | collective-permute-start | bytes 319496 | tf_op jit(solution)/shard_map/ppermute | solution.py:534
  29.4 2.5 %collective-permute-done.7.refs_0_ = bf16[208,256]{1,0:T(8,128)(2,1)S(1)} collective-permute-done((bf16[208,256]{1,0:T(8,128)(2,1)S(1)}, bf16[208,256]{1,0:T(8,128)(2,1)S(1)}, u32[]{:S(2)}, u32[]{:S(2)}) %collective-permute-start.7) | collective-permute-done | bytes 106528 | tf_op jit(solution)/shard_map/ppermute | solution.py:534
  31.9 2.2 %collective-permute-done.8.refs_1_ = bf16[208,256]{1,0:T(8,128)(2,1)S(1)} collective-permute-done((bf16[208,256]{1,0:T(8,128)(2,1)S(1)}, bf16[208,256]{1,0:T(8,128)(2,1)S(1)}, u32[]{:S(2)}, u32[]{:S(2)}) %collective-permute-start.8) | collective-permute-done | bytes 106528 | tf_op jit(solution)/shard_map/ppermute | solution.py:534
  34.1 0.1 collective-permute-done.9.refs_2_
  34.2 0.2 shard_map.110
  34.3 0.1 collective-permute-start.10
  34.4 0.8 %copy.11 = f32[12,2,2048]{2,1,0:T(2,128)} copy(f32[12,2,2048]{2,0,1:T(8,128)S(1)} %pad_maximum_fusion) | data formatting | bytes 393216
  35.3 0.3 collective-permute-done.10.got
  35.6 0.7 %shard_map.111 = (f32[12,256]{1,0:T(8,128)}, f32[12,4,256]{2,1,0:T(4,128)}) custom-call(f32[64,256]{1,0:T(8,128)S(1)} %get-tuple-element.49.total, f32[12,128]{1,0:T(8,128)S(1)} %get-tuple-element.50.mine, f32[12,128]{1,0:T(8,128)S(1)} %collective-permute-done.10.got), custom_call_target="tpu_custom_call" | custom-call | tf_op jit(solution)/shard_map/pallas_call | solution.py:552
  (2 shorter events, 0.1 us)
Async XLA Ops:
  0.6 8.7 %collective-permute-start.2 = (s32[2,12]{1,0:T(2,128)}, s32[2,12]{1,0:T(2,128)S(1)}, u32[]{:S(2)}, u32[]{:S(2)}) collective-permute-start(s32[2,12]{1,0:T(2,128)} %bitcast.8), channel_id=1, source_target_pairs={{0,8},{8,16},{16,24},{24,0},{1,9},{9,17},{17,25},{25,1},{2,10},{10... | collective-permute-start | bytes 296 | tf_op jit(solution)/shard_map/ppermute | solution.py:448
  3.7 4.0 %collective-permute-start = (s32[2,12]{1,0:T(2,128)}, s32[2,12]{1,0:T(2,128)S(1)}, u32[]{:S(2)}, u32[]{:S(2)}) collective-permute-start(s32[2,12]{1,0:T(2,128)} %bitcast.9), channel_id=1, source_target_pairs={{8,0},{16,8},{24,16},{0,24},{9,1},{17,9},{25,17},{1,25},{10,2},{18... | collective-permute-start | bytes 296 | tf_op jit(solution)/shard_map/ppermute | solution.py:449
  7.9 10.4 %collective-permute-start.1 = (bf16[4,16,1024]{2,1,0:T(8,128)(2,1)S(1)}, bf16[4,16,1024]{2,1,0:T(8,128)(2,1)S(1)}, u32[]{:S(2)}, u32[]{:S(2)}) collective-permute-start(bf16[4,16,1024]{2,1,0:T(8,128)(2,1)S(1)} %get-tuple-element.30.early), channel_id=1, source_target_pairs={{0,8},{8,16},{16,24},{24,0},{1,9},{9,17},{17,25},{25,1},{2,10},{10... | collective-permute-start | bytes 393224 | tf_op jit(solution)/shard_map/ppermute | solution.py:473
  9.6 9.3 %collective-permute-start.3 = (bf16[4,16,1024]{2,1,0:T(8,128)(2,1)S(1)}, bf16[4,16,1024]{2,1,0:T(8,128)(2,1)S(1)}, u32[]{:S(2)}, u32[]{:S(2)}) collective-permute-start(bf16[4,16,1024]{2,1,0:T(8,128)(2,1)S(1)} %get-tuple-element.32), channel_id=1, source_target_pairs={{8,0},{16,8},{24,16},{0,24},{9,1},{17,9},{25,17},{1,25},{10,2},{18... | collective-permute-start | bytes 393224 | tf_op jit(solution)/shard_map/ppermute | solution.py:474
  12.1 9.7 %collective-permute-start.4 = (bf16[4,16,1024]{2,1,0:T(8,128)(2,1)S(1)}, bf16[4,16,1024]{2,1,0:T(8,128)(2,1)S(1)}, u32[]{:S(2)}, u32[]{:S(2)}) collective-permute-start(bf16[4,16,1024]{2,1,0:T(8,128)(2,1)S(1)} %get-tuple-element.39), channel_id=1, source_target_pairs={{0,8},{8,16},{16,24},{24,0},{1,9},{9,17},{17,25},{25,1},{2,10},{10... | collective-permute-start | bytes 393224 | tf_op jit(solution)/shard_map/ppermute | solution.py:473
  12.1 9.8 %collective-permute-start.5 = (bf16[4,16,1024]{2,1,0:T(8,128)(2,1)S(1)}, bf16[4,16,1024]{2,1,0:T(8,128)(2,1)S(1)}, u32[]{:S(2)}, u32[]{:S(2)}) collective-permute-start(bf16[4,16,1024]{2,1,0:T(8,128)(2,1)S(1)} %get-tuple-element.40), channel_id=1, source_target_pairs={{8,0},{16,8},{24,16},{0,24},{9,1},{17,9},{25,17},{1,25},{10,2},{18... | collective-permute-start | bytes 393224 | tf_op jit(solution)/shard_map/ppermute | solution.py:474
  24.4 1.4 %collective-permute-start.6 = (bf16[4,64,256]{2,1,0:T(8,128)(2,1)S(1)}, bf16[4,64,256]{2,1,0:T(8,128)(2,1)S(1)}, u32[]{:S(2)}, u32[]{:S(2)}) collective-permute-start(bf16[4,64,256]{2,1,0:T(8,128)(2,1)S(1)} %get-tuple-element.44), channel_id=1, source_target_pairs={{0,1},{1,0},{2,3},{3,2},{4,5},{5,4},{6,7},{7,6},{8,9},{9,8},{10,11... | collective-permute-start | bytes 393224 | tf_op jit(solution)/shard_map/ppermute | solution.py:534
  25.8 6.1 %collective-permute-start.7 = (bf16[208,256]{1,0:T(8,128)(2,1)S(1)}, bf16[208,256]{1,0:T(8,128)(2,1)S(1)}, u32[]{:S(2)}, u32[]{:S(2)}) collective-permute-start(bf16[208,256]{1,0:T(8,128)(2,1)S(1)} %get-tuple-element.46), channel_id=1, source_target_pairs={{0,6},{1,7},{2,4},{3,5},{4,2},{5,3},{6,0},{7,1},{8,14},{9,15},{10,... | collective-permute-start | bytes 319496 | tf_op jit(solution)/shard_map/ppermute | solution.py:534
  28.4 5.8 %collective-permute-start.8 = (bf16[208,256]{1,0:T(8,128)(2,1)S(1)}, bf16[208,256]{1,0:T(8,128)(2,1)S(1)}, u32[]{:S(2)}, u32[]{:S(2)}) collective-permute-start(bf16[208,256]{1,0:T(8,128)(2,1)S(1)} %get-tuple-element.47), channel_id=1, source_target_pairs={{0,4},{1,5},{2,6},{3,7},{4,0},{5,1},{6,2},{7,3},{8,12},{9,13},{10,... | collective-permute-start | bytes 319496 | tf_op jit(solution)/shard_map/ppermute | solution.py:534
  28.9 5.3 %collective-permute-start.9 = (bf16[208,256]{1,0:T(8,128)(2,1)S(1)}, bf16[208,256]{1,0:T(8,128)(2,1)S(1)}, u32[]{:S(2)}, u32[]{:S(2)}) collective-permute-start(bf16[208,256]{1,0:T(8,128)(2,1)S(1)} %get-tuple-element.48), channel_id=1, source_target_pairs={{0,2},{1,3},{2,0},{3,1},{4,6},{5,7},{6,4},{7,5},{8,10},{9,11},{10,... | collective-permute-start | bytes 319496 | tf_op jit(solution)/shard_map/ppermute | solution.py:534
  34.3 1.2 %collective-permute-start.10 = (f32[12,128]{1,0:T(8,128)S(1)}, f32[12,128]{1,0:T(8,128)S(1)}, u32[]{:S(2)}, u32[]{:S(2)}) collective-permute-start(f32[12,128]{1,0:T(8,128)S(1)} %get-tuple-element.50.mine), channel_id=1, source_target_pairs={{0,1},{1,0},{2,3},{3,2},{4,5},{5,4},{6,7},{7,6},{8,9},{9,8},{10,11... | collective-permute-start | bytes 18440 | tf_op jit(solution)/shard_map/ppermute | solution.py:534

commit v10 on v9

--- a/solution.py
+++ b/solution.py
@@ -59,13 +59,6 @@
 def two_parts(values):
     high = values.astype(BF16)
     return high, (values - high.astype(F32)).astype(BF16)
-
-
-def three_parts(values):
-    high = values.astype(BF16)
-    rest = values - high.astype(F32)
-    mid = rest.astype(BF16)
-    return high, mid, (rest - mid.astype(F32)).astype(BF16)
 
 
 def dot(left, right):
@@ -287,8 +280,8 @@
     ]
     stacked = jnp.concatenate([blocks, basis_rows] + turned, 0)
     count = stacked.shape[0]
-    moved = dot(jnp.concatenate(three_parts(stacked), 0), pick[...])
-    moved = moved[0:count] + moved[count : 2 * count] + moved[2 * count :]
+    moved = dot(jnp.concatenate(two_parts(stacked), 0), pick[...])
+    moved = moved[0:count] + moved[count:]
     products = [moved[0:16, k * LANE : (k + 1) * LANE] for k in range(seg)]
     side_at = (seg + rank) * LANE
     for row in range(rank):

time: 36.5 us -> 36.5 us (level)
  no operation moved by 1% of the time
where the time goes in v10:
time: 36.5 us; the launch traced here: 36.3 us
  starting transfers between devices  16.6 us (45%)
  Pallas kernels  10.6 us (29%)
  waiting for transfers between devices  7.52 us (21%)
  local copies, waits for them, and re-layouts  0.83 us (2%)
  between operations  0.74 us (2%)
    ppermute x5, waiting for transfers between devices, on_device(): lax.ppermute(value, 'hours', [(k, k ^ step) for k in range(slices)])  6.39 us
    ppermute x2, starting transfers between devices, on_device(): highs = [lax.ppermute(one, 'pairs', backward) for one in to_last]  6.31 us
    pallas_call x2, Pallas kernels, on_device(): call(functools.partial(window_kernel, sizes), outs, specs, [VMEM] * len(o...  4.93 us
    ppermute x5, starting transfers between devices, on_device(): lax.ppermute(value, 'hours', [(k, k ^ step) for k in range(slices)])  3.69 us
    ppermute x1, starting transfers between devices, on_device(): before = lax.ppermute(rows, 'pairs', forward)  3.08 us
    pallas_call x1, Pallas kernels, on_device(): call(functools.partial(stage_kernel, groups, stations), [struct(one.shape...  2.35 us
    ppermute x1, starting transfers between devices, on_device(): after = lax.ppermute(rows, 'pairs', backward)  2.09 us
    pallas_call x1, Pallas kernels, on_device(): call(whiten_kernel, [struct((stations, parts * seg, freq), BF16)] * windo...  1.86 us
  transfers between devices with their start and end apart: 11, of which 8 were waited for; matrix products, arithmetic and copies ran while one was open for 2% of the time, Pallas kernels for 20%

profile of v10, /device:TPU:0, one launch (start us, length us, event | category | flops | bytes accessed | tf_op | source)
XLA Modules:
  0.0 36.3 jit_solution(12200183059037817440)
XLA Ops:
  0.6 3.1 %collective-permute-start.2 = (s32[2,12]{1,0:T(2,128)}, s32[2,12]{1,0:T(2,128)S(1)}, u32[]{:S(2)}, u32[]{:S(2)}) collective-permute-start(s32[2,12]{1,0:T(2,128)} %bitcast.8), channel_id=1, source_target_pairs={{0,8},{8,16},{16,24},{24,0},{1,9},{9,17},{17,25},{25,1},{2,10},{10... | collective-permute-start | bytes 296 | tf_op jit(solution)/shard_map/ppermute | solution.py:441
  3.7 2.1 %collective-permute-start = (s32[2,12]{1,0:T(2,128)}, s32[2,12]{1,0:T(2,128)S(1)}, u32[]{:S(2)}, u32[]{:S(2)}) collective-permute-start(s32[2,12]{1,0:T(2,128)} %bitcast.9), channel_id=1, source_target_pairs={{8,0},{16,8},{24,16},{0,24},{9,1},{17,9},{25,17},{1,25},{10,2},{18... | collective-permute-start | bytes 296 | tf_op jit(solution)/shard_map/ppermute | solution.py:442
  5.8 1.9 %shard_map.103 = (bf16[8,16,1024]{2,1,0:T(8,128)(2,1)S(1)}, bf16[8,16,1024]{2,1,0:T(8,128)(2,1)S(1)}) custom-call(bf16[8,2,8,2,1024]{4,3,2,1,0:T(2,128)(2,1)} %far_spectra.1, s32[8,2,8]{2,1,0:T(2,128)} %far_masks.1), custom_call_target="tpu_custom_call" | custom-call | tf_op jit(solution)/shard_map/pallas_call | solution.py:444
  7.7 0.0 collective-permute-done.rows
  7.7 0.2 shard_map.104
  7.9 1.4 %collective-permute-start.1 = (bf16[4,16,1024]{2,1,0:T(8,128)(2,1)S(1)}, bf16[4,16,1024]{2,1,0:T(8,128)(2,1)S(1)}, u32[]{:S(2)}, u32[]{:S(2)}) collective-permute-start(bf16[4,16,1024]{2,1,0:T(8,128)(2,1)S(1)} %get-tuple-element.30.early), channel_id=1, source_target_pairs={{0,8},{8,16},{16,24},{24,0},{1,9},{9,17},{17,25},{25,1},{2,10},{10... | collective-permute-start | bytes 393224 | tf_op jit(solution)/shard_map/ppermute | solution.py:466
  9.4 0.0 collective-permute-done.2.rows
  9.4 0.2 shard_map.106
  9.6 2.5 %collective-permute-start.3 = (bf16[4,16,1024]{2,1,0:T(8,128)(2,1)S(1)}, bf16[4,16,1024]{2,1,0:T(8,128)(2,1)S(1)}, u32[]{:S(2)}, u32[]{:S(2)}) collective-permute-start(bf16[4,16,1024]{2,1,0:T(8,128)(2,1)S(1)} %get-tuple-element.32), channel_id=1, source_target_pairs={{8,0},{16,8},{24,16},{0,24},{9,1},{17,9},{25,17},{1,25},{10,2},{18... | collective-permute-start | bytes 393224 | tf_op jit(solution)/shard_map/ppermute | solution.py:467
  12.1 0.0 collective-permute-start.4
  12.1 3.8 %collective-permute-start.5 = (bf16[4,16,1024]{2,1,0:T(8,128)(2,1)S(1)}, bf16[4,16,1024]{2,1,0:T(8,128)(2,1)S(1)}, u32[]{:S(2)}, u32[]{:S(2)}) collective-permute-start(bf16[4,16,1024]{2,1,0:T(8,128)(2,1)S(1)} %get-tuple-element.40), channel_id=1, source_target_pairs={{8,0},{16,8},{24,16},{0,24},{9,1},{17,9},{25,17},{1,25},{10,2},{18... | collective-permute-start | bytes 393224 | tf_op jit(solution)/shard_map/ppermute | solution.py:467
  15.9 2.3 %shard_map.105 = (f32[4,2048]{1,0:T(4,128)S(1)}, bf16[2048,1024]{1,0:T(8,128)(2,1)S(1)}, f32[2,1024]{1,0:T(2,128)S(1)}, bf16[128,256]{1,0:T(8,128)(2,1)S(1)}, bf...) custom-call(s32[1]{0:T(128)} %bitcast.place, bf16[4,16,1024]{2,1,0:T(8,128)(2,1)S(1)} %get-tuple-element.30.early, ...), custom_call_target="tpu_custom_call" | custom-call | bytes 4194304 | tf_op jit(solution)/shard_map/pallas_call | solution.py:476
  18.3 0.0 collective-permute-done.1.low
  18.3 0.6 %collective-permute-done.3.high = bf16[4,16,1024]{2,1,0:T(8,128)(2,1)S(1)} collective-permute-done((bf16[4,16,1024]{2,1,0:T(8,128)(2,1)S(1)}, bf16[4,16,1024]{2,1,0:T(8,128)(2,1)S(1)}, u32[]{:S(2)}, u32[]{:S(2)}) %collective-permute-start.3) | collective-permute-done | bytes 131104 | tf_op jit(solution)/shard_map/ppermute | solution.py:467
  18.9 2.4 %shard_map.107 = (f32[12,2048]{1,0:T(8,128)S(1)}, f32[64,2048]{1,0:T(8,128)S(1)}) custom-call(s32[2,12]{1,0:T(2,128)S(1)} %get-tuple-element.31.index, bf16[8,16,1024]{2,1,0:T(8,128)(2,1)S(1)} %get-tuple-element.28.early.refs_0_.own, bf16[4,16,1024]{2,1,0:T(8,128)(2,1)S(1)} %collective-permute-done.1.low, ...), custom_call_target="tpu_custom_call" | custom-call | flops 402653184 | bytes 4194304 | tf_op jit(solution)/shard_map/pallas_call | solution.py:512
  21.3 0.5 %collective-permute-done.4.low = bf16[4,16,1024]{2,1,0:T(8,128)(2,1)S(1)} collective-permute-done((bf16[4,16,1024]{2,1,0:T(8,128)(2,1)S(1)}, bf16[4,16,1024]{2,1,0:T(8,128)(2,1)S(1)}, u32[]{:S(2)}, u32[]{:S(2)}) %collective-permute-start.4) | collective-permute-done | bytes 131104 | tf_op jit(solution)/shard_map/ppermute | solution.py:466
  21.8 0.1 collective-permute-done.5.high
  21.9 2.5 %shard_map.108 = (f32[12,2048]{1,0:T(8,128)S(1)}, bf16[4,64,256]{2,1,0:T(8,128)(2,1)S(1)}, f32[4,64,256]{2,1,0:T(8,128)S(1)}) custom-call(s32[2,12]{1,0:T(2,128)S(1)} %get-tuple-element.31.index, bf16[8,16,1024]{2,1,0:T(8,128)(2,1)S(1)} %get-tuple-element.29.refs_1_.own, bf16[4,16,1024]{2,1,0:T(8,128)(2,1)S(1)} %collective-permute-done.4.low, ...), custom_call_target="tpu_custom_call" | custom-call | flops 402653184 | bytes 4194304 | tf_op jit(solution)/shard_map/pallas_call | solution.py:512
  24.4 0.1 collective-permute-start.6
  24.4 1.3 %collective-permute-done.6.got = bf16[4,64,256]{2,1,0:T(8,128)(2,1)S(1)} collective-permute-done((bf16[4,64,256]{2,1,0:T(8,128)(2,1)S(1)}, bf16[4,64,256]{2,1,0:T(8,128)(2,1)S(1)}, u32[]{:S(2)}, u32[]{:S(2)}) %collective-permute-start.6) | collective-permute-done | bytes 131104 | tf_op jit(solution)/shard_map/ppermute | solution.py:527
  25.8 2.5 %collective-permute-start.7 = (bf16[208,256]{1,0:T(8,128)(2,1)S(1)}, bf16[208,256]{1,0:T(8,128)(2,1)S(1)}, u32[]{:S(2)}, u32[]{:S(2)}) collective-permute-start(bf16[208,256]{1,0:T(8,128)(2,1)S(1)} %get-tuple-element.46), channel_id=1, source_target_pairs={{0,6},{1,7},{2,4},{3,5},{4,2},{5,3},{6,0},{7,1},{8,14},{9,15},{10,... | collective-permute-start | bytes 319496 | tf_op jit(solution)/shard_map/ppermute | solution.py:527
  28.3 0.5 %collective-permute-start.8 = (bf16[208,256]{1,0:T(8,128)(2,1)S(1)}, bf16[208,256]{1,0:T(8,128)(2,1)S(1)}, u32[]{:S(2)}, u32[]{:S(2)}) collective-permute-start(bf16[208,256]{1,0:T(8,128)(2,1)S(1)} %get-tuple-element.47), channel_id=1, source_target_pairs={{0,4},{1,5},{2,6},{3,7},{4,0},{5,1},{6,2},{7,3},{8,12},{9,13},{10,... | collective-permute-start | bytes 319496 | tf_op jit(solution)/shard_map/ppermute | solution.py:527
  28.8 0.5 %collective-permute-start.9 = (bf16[208,256]{1,0:T(8,128)(2,1)S(1)}, bf16[208,256]{1,0:T(8,128)(2,1)S(1)}, u32[]{:S(2)}, u32[]{:S(2)}) collective-permute-start(bf16[208,256]{1,0:T(8,128)(2,1)S(1)} %get-tuple-element.48), channel_id=1, source_target_pairs={{0,2},{1,3},{2,0},{3,1},{4,6},{5,7},{6,4},{7,5},{8,10},{9,11},{10,... | collective-permute-start | bytes 319496 | tf_op jit(solution)/shard_map/ppermute | solution.py:527
  29.4 2.5 %collective-permute-done.7.refs_0_ = bf16[208,256]{1,0:T(8,128)(2,1)S(1)} collective-permute-done((bf16[208,256]{1,0:T(8,128)(2,1)S(1)}, bf16[208,256]{1,0:T(8,128)(2,1)S(1)}, u32[]{:S(2)}, u32[]{:S(2)}) %collective-permute-start.7) | collective-permute-done | bytes 106528 | tf_op jit(solution)/shard_map/ppermute | solution.py:527
  31.9 2.2 %collective-permute-done.8.refs_1_ = bf16[208,256]{1,0:T(8,128)(2,1)S(1)} collective-permute-done((bf16[208,256]{1,0:T(8,128)(2,1)S(1)}, bf16[208,256]{1,0:T(8,128)(2,1)S(1)}, u32[]{:S(2)}, u32[]{:S(2)}) %collective-permute-start.8) | collective-permute-done | bytes 106528 | tf_op jit(solution)/shard_map/ppermute | solution.py:527
  34.1 0.1 collective-permute-done.9.refs_2_
  34.1 0.2 shard_map.110
  34.3 0.1 collective-permute-start.10
  34.4 0.8 %copy.11 = f32[12,2,2048]{2,1,0:T(2,128)} copy(f32[12,2,2048]{2,0,1:T(8,128)S(1)} %pad_maximum_fusion) | data formatting | bytes 393216
  35.2 0.3 collective-permute-done.10.got
  35.5 0.7 %shard_map.111 = (f32[12,256]{1,0:T(8,128)}, f32[12,4,256]{2,1,0:T(4,128)}) custom-call(f32[64,256]{1,0:T(8,128)S(1)} %get-tuple-element.49.total, f32[12,128]{1,0:T(8,128)S(1)} %get-tuple-element.50.mine, f32[12,128]{1,0:T(8,128)S(1)} %collective-permute-done.10.got), custom_call_target="tpu_custom_call" | custom-call | tf_op jit(solution)/shard_map/pallas_call | solution.py:545
  (2 shorter events, 0.1 us)
Async XLA Ops:
  0.6 8.7 %collective-permute-start.2 = (s32[2,12]{1,0:T(2,128)}, s32[2,12]{1,0:T(2,128)S(1)}, u32[]{:S(2)}, u32[]{:S(2)}) collective-permute-start(s32[2,12]{1,0:T(2,128)} %bitcast.8), channel_id=1, source_target_pairs={{0,8},{8,16},{16,24},{24,0},{1,9},{9,17},{17,25},{25,1},{2,10},{10... | collective-permute-start | bytes 296 | tf_op jit(solution)/shard_map/ppermute | solution.py:441
  3.7 4.0 %collective-permute-start = (s32[2,12]{1,0:T(2,128)}, s32[2,12]{1,0:T(2,128)S(1)}, u32[]{:S(2)}, u32[]{:S(2)}) collective-permute-start(s32[2,12]{1,0:T(2,128)} %bitcast.9), channel_id=1, source_target_pairs={{8,0},{16,8},{24,16},{0,24},{9,1},{17,9},{25,17},{1,25},{10,2},{18... | collective-permute-start | bytes 296 | tf_op jit(solution)/shard_map/ppermute | solution.py:442
  7.9 10.4 %collective-permute-start.1 = (bf16[4,16,1024]{2,1,0:T(8,128)(2,1)S(1)}, bf16[4,16,1024]{2,1,0:T(8,128)(2,1)S(1)}, u32[]{:S(2)}, u32[]{:S(2)}) collective-permute-start(bf16[4,16,1024]{2,1,0:T(8,128)(2,1)S(1)} %get-tuple-element.30.early), channel_id=1, source_target_pairs={{0,8},{8,16},{16,24},{24,0},{1,9},{9,17},{17,25},{25,1},{2,10},{10... | collective-permute-start | bytes 393224 | tf_op jit(solution)/shard_map/ppermute | solution.py:466
  9.6 9.3 %collective-permute-start.3 = (bf16[4,16,1024]{2,1,0:T(8,128)(2,1)S(1)}, bf16[4,16,1024]{2,1,0:T(8,128)(2,1)S(1)}, u32[]{:S(2)}, u32[]{:S(2)}) collective-permute-start(bf16[4,16,1024]{2,1,0:T(8,128)(2,1)S(1)} %get-tuple-element.32), channel_id=1, source_target_pairs={{8,0},{16,8},{24,16},{0,24},{9,1},{17,9},{25,17},{1,25},{10,2},{18... | collective-permute-start | bytes 393224 | tf_op jit(solution)/shard_map/ppermute | solution.py:467
  12.1 9.7 %collective-permute-start.4 = (bf16[4,16,1024]{2,1,0:T(8,128)(2,1)S(1)}, bf16[4,16,1024]{2,1,0:T(8,128)(2,1)S(1)}, u32[]{:S(2)}, u32[]{:S(2)}) collective-permute-start(bf16[4,16,1024]{2,1,0:T(8,128)(2,1)S(1)} %get-tuple-element.39), channel_id=1, source_target_pairs={{0,8},{8,16},{16,24},{24,0},{1,9},{9,17},{17,25},{25,1},{2,10},{10... | collective-permute-start | bytes 393224 | tf_op jit(solution)/shard_map/ppermute | solution.py:466
  12.1 9.8 %collective-permute-start.5 = (bf16[4,16,1024]{2,1,0:T(8,128)(2,1)S(1)}, bf16[4,16,1024]{2,1,0:T(8,128)(2,1)S(1)}, u32[]{:S(2)}, u32[]{:S(2)}) collective-permute-start(bf16[4,16,1024]{2,1,0:T(8,128)(2,1)S(1)} %get-tuple-element.40), channel_id=1, source_target_pairs={{8,0},{16,8},{24,16},{0,24},{9,1},{17,9},{25,17},{1,25},{10,2},{18... | collective-permute-start | bytes 393224 | tf_op jit(solution)/shard_map/ppermute | solution.py:467
  24.4 1.4 %collective-permute-start.6 = (bf16[4,64,256]{2,1,0:T(8,128)(2,1)S(1)}, bf16[4,64,256]{2,1,0:T(8,128)(2,1)S(1)}, u32[]{:S(2)}, u32[]{:S(2)}) collective-permute-start(bf16[4,64,256]{2,1,0:T(8,128)(2,1)S(1)} %get-tuple-element.44), channel_id=1, source_target_pairs={{0,1},{1,0},{2,3},{3,2},{4,5},{5,4},{6,7},{7,6},{8,9},{9,8},{10,11... | collective-permute-start | bytes 393224 | tf_op jit(solution)/shard_map/ppermute | solution.py:527
  25.8 6.1 %collective-permute-start.7 = (bf16[208,256]{1,0:T(8,128)(2,1)S(1)}, bf16[208,256]{1,0:T(8,128)(2,1)S(1)}, u32[]{:S(2)}, u32[]{:S(2)}) collective-permute-start(bf16[208,256]{1,0:T(8,128)(2,1)S(1)} %get-tuple-element.46), channel_id=1, source_target_pairs={{0,6},{1,7},{2,4},{3,5},{4,2},{5,3},{6,0},{7,1},{8,14},{9,15},{10,... | collective-permute-start | bytes 319496 | tf_op jit(solution)/shard_map/ppermute | solution.py:527
  28.3 5.8 %collective-permute-start.8 = (bf16[208,256]{1,0:T(8,128)(2,1)S(1)}, bf16[208,256]{1,0:T(8,128)(2,1)S(1)}, u32[]{:S(2)}, u32[]{:S(2)}) collective-permute-start(bf16[208,256]{1,0:T(8,128)(2,1)S(1)} %get-tuple-element.47), channel_id=1, source_target_pairs={{0,4},{1,5},{2,6},{3,7},{4,0},{5,1},{6,2},{7,3},{8,12},{9,13},{10,... | collective-permute-start | bytes 319496 | tf_op jit(solution)/shard_map/ppermute | solution.py:527
  28.8 5.3 %collective-permute-start.9 = (bf16[208,256]{1,0:T(8,128)(2,1)S(1)}, bf16[208,256]{1,0:T(8,128)(2,1)S(1)}, u32[]{:S(2)}, u32[]{:S(2)}) collective-permute-start(bf16[208,256]{1,0:T(8,128)(2,1)S(1)} %get-tuple-element.48), channel_id=1, source_target_pairs={{0,2},{1,3},{2,0},{3,1},{4,6},{5,7},{6,4},{7,5},{8,10},{9,11},{10,... | collective-permute-start | bytes 319496 | tf_op jit(solution)/shard_map/ppermute | solution.py:527
  34.3 1.2 %collective-permute-start.10 = (f32[12,128]{1,0:T(8,128)S(1)}, f32[12,128]{1,0:T(8,128)S(1)}, u32[]{:S(2)}, u32[]{:S(2)}) collective-permute-start(f32[12,128]{1,0:T(8,128)S(1)} %get-tuple-element.50.mine), channel_id=1, source_target_pairs={{0,1},{1,0},{2,3},{3,2},{4,5},{5,4},{6,7},{7,6},{8,9},{9,8},{10,11... | collective-permute-start | bytes 18440 | tf_op jit(solution)/shard_map/ppermute | solution.py:527
